TPU v7x, 32 devices: a whole 2x2x4 slice. The times are simulated.
32 devices in a mesh: items: 16 (over z, x, core), frames: 2 (over y).
Axes of the slice: x: 2, y: 2, z: 4, core: 2. Of those that a mesh axis runs over, the one named last changes fastest.
Arguments:
- tokens: bfloat16 [64, 1024, 768], P('items', 'frames'), may hold values from -6 to 6
- skip: int32 [64], P('items'), may hold values from 0 to 1
- latent_init: bfloat16 [128, 768], replicated, may hold values from -6 to 6
- tok_gain: float32 [768], replicated, may hold values from 0.25 to 1.75
- query_gain: float32 [768], replicated, may hold values from 0.25 to 1.75
- mlp_gain: float32 [768], replicated, may hold values from 0.25 to 1.75
- self_gain: float32 [768], replicated, may hold values from 0.25 to 1.75
- w_query: bfloat16 [768, 768], replicated, may hold values from -0.4375 to 0.4375
- w_keyval: bfloat16 [768, 1536], replicated, may hold values from -0.21875 to 0.21875
- w_out: bfloat16 [768, 768], replicated, may hold values from -1.75 to 1.75
- w_up: bfloat16 [768, 3072], replicated, may hold values from -0.21875 to 0.21875
- w_down: bfloat16 [3072, 768], replicated, may hold values from -0.15625 to 0.15625
- w_self_qkv: bfloat16 [768, 2304], replicated, may hold values from -0.3125 to 0.3125
- w_self_out: bfloat16 [768, 768], replicated, may hold values from -0.3125 to 0.3125
- grad_out: bfloat16 [64, 128, 768], P('items'), may hold values from -6 to 6
Outputs:
- latents: bfloat16 [64, 128, 768], P('items', 'frames')
- token_grad: bfloat16 [64, 1024, 768], P('items', 'frames')
- latent_grad: float32 [128, 768], P(None, 'frames')
- tok_gain_grad: float32 [768], P('frames')
- query_gain_grad: float32 [768], P('frames')
- mlp_gain_grad: float32 [768], P('frames')
- self_gain_grad: float32 [768], P('frames')
- w_query_grad: float32 [768, 768], P(None, 'frames')
- w_keyval_grad: float32 [768, 1536], P(None, 'frames')
- w_out_grad: float32 [768, 768], P(None, 'frames')
- w_up_grad: float32 [768, 3072], P(None, 'frames')
- w_down_grad: float32 [3072, 768], P(None, 'frames')
- w_self_qkv_grad: float32 [768, 2304], P(None, 'frames')
- w_self_out_grad: float32 [768, 768], P(None, 'frames')
Inputs may be any that keep to these rules, and one draw needn't show every extreme that they name: `skip`: 1 skips the item's cross-attention, 0 keeps it.
All inputs are finite; a program needn't handle non-finite values.
Results may differ from a plain program's by a relative error of at most 0.023.
The roundings to bfloat16 on the way count: a program that leaves them out, or rounds other values in their place, can miss the bound.
Values sent between devices are 32-bit elements; how exact they have to be, the bound alone decides.
A program may use at most 192 MiB of HBM per device.

v0:
```python
import jax
import jax.numpy as jnp
from jax import lax
from jax.sharding import PartitionSpec as P

HEADS = 12


EPSILON = 1e-05


def norm_parts(values):
    center = jnp.mean(values, axis=-1, keepdims=True)
    centered = values - center
    inverse = lax.rsqrt(jnp.mean(centered * centered, axis=-1, keepdims=True) + EPSILON)
    return (centered * inverse, inverse)


def norm_back(incoming, normed, inverse, gain):
    scaled = incoming * gain
    gain_grad = jnp.sum((incoming * normed).reshape(-1, normed.shape[-1]), axis=0)
    average = jnp.mean(scaled, axis=-1, keepdims=True)
    along = jnp.mean(scaled * normed, axis=-1, keepdims=True)
    return (inverse * (scaled - average - normed * along), gain_grad)


def forward_mul(left, weight):
    return jnp.einsum("irk,kn->irn", left, weight, preferred_element_type=jnp.float32)


def input_mul(grad_rows, weight):
    return jnp.einsum("irn,kn->irk", grad_rows, weight, preferred_element_type=jnp.float32)


def weight_mul(left, grad_rows):
    return jnp.einsum("irk,irn->kn", left, grad_rows, preferred_element_type=jnp.float32)


def split_heads(values):
    return values.reshape(values.shape[0], values.shape[1], HEADS, values.shape[2] // HEADS)


def join_heads(values):
    return values.reshape(values.shape[0], values.shape[1], values.shape[2] * values.shape[3])


def own_columns(gradient, column_index, parts):
    span = gradient.shape[-1] // parts
    return lax.dynamic_slice_in_dim(gradient, column_index * span, span, gradient.ndim - 1)


def shards(
    tokens,
    skip,
    latent_init,
    tok_gain,
    query_gain,
    mlp_gain,
    self_gain,
    w_query,
    w_keyval,
    w_out,
    w_up,
    w_down,
    w_self_qkv,
    w_self_out,
    grad_out,
):
    item_count, row_count, width = tokens.shape
    latent_count = latent_init.shape[0]
    factor = (width // HEADS) ** (-0.5)
    keep_flag = (1 - skip).astype(jnp.float32)[:, None, None]
    tok_normed, tok_inverse = norm_parts(tokens.astype(jnp.float32))
    tok_in = (tok_normed * tok_gain).astype(jnp.bfloat16)
    keyval = forward_mul(tok_in, w_keyval).astype(jnp.bfloat16)
    key_heads = split_heads(keyval[..., :width])
    value_heads = split_heads(keyval[..., width:])
    latent_rows = latent_init.astype(jnp.float32)
    query_normed, query_inverse = norm_parts(latent_rows)
    query_in = (query_normed * query_gain).astype(jnp.bfloat16)
    query_one = jnp.dot(query_in, w_query, preferred_element_type=jnp.float32).astype(jnp.bfloat16)
    queries = jnp.broadcast_to(query_one, (item_count, latent_count, width))
    query_heads = split_heads(queries)
    scores = (
        jnp.einsum("iqhe,ikhe->ihqk", query_heads, key_heads, preferred_element_type=jnp.float32)
        * factor
    )
    local_max = jnp.max(scores, axis=-1)
    row_max = lax.pmax(local_max, "frames")
    row_total = lax.psum(jnp.sum(jnp.exp(scores - row_max[..., None]), axis=-1), "frames")
    log_total = row_max + jnp.log(row_total)
    probs_low = jnp.exp(scores - log_total[..., None]).astype(jnp.bfloat16)
    heard_part = join_heads(
        jnp.einsum("ihqk,ikhe->iqhe", probs_low, value_heads, preferred_element_type=jnp.float32)
    )
    heard = lax.psum(heard_part, "frames")
    heard_low = heard.astype(jnp.bfloat16)
    after_cross = latent_rows[None] + keep_flag * forward_mul(heard_low, w_out)
    mlp_normed, mlp_inverse = norm_parts(after_cross)
    mlp_in = (mlp_normed * mlp_gain).astype(jnp.bfloat16)
    hidden = forward_mul(mlp_in, w_up)
    activation, gelu_pull = jax.vjp(jax.nn.gelu, hidden)
    activation_low = activation.astype(jnp.bfloat16)
    after_mlp = after_cross + forward_mul(activation_low, w_down)
    self_normed, self_inverse = norm_parts(after_mlp)
    self_in = (self_normed * self_gain).astype(jnp.bfloat16)
    triple = forward_mul(self_in, w_self_qkv).astype(jnp.bfloat16)
    self_query = split_heads(triple[..., :width])
    self_key = split_heads(triple[..., width : 2 * width])
    self_value = split_heads(triple[..., 2 * width :])
    self_scores = (
        jnp.einsum("iqhe,ikhe->ihqk", self_query, self_key, preferred_element_type=jnp.float32)
        * factor
    )
    self_shifted = jnp.exp(self_scores - jnp.max(self_scores, axis=-1, keepdims=True))
    self_probs = self_shifted / jnp.sum(self_shifted, axis=-1, keepdims=True)
    self_low = self_probs.astype(jnp.bfloat16)
    mixed = join_heads(
        jnp.einsum("ihqk,ikhe->iqhe", self_low, self_value, preferred_element_type=jnp.float32)
    )
    mixed_low = mixed.astype(jnp.bfloat16)
    after_self = after_mlp + forward_mul(mixed_low, w_self_out)
    frame_count = lax.axis_size("frames")
    frame_index = lax.axis_index("frames")
    latent_share = latent_count // frame_count
    out_latents = lax.dynamic_slice_in_dim(
        after_self, frame_index * latent_share, latent_share, 1
    ).astype(jnp.bfloat16)
    cotangent = grad_out.astype(jnp.float32)
    grad_self_out = weight_mul(mixed_low, grad_out)
    d_mixed = input_mul(grad_out, w_self_out).astype(jnp.bfloat16)
    d_mixed_heads = split_heads(d_mixed)
    d_self_probs = jnp.einsum(
        "iqhe,ikhe->ihqk", d_mixed_heads, self_value, preferred_element_type=jnp.float32
    )
    self_delta = jnp.einsum("iqhe,iqhe->ihq", d_mixed_heads.astype(jnp.float32), split_heads(mixed))
    d_self_scores = (self_probs * (d_self_probs - self_delta[..., None])).astype(jnp.bfloat16)
    d_self_query = (
        jnp.einsum("ihqk,ikhe->iqhe", d_self_scores, self_key, preferred_element_type=jnp.float32)
        * factor
    )
    d_self_key = (
        jnp.einsum("ihqk,iqhe->ikhe", d_self_scores, self_query, preferred_element_type=jnp.float32)
        * factor
    )
    d_self_value = jnp.einsum(
        "ihqk,iqhe->ikhe", self_low, d_mixed_heads, preferred_element_type=jnp.float32
    )
    d_triple = jnp.concatenate(
        [join_heads(d_self_query), join_heads(d_self_key), join_heads(d_self_value)], axis=-1
    ).astype(jnp.bfloat16)
    grad_self_qkv = weight_mul(self_in, d_triple)
    self_back, grad_self_gain = norm_back(
        input_mul(d_triple, w_self_qkv), self_normed, self_inverse, self_gain
    )
    d_after_mlp = cotangent + self_back
    mlp_branch = d_after_mlp.astype(jnp.bfloat16)
    grad_down = weight_mul(activation_low, mlp_branch)
    d_activation = input_mul(mlp_branch, w_down)
    d_hidden = gelu_pull(d_activation)[0].astype(jnp.bfloat16)
    grad_up = weight_mul(mlp_in, d_hidden)
    mlp_back, grad_mlp_gain = norm_back(
        input_mul(d_hidden, w_up), mlp_normed, mlp_inverse, mlp_gain
    )
    d_after_cross = d_after_mlp + mlp_back
    d_attn = (keep_flag * d_after_cross).astype(jnp.bfloat16)
    grad_out_w = weight_mul(heard_low, d_attn)
    d_heard = input_mul(d_attn, w_out).astype(jnp.bfloat16)
    d_heard_heads = split_heads(d_heard)
    again_scores = (
        jnp.einsum("iqhe,ikhe->ihqk", query_heads, key_heads, preferred_element_type=jnp.float32)
        * factor
    )
    probs_full = jnp.exp(again_scores - log_total[..., None])
    probs_again = probs_full.astype(jnp.bfloat16)
    d_probs = jnp.einsum(
        "iqhe,ikhe->ihqk", d_heard_heads, value_heads, preferred_element_type=jnp.float32
    )
    cross_delta = jnp.einsum(
        "iqhe,iqhe->ihq", d_heard_heads.astype(jnp.float32), split_heads(heard)
    )
    d_scores = (probs_full * (d_probs - cross_delta[..., None])).astype(jnp.bfloat16)
    query_part = join_heads(
        jnp.einsum("ihqk,ikhe->iqhe", d_scores, key_heads, preferred_element_type=jnp.float32)
        * factor
    )
    query_total = jnp.sum(lax.psum(query_part, "frames"), axis=0)
    d_keys = (
        jnp.einsum("ihqk,iqhe->ikhe", d_scores, query_heads, preferred_element_type=jnp.float32)
        * factor
    )
    d_values = jnp.einsum(
        "ihqk,iqhe->ikhe", probs_again, d_heard_heads, preferred_element_type=jnp.float32
    )
    d_keyval = jnp.concatenate([join_heads(d_keys), join_heads(d_values)], axis=-1).astype(
        jnp.bfloat16
    )
    keyval_part = weight_mul(tok_in, d_keyval)
    token_back, tok_gain_part = norm_back(
        input_mul(d_keyval, w_keyval), tok_normed, tok_inverse, tok_gain
    )
    token_grad = token_back.astype(jnp.bfloat16)
    grad_query_w = jnp.dot(
        query_in.astype(jnp.float32).T, query_total, precision=lax.Precision.HIGHEST
    )
    query_incoming = jnp.dot(
        query_total, w_query.astype(jnp.float32).T, precision=lax.Precision.HIGHEST
    )
    query_back, grad_query_gain = norm_back(query_incoming, query_normed, query_inverse, query_gain)
    grad_latent = jnp.sum(d_after_cross, axis=0) + query_back
    mine_latent = own_columns(grad_latent, frame_index, frame_count)
    mine_query_gain = own_columns(grad_query_gain, frame_index, frame_count)
    mine_mlp_gain = own_columns(grad_mlp_gain, frame_index, frame_count)
    mine_self_gain = own_columns(grad_self_gain, frame_index, frame_count)
    mine_query_w = own_columns(grad_query_w, frame_index, frame_count)
    mine_out_w = own_columns(grad_out_w, frame_index, frame_count)
    mine_up = own_columns(grad_up, frame_index, frame_count)
    mine_down = own_columns(grad_down, frame_index, frame_count)
    mine_self_qkv = own_columns(grad_self_qkv, frame_index, frame_count)
    mine_self_out = own_columns(grad_self_out, frame_index, frame_count)
    summed = lax.psum(
        (
            mine_latent,
            mine_query_gain,
            mine_mlp_gain,
            mine_self_gain,
            mine_query_w,
            mine_out_w,
            mine_up,
            mine_down,
            mine_self_qkv,
            mine_self_out,
            keyval_part,
            tok_gain_part,
        ),
        "items",
    )
    keyval_grad, tok_gain_grad = (
        lax.psum_scatter(summed[10], "frames", scatter_dimension=1, tiled=True),
        lax.psum_scatter(summed[11], "frames", scatter_dimension=0, tiled=True),
    )
    return (
        out_latents,
        token_grad,
        summed[0],
        tok_gain_grad,
        summed[1],
        summed[2],
        summed[3],
        summed[4],
        keyval_grad,
        summed[5],
        summed[6],
        summed[7],
        summed[8],
        summed[9],
    )


def solution(mesh):
    in_specs = (
        P("items", "frames", None),
        P("items"),
        P(),
        P(),
        P(),
        P(),
        P(),
        P(),
        P(),
        P(),
        P(),
        P(),
        P(),
        P(),
        P("items", None, None),
    )
    out_specs = (
        P("items", "frames", None),
        P("items", "frames", None),
        P(None, "frames"),
        P("frames"),
        P("frames"),
        P("frames"),
        P("frames"),
        P(None, "frames"),
        P(None, "frames"),
        P(None, "frames"),
        P(None, "frames"),
        P(None, "frames"),
        P(None, "frames"),
        P(None, "frames"),
    )
    return jax.shard_map(shards, mesh=mesh, in_specs=in_specs, out_specs=out_specs, check_vma=False)
```

profile of v0, /device:TPU:0, one launch (start us, length us, event | category | flops | bytes accessed | tf_op | source)
XLA Modules:
  0.0 712.5 jit_solution(1599837337625001319)
XLA Ops:
  7.3 2.5 convert_reduce_fusion
  11.9 5.6 convolution_convert_fusion
  17.5 3.1 fusion.82
  20.6 4.7 copy.89
  28.0 2.4 convolution_convert_fusion.6
  32.2 9.0 %multiply_reduce_fusion = (f32[4,12,128]{2,1,0:T(8,128)}, f32[4,12,128,512]{3,2,1,0:T(8,128)}) fusion(bf16[4,512,12,64]{1,3,2,0:T(8,128)(2,1)} %bitcast.140, bf16[128,12,64]{0,2,1:T(8,128)(2,1)} %bitcast.155), kind=kOutput, calls=%fused_computation.5 | convolution fusion | flops 408938496 | bytes 15949824 | tf_op jit(solution)/shard_map/iqhe,ikhe->ihqk/dot_general | solution.py:85
  41.2 11.2 %pmax.7 = f32[4,12,128]{2,1,0:T(8,128)} all-reduce(f32[4,12,128]{2,1,0:T(8,128)} %get-tuple-element.47), channel_id=1, replica_groups=mesh['items'=16,'frames'=2] {'frames'}, use_global_device_ids=true, to_apply=%region_5.0 | all-reduce | flops 6144 | bytes 49152 | tf_op jit(solution)/shard_map/pmax | solution.py:89
  52.4 7.0 exponential_reduce_fusion
  59.4 8.1 %psum.105 = f32[4,12,128]{2,1,0:T(8,128)} all-reduce(f32[4,12,128]{2,1,0:T(8,128)} %exponential_reduce_fusion), channel_id=1, replica_groups=mesh['items'=16,'frames'=2] {'frames'}, use_global_device_ids=true, to_apply=%region_7.0 | all-reduce | flops 6144 | bytes 49152 | tf_op jit(solution)/shard_map/psum | solution.py:90
  68.9 4.6 copy.87
  73.5 9.3 %fusion.58 = f32[4,12,64,128]{3,2,1,0:T(8,128)} fusion(bf16[4,512,12,64]{1,3,2,0:T(8,128)(2,1)} %bitcast.138, f32[4,12,128,512]{3,2,1,0:T(8,128)} %get-tuple-element.48, f32[4,12,128]{2,1,0:T(8,128)} %log_add_fusion), kind=kOutput, calls=%fused_computation.100 | convolution fusion | flops 412090368 | bytes 17326080 | tf_op jit(solution)/shard_map/ihqk,ikhe->iqhe/dot_general | solution.py:94
  82.8 3.0 copy.90
  88.1 3.2 convolution_convert_fusion.4
  91.3 2.3 copy.96
  93.6 45.5 %all-reduce.7.cloned.1.call-done = f32[4,128,768]{2,1,0:T(8,128)} async-done(((f32[4,128,768]{2,1,0:T(8,128)}), f32[4,128,768]{2,1,0:T(8,128)}) %all-reduce.7.cloned.1.call-update) | async-done | bytes 1572880 | tf_op jit(solution)/shard_map/psum | solution.py:96
  139.1 2.7 fusion.84
  142.8 5.4 fusion.28
  148.2 3.8 fusion.85
  162.9 4.9 fusion.86
  167.8 2.4 fusion.51
  181.6 2.3 copy.102
  183.9 2.3 copy.103
  186.2 5.3 multiply_reduce_fusion.3
  192.2 9.6 %fusion.21 = bf16[4,128,3072]{2,1,0:T(8,128)(2,1)S(1)} fusion(f32[4,128,3072]{2,1,0:T(8,128)} %copy-done.68, bf16[3072,768]{1,0:T(8,128)(2,1)} %param.26, f32[4,128,768]{2,1,0:T(8,128)S(1)} %multiply_add_fusion.1), kind=kOutput, calls=%fused_computation.29 | convolution fusion | flops 2447769600 | bytes 15728640 | tf_op jit(solution)/shard_map/irn,kn->irk/dot_general | solution.py:32
  201.8 3.0 multiply_reduce_fusion.4
  209.3 3.2 copy.140
  214.5 7.5 %multiply_convert_fusion = bf16[4,12,128,512]{3,2,1,0:T(8,128)(2,1)S(1)} fusion(f32[4,12,128,512]{3,2,1,0:T(8,128)} %get-tuple-element.48, f32[4,12,128]{2,1,0:T(8,128)S(1)} %fusion.45, f32[4,12,128]{2,1,0:T(8,128)S(1)} %copy-done.42, bf16[4,128,12,64]{1,3,2,0:T(8,128)(2,1)S(1)} %bitcast.143, bf16[4,512,12,64]{1,3,2,0:T(8,128)(2,1)S(1)} %bitcast.139), kind=kOutput, calls=%fused_computation.1 | convolution fusion | flops 418381824 | bytes 22855680 | tf_op jit(solution)/shard_map/iqhe,ikhe->ihqk/dot_general | solution.py:176
  222.0 3.4 convolution_multiply_fusion
  225.4 2.7 multiply_convert_fusion.1
  228.2 4.7 copy.106
  232.9 7.6 %convolution_convert_fusion.2 = bf16[4,12,64,512]{3,2,1,0:T(8,128)(2,1)} fusion(bf16[4,128,12,64]{1,3,2,0:T(8,128)(2,1)S(1)} %bitcast.144, f32[4,12,128,512]{3,2,1,0:T(8,128)} %get-tuple-element.48, f32[4,12,128]{2,1,0:T(8,128)S(1)} %copy-done.42), kind=kOutput, calls=%fused_computation.60 | convolution fusion | flops 413663232 | bytes 16539648 | tf_op jit(solution)/shard_map/ihqk,iqhe->ikhe/dot_general | solution.py:192
  240.5 4.9 copy.107
  245.4 10.4 %fusion.32 = f32[768,1536]{1,0:T(8,128)} fusion(bf16[4,512,768]{2,1,0:T(8,128)(2,1)} %copy.107, bf16[4,512,768]{2,1,0:T(8,128)(2,1)} %copy.106, bf16[4,512,768]{2,1,0:T(8,128)(2,1)S(1)} %copy-done.5, f32[768]{0:T(1024)S(1)} %copy-done.62, f32[4,512]{1,0:T(4,128)S(1)} %copy-done.56, f32[4,512]{1,0:T(4,128)S(1)} %copy-done.46), kind=kOutput, calls=%fused_computation.49 | convolution fusion | flops 4852285440 | bytes 14175232 | tf_op jit(solution)/shard_map/irk,irn->kn/dot_general | solution.py:36
  256.3 2.9 convolution_bitcast_fusion.4
  268.9 2.8 convolution_bitcast_fusion.2
  271.7 2.7 constant_dynamic-slice_fusion.3
  274.4 3.3 convolution_bitcast_fusion.1
  277.7 2.5 constant_dynamic-slice_fusion.2
  282.6 2.3 fusion.72
  288.2 54.5 %reduce-scatter.2.cloned.1.call-done = f32[768,768]{1,0:T(8,128)} async-done(((f32[768,1536]{1,0:T(8,128)}), f32[768,768]{1,0:T(8,128)}) %reduce-scatter.2.cloned.1.call-update) | async-done | bytes 2359312 | tf_op jit(solution)/shard_map/reduce_scatter | solution.py:239
  344.7 10.5 %fusion.13 = (f32[768]{0:T(1024)S(1)}, f32[4,512]{1,0:T(4,128)S(1)}, f32[4,512]{1,0:T(4,128)S(1)}, f32[4,512,768]{2,1,0:T(8,128)}) fusion(bf16[4,512,768]{2,1,0:T(8,128)(2,1)S(1)} %copy-done.5, f32[4,512]{1,0:T(4,128)S(1)} %copy-done.56, f32[4,512]{1,0:T(4,128)S(1)} %copy-done.46, f32[768]{0:T(1024)S(1)} %copy-done.62, bf16[768,1536]{1,0:T(8,128)(2,1)} %param.23, ...), kind=kOutput, calls=%fused_computation.21 | convolution fusion | flops 4858571776 | bytes 18126848 | tf_op jit(solution)/shard_map/irn,kn->irk/dot_general | solution.py:32
  355.3 4.9 all-reduce
  360.3 2.4 fusion.53
  363.5 5.1 fusion.12
  368.7 36.2 %all-reduce.1 = (f32[384]{0:T(512)}, f32[384]{0:T(512)}, f32[384]{0:T(512)}, f32[384]{0:T(512)}) all-reduce(f32[384]{0:T(512)S(1)} %dynamic-slice.1, f32[384]{0:T(512)S(1)} %dynamic_slice.35, f32[384]{0:T(512)S(1)} %dynamic_slice.36, f32[384]{0:T(512)S(1)} %dynamic_slice.37), channel_id=1, replica_groups=mesh['items'=16,'frames'=2] {'items'}, use_global_device_ids=true, to_apply=%region_28.0 | all-reduce | flops 1536 | bytes 12288 | tf_op jit(solution)/shard_map/psum | solution.py:221
  404.9 283.4 %all-reduce.11.cloned.1.call-done = (f32[128,384]{1,0:T(8,128)}, f32[768,384]{1,0:T(8,128)}, f32[768,768]{1,0:T(8,128)}, f32[768,384]{1,0:T(8,128)}, f32[768,153...) async-done(((f32[128,384]{1,0:T(8,128)}, f32[768,384]{1,0:T(8,128)}, f32[768,768]{1,0:T(8,128)}, f32[768,384]{1,0:T(8,128)}, ...) | async-done | bytes 19070992 | tf_op jit(solution)/shard_map/psum | solution.py:221
  690.1 2.5 copy.154
  698.7 2.4 copy.158
  (231 shorter events, 71.0 us)
Async XLA Ops:
  7.2 145.3 %copy-start = (bf16[768,2304]{1,0:T(8,128)(2,1)S(1)}, bf16[768,2304]{1,0:T(8,128)(2,1)}, u32[]{:S(2)}) copy-start(bf16[768,2304]{1,0:T(8,128)(2,1)} %param.27) | copy-start | bytes 10616836
  7.2 4.7 copy-start.61
  7.2 131.9 %all-reduce.7.cloned.1.call-start = ((), (), s32[]{:S(2)}) async-start(), calls=%async_computation.1 | async-start | bytes 3145728 | tf_op jit(solution)/shard_map/psum | solution.py:96
  7.3 4.7 copy-start.66
  20.6 7.4 %copy-start.52 = (f32[768]{0:T(1024)S(1)}, f32[768]{0:T(1024)}, u32[]{:S(2)}) copy-start(f32[768]{0:T(1024)} %param.19) | copy-start | bytes 9220
  85.9 7.7 %copy-start.67 = (s32[4]{0:T(128)S(1)}, s32[4]{0:T(128)}, u32[]{:S(2)}) copy-start(s32[4]{0:T(128)} %param.16) | copy-start | bytes 52
  85.9 194.4 %all-reduce.9.cloned.1.call-start = ((), (), s32[]{:S(2)}) async-start(), calls=%async_computation.2 | async-start | bytes 3145728 | tf_op jit(solution)/shard_map/psum | solution.py:187
  93.6 48.2 %copy-start.63 = (f32[4]{0:T(128)}, f32[4]{0:T(128)S(1)}, u32[]{:S(2)}) copy-start(f32[4]{0:T(128)S(1)} %subtract_convert_fusion) | copy-start | bytes 52
  93.6 49.1 %copy-start.43 = (f32[768]{0:T(1024)S(1)}, f32[768]{0:T(1024)}, u32[]{:S(2)}) copy-start(f32[768]{0:T(1024)} %param.20) | copy-start | bytes 9220
  141.8 6.4 copy-start.6
  141.8 6.4 slice-start.2
  142.7 5.5 slice-start.3
  148.2 3.9 copy-start.68
  148.2 4.2 copy-start.44
  186.2 5.3 copy-start.10
  186.2 5.3 copy-start.30
  186.2 5.3 copy-start.48
  191.6 10.2 %slice-start.4 = ((s8[4718592]{0:T(1024)(128)(4,1)}), s8[4194304]{0:T(1024)(128)(4,1)S(1)}, s32[]{:S(2)}) async-start(s8[4718592]{0:T(1024)(128)(4,1)} %bitcast.170), calls=%async_computation.9 | async-start | bytes 8388608
  192.2 12.7 %copy-start.18 = (f32[4,128,768]{2,1,0:T(8,128)}, f32[4,128,768]{2,1,0:T(8,128)S(1)}, u32[]{:S(2)}) copy-start(f32[4,128,768]{2,1,0:T(8,128)S(1)} %multiply_add_fusion.1) | copy-start | bytes 4718596
  192.2 9.6 %copy-start.7 = (f32[4,128,768]{2,1,0:T(8,128)S(1)}, f32[4,128,768]{2,1,0:T(8,128)}, u32[]{:S(2)}) copy-start(f32[4,128,768]{2,1,0:T(8,128)} %copy-done.6) | copy-start | bytes 4718596
  192.2 9.6 %copy-start.51 = (f32[4,128]{1,0:T(4,128)S(1)}, f32[4,128]{1,0:T(4,128)}, u32[]{:S(2)}) copy-start(f32[4,128]{1,0:T(4,128)} %copy-done.50) | copy-start | bytes 6148
  192.2 9.6 %slice-start.5 = ((s8[4718592]{0:T(1024)(128)(4,1)}), s8[524288]{0:T(1024)(128)(4,1)S(1)}, s32[]{:S(2)}) async-start(s8[4718592]{0:T(1024)(128)(4,1)} %bitcast.170), calls=%async_computation.10 | async-start | bytes 1048576
  209.3 5.2 copy-start.2
  209.3 5.2 copy-start.42
  214.5 7.5 %copy-start.3 = (bf16[4,512,768]{1,2,0:T(8,128)(2,1)S(1)}, bf16[4,512,768]{1,2,0:T(8,128)(2,1)}, u32[]{:S(2)}) copy-start(bf16[4,512,768]{1,2,0:T(8,128)(2,1)} %copy.89) | copy-start | bytes 9437188
  228.1 114.6 %reduce-scatter.2.cloned.1.call-start = ((), (), s32[]{:S(2)}) async-start(), calls=%async_computation.3 | async-start | bytes 7077888 | tf_op jit(solution)/shard_map/reduce_scatter | solution.py:239
  228.2 4.8 copy-start.14
  240.5 4.9 copy-start.5
  240.5 4.9 copy-start.46
  240.5 4.9 copy-start.56
  240.5 4.9 copy-start.62
  255.8 432.6 %all-reduce.11.cloned.1.call-start = ((), (), s32[]{:S(2)}) async-start(), calls=%async_computation.4 | async-start | bytes 38141952 | tf_op jit(solution)/shard_map/psum | solution.py:221
  256.3 4.0 copy-start.15
  256.3 4.0 copy-start.31
  265.3 3.6 copy-start.33
  265.3 9.1 %slice-start.6 = ((s8[6291456]{0:T(1024)(128)(4,1)}), s8[4194304]{0:T(1024)(128)(4,1)S(1)}, s32[]{:S(2)}) async-start(s8[6291456]{0:T(1024)(128)(4,1)} %bitcast.172), calls=%async_computation.11 | async-start | bytes 8388608
  268.9 5.5 slice-start.7
  277.7 4.9 copy-start.17
  277.7 4.9 copy-start.53
  277.7 4.8 copy-start.58
  277.7 4.8 copy-start.60
  282.5 3.5 copy-start.23
  688.4 4.2 copy-start.37
  690.1 3.9 copy-start.39
  692.6 3.6 copy-start.22
  694.0 4.4 slice-start
  698.7 3.7 copy-start.24
  698.7 7.1 copy-start.1
  (34 other events, 69.9 us)
Sparse Core Ops, SparseCore 0:
  86.0 53.0 all-reduce.6
  228.3 51.4 all-reduce.8
  282.7 59.9 reduce-scatter.1
  350.1 338.2 all-reduce.10
where the time goes:
time: 722 us; the launch traced here: 713 us
  waiting for transfers between devices  383 us (53%)
  matrix products  135 us (19%)
  local copies, waits for them, and re-layouts  85 us (12%)
  blocking collectives  60.5 us (8%)
  other arithmetic  32.2 us (4%)
  between operations  15.5 us (2%)
    psum x1, waiting for transfers between devices, shards(): lax.psum((mine_latent, mine_query_gain, mine_mlp_gain, mine_self_gain, mi...  283 us
    reduce_scatter x1, waiting for transfers between devices, shards(): lax.psum_scatter(summed[10], 'frames', scatter_dimension=1, tiled=True)  54.5 us
    psum x1, waiting for transfers between devices, shards(): heard = lax.psum(heard_part, 'frames')  45.5 us
    psum x1, blocking collectives, shards(): lax.psum((mine_latent, mine_query_gain, mine_mlp_gain, mine_self_gain, mi...  36.2 us
    dot_general x6, matrix products, input_mul(): jnp.einsum('irn,kn->irk', grad_rows, weight, preferred_element_type=jnp.f...  32.4 us
    unnamed x167, local copies, waits for them, and re-layouts  28.7 us
    dot_general x6, matrix products, weight_mul(): jnp.einsum('irk,irn->kn', left, grad_rows, preferred_element_type=jnp.flo...  22.2 us
    dot_general x6, matrix products, forward_mul(): jnp.einsum('irk,kn->irn', left, weight, preferred_element_type=jnp.float32)  22 us
  transfers between devices with their start and end apart: 4, of which 3 were waited for; matrix products, arithmetic and copies ran while one was open for 12% of the time, Pallas kernels for 0%

commit v1 on v0

--- a/solution.py
+++ b/solution.py
@@ -1,6 +1,10 @@
+import functools
+
 import jax
 import jax.numpy as jnp
 from jax import lax
+from jax.experimental import pallas as pl
+from jax.experimental.pallas import tpu as pltpu
 from jax.sharding import PartitionSpec as P
 
 HEADS = 12
@@ -47,6 +51,285 @@
 def own_columns(gradient, column_index, parts):
     span = gradient.shape[-1] // parts
     return lax.dynamic_slice_in_dim(gradient, column_index * span, span, gradient.ndim - 1)
+
+
+def pack(array, pieces, width):
+    rows, columns = array.shape[-2] // pieces, array.shape[-1] // width
+    split = array.reshape(array.shape[:-2] + (pieces, rows, columns, width))
+    split = jnp.swapaxes(split, -3, -2)
+    return split.reshape(array.shape[:-2] + (pieces, columns * rows, width))
+
+
+def unpack(packed, rows, columns):
+    pieces, _, width = packed.shape
+    split = packed.reshape(pieces, columns // width, rows // pieces, width)
+    return jnp.swapaxes(split, 1, 2).reshape(rows, columns)
+
+
+def cut(packed, shapes):
+    width, start, out = packed.shape[-1], 0, []
+    for rows, columns in shapes:
+        count = rows * columns // width // packed.shape[0]
+        out.append(unpack(packed[:, start : start + count], rows, columns))
+        start += count
+    return out
+
+
+MESH = pl.DeviceIdType.MESH
+
+
+def add_into(target, parts, rows):
+    step = next(size for size in (104, 80, 64, 48, 40, 24, 16, 8) if rows % size == 0)
+
+    def body(index, carry):
+        window = pl.ds(pl.multiple_of(index * step, 8), step)
+        total = parts[0][window]
+        for part in parts[1:]:
+            total = total + part[window]
+        target[window] = total
+        return carry
+
+    lax.fori_loop(0, rows // step, body, 0)
+
+
+def reduce_kernel(
+    chips, frames, spans,
+    mid_ref, kv_ref, mid_out, kv_out,
+    mine, sib, rx, kmine, ksib, ky, krx,
+    ld_sem, sib_send, sib_recv, rs_send, rs_recv, ag_send, ag_recv, share_send, share_recv, own_sem,
+    kld_sem, ksib_send, ksib_recv, y_send, y_recv, krs_send, krs_recv, kag_send, kag_recv, kshare_send, kshare_recv,
+):
+    items = lax.axis_index("items")
+    frame = lax.axis_index("frames")
+    core = lax.rem(items, 2)
+    chip = items // 2
+    column = lax.rem(chip, 2)
+    line = chip // 2
+    place = line + column * (chips - 1 - 2 * line)
+    way = 1 - 2 * core
+
+    def device_at(position):
+        position = lax.rem(position + 2 * chips, chips)
+        far = position // (chips // 2)
+        return (2 * (position + far * (chips - 1 - 2 * position)) + far) * 2 + core
+
+    right, left = device_at(place + way), device_at(place - way)
+    sibling = items + way
+    kv_rows = kv_ref.shape[3]
+
+    def chunk(offset):
+        return lax.rem(place + way * offset + 2 * chips, chips)
+
+    def sib_chunk(offset):
+        return lax.rem(place - way * offset + 2 * chips, chips)
+
+    barrier = pltpu.get_barrier_semaphore()
+    for peer in (left, right, sibling):
+        pl.semaphore_signal(barrier, inc=1, device_id=(peer, frame), device_id_type=MESH)
+    for hop in range(1, frames):
+        pl.semaphore_signal(barrier, inc=1, device_id=(items, lax.rem(frame + hop, frames)), device_id_type=MESH)
+    pl.semaphore_wait(barrier, 3 + frames - 1)
+
+    def remote(src, dst, send, recv, peer):
+        return pltpu.make_async_remote_copy(
+            src_ref=src, dst_ref=dst, send_sem=send, recv_sem=recv, device_id=peer, device_id_type=MESH
+        )
+
+    def load(k):
+        return pltpu.make_async_copy(mid_ref.at[core, k], mine.at[k], ld_sem.at[k])
+
+    def pair(k):
+        return remote(mid_ref.at[1 - core, k], sib.at[k], sib_send.at[k], sib_recv.at[k], (sibling, frame))
+
+    def ring(j, k):
+        rows = pl.ds(*spans[j])
+        return remote(mine.at[k, rows], rx.at[k, rows], rs_send.at[j, k], rs_recv.at[j, k], (right, frame))
+
+    def gather(j, k, source):
+        rows = pl.ds(*spans[j])
+        return remote(source.at[k, rows], mid_out.at[core, k, rows], ag_send.at[j, k], ag_recv.at[j, k], (right, frame))
+
+    def share(j, k, source):
+        rows = pl.ds(*spans[j])
+        return remote(source.at[k, rows], mid_out.at[core, k, rows], share_send.at[j, k], share_recv.at[j, k], (sibling, frame))
+
+    def share_from(j, k):
+        rows = pl.ds(*spans[j])
+        return remote(mine.at[k, rows], mid_out.at[1 - core, k, rows], share_send.at[j, k], share_recv.at[j, k], (sibling, frame))
+
+    def kload(k):
+        return pltpu.make_async_copy(kv_ref.at[:, core, k], kmine.at[:, k], kld_sem.at[k])
+
+    def kpair(k):
+        return remote(kv_ref.at[:, 1 - core, k], ksib.at[:, k], ksib_send.at[k], ksib_recv.at[k], (sibling, frame))
+
+    def across(hop):
+        other = lax.rem(frame + hop, frames)
+        return remote(kmine.at[other], ky.at[hop - 1], y_send.at[hop - 1], y_recv.at[hop - 1], (items, other))
+
+    def kring(k):
+        return remote(kmine.at[frame, k], krx.at[k], krs_send.at[k], krs_recv.at[k], (right, frame))
+
+    def kgather(k, source):
+        return remote(source, kv_out.at[core, k], kag_send.at[k], kag_recv.at[k], (right, frame))
+
+    def kshare(k, source):
+        return remote(source, kv_out.at[core, k], kshare_send.at[k], kshare_recv.at[k], (sibling, frame))
+
+    def kshare_from(k):
+        return remote(kmine.at[frame, k], kv_out.at[1 - core, k], kshare_send.at[k], kshare_recv.at[k], (sibling, frame))
+
+    def start_stage(index, carry):
+        load(chunk(-index)).start()
+        pair(sib_chunk(-index)).start()
+        return carry
+
+    lax.fori_loop(0, chips, start_stage, 0)
+
+    def start_kstage(index, carry):
+        kload(index).start()
+        kpair(index).start()
+        return carry
+
+    lax.fori_loop(0, chips, start_kstage, 0)
+
+    def ring_step(step, first):
+        k = chunk(-step)
+        load(k).wait()
+        pair(k).wait_recv()
+        for j, (start, count) in enumerate(spans):
+            rows = pl.ds(start, count)
+            parts = [mine.at[k, rows], sib.at[k, rows]]
+            if not first:
+                ring(j, k).wait_recv()
+                parts.append(rx.at[k, rows])
+            add_into(mine.at[k, rows], parts, count)
+            ring(j, k).start()
+
+    ring_step(0, True)
+
+    def kstage(k, carry):
+        kload(k).wait()
+        kpair(k).wait_recv()
+        for f in range(frames):
+            add_into(kmine.at[f, k], [kmine.at[f, k], ksib.at[f, k]], kv_rows)
+        return carry
+
+    lax.fori_loop(0, chips, kstage, 0)
+    for hop in range(1, frames):
+        across(hop).start()
+
+    def ring_loop(step, carry):
+        ring_step(step, False)
+        return carry
+
+    lax.fori_loop(1, chips - 1, ring_loop, 0)
+
+    k = chunk(1)
+    load(k).wait()
+    pair(k).wait_recv()
+    for j, (start, count) in enumerate(spans):
+        rows = pl.ds(start, count)
+        ring(j, k).wait_recv()
+        add_into(mine.at[k, rows], [mine.at[k, rows], sib.at[k, rows], rx.at[k, rows]], count)
+        gather(j, k, mine).start()
+        share(j, k, mine).start()
+        pltpu.make_async_copy(mine.at[k, rows], mid_out.at[core, k, rows], own_sem.at[j]).start()
+
+    for hop in range(1, frames):
+        across(hop).wait_recv()
+
+    def kstep(step):
+        k = chunk(-step)
+        if step < chips:
+            parts = [kmine.at[frame, k]] + [ky.at[hop, k] for hop in range(frames - 1)]
+            if step > 0:
+                kring(k).wait_recv()
+                parts.append(krx.at[k])
+            add_into(kmine.at[frame, k], parts, kv_rows)
+            if step < chips - 1:
+                kring(k).start()
+            else:
+                kgather(k, kmine.at[frame, k]).start()
+                kshare(k, kmine.at[frame, k]).start()
+                pltpu.make_async_copy(kmine.at[frame, k], kv_out.at[core, k], own_sem.at[len(spans)]).start()
+        else:
+            kgather(k, kmine.at[frame, k]).wait_recv()
+            if step < 2 * chips - 2:
+                kgather(k, kv_out.at[core, k]).start()
+            kshare(k, kv_out.at[core, k]).start()
+
+    kdone = 0
+    for step in range(1, chips):
+        k = chunk(1 - step)
+        for j in range(len(spans)):
+            gather(j, k, mine).wait_recv()
+            if step < chips - 1:
+                gather(j, k, mid_out.at[core]).start()
+            share(j, k, mid_out.at[core]).start()
+            if kdone < 2 * chips - 1:
+                kstep(kdone)
+                kdone += 1
+    for step in range(kdone, 2 * chips - 1):
+        kstep(step)
+
+    def drain(k, carry):
+        pair(k).wait_send()
+        kpair(k).wait_send()
+        for j in range(len(spans)):
+            share(j, k, mine).wait_send()
+            share_from(j, k).wait_recv()
+        kshare(k, kmine.at[frame, k]).wait_send()
+        kshare_from(k).wait_recv()
+        return carry
+
+    lax.fori_loop(0, chips, drain, 0)
+
+    def drain_ring(step, carry):
+        for j in range(len(spans)):
+            ring(j, chunk(-step)).wait_send()
+            gather(j, chunk(1 - step), mine).wait_send()
+        kring(chunk(-step)).wait_send()
+        kgather(chunk(1 - step), kmine.at[frame, 0]).wait_send()
+        return carry
+
+    lax.fori_loop(0, chips - 1, drain_ring, 0)
+    for hop in range(1, frames):
+        across(hop).wait_send()
+    k = chunk(1)
+    for j, (start, count) in enumerate(spans):
+        rows = pl.ds(start, count)
+        pltpu.make_async_copy(mine.at[k, rows], mid_out.at[core, k, rows], own_sem.at[j]).wait()
+    pltpu.make_async_copy(kmine.at[frame, k], kv_out.at[core, k], own_sem.at[len(spans)]).wait()
+
+
+def reduce_all(mid, kv):
+    chips, rows, width = mid.shape[1:]
+    frames, kv_rows = kv.shape[0], kv.shape[3]
+    half = (rows // 16 + 1) // 2 * 8
+    spans = ((0, rows - half), (rows - half, half))
+    dma = pltpu.SemaphoreType.DMA
+    n = len(spans)
+    f32 = jnp.float32
+    scratch = [
+        pltpu.VMEM((chips, rows, width), f32), pltpu.VMEM((chips, rows, width), f32), pltpu.VMEM((chips, rows, width), f32),
+        pltpu.VMEM((frames, chips, kv_rows, width), f32), pltpu.VMEM((frames, chips, kv_rows, width), f32),
+        pltpu.VMEM((max(frames - 1, 1), chips, kv_rows, width), f32), pltpu.VMEM((chips, kv_rows, width), f32),
+        dma((chips,)), dma((chips,)), dma((chips,)),
+        dma((n, chips)), dma((n, chips)), dma((n, chips)), dma((n, chips)), dma((n, chips)), dma((n, chips)), dma((n + 1,)),
+        dma((chips,)), dma((chips,)), dma((chips,)),
+        dma((max(frames - 1, 1),)), dma((max(frames - 1, 1),)),
+        dma((chips,)), dma((chips,)), dma((chips,)), dma((chips,)), dma((chips,)), dma((chips,)),
+    ]
+    return pl.pallas_call(
+        functools.partial(reduce_kernel, chips, frames, spans),
+        out_shape=(jax.ShapeDtypeStruct(mid.shape, f32), jax.ShapeDtypeStruct(kv.shape[1:], f32)),
+        in_specs=[pl.BlockSpec(memory_space=pl.ANY)] * 2,
+        out_specs=(pl.BlockSpec(memory_space=pl.ANY),) * 2,
+        scratch_shapes=scratch,
+        compiler_params=pltpu.CompilerParams(collective_id=0, has_side_effects=True, vmem_limit_bytes=56 * 2**20),
+        name="reduce_all",
+    )(mid, kv)
 
 
 def shards(
@@ -127,7 +410,7 @@
         after_self, frame_index * latent_share, latent_share, 1
     ).astype(jnp.bfloat16)
     cotangent = grad_out.astype(jnp.float32)
-    grad_self_out = weight_mul(mixed_low, grad_out)
+    grad_self_out = weight_mul(mixed_low, own_columns(grad_out, frame_index, frame_count))
     d_mixed = input_mul(grad_out, w_self_out).astype(jnp.bfloat16)
     d_mixed_heads = split_heads(d_mixed)
     d_self_probs = jnp.einsum(
@@ -149,22 +432,22 @@
     d_triple = jnp.concatenate(
         [join_heads(d_self_query), join_heads(d_self_key), join_heads(d_self_value)], axis=-1
     ).astype(jnp.bfloat16)
-    grad_self_qkv = weight_mul(self_in, d_triple)
+    grad_self_qkv = weight_mul(self_in, own_columns(d_triple, frame_index, frame_count))
     self_back, grad_self_gain = norm_back(
         input_mul(d_triple, w_self_qkv), self_normed, self_inverse, self_gain
     )
     d_after_mlp = cotangent + self_back
     mlp_branch = d_after_mlp.astype(jnp.bfloat16)
-    grad_down = weight_mul(activation_low, mlp_branch)
+    grad_down = weight_mul(activation_low, own_columns(mlp_branch, frame_index, frame_count))
     d_activation = input_mul(mlp_branch, w_down)
     d_hidden = gelu_pull(d_activation)[0].astype(jnp.bfloat16)
-    grad_up = weight_mul(mlp_in, d_hidden)
+    grad_up = weight_mul(mlp_in, own_columns(d_hidden, frame_index, frame_count))
     mlp_back, grad_mlp_gain = norm_back(
         input_mul(d_hidden, w_up), mlp_normed, mlp_inverse, mlp_gain
     )
     d_after_cross = d_after_mlp + mlp_back
     d_attn = (keep_flag * d_after_cross).astype(jnp.bfloat16)
-    grad_out_w = weight_mul(heard_low, d_attn)
+    grad_out_w = weight_mul(heard_low, own_columns(d_attn, frame_index, frame_count))
     d_heard = input_mul(d_attn, w_out).astype(jnp.bfloat16)
     d_heard_heads = split_heads(d_heard)
     again_scores = (
@@ -184,7 +467,7 @@
         jnp.einsum("ihqk,ikhe->iqhe", d_scores, key_heads, preferred_element_type=jnp.float32)
         * factor
     )
-    query_total = jnp.sum(lax.psum(query_part, "frames"), axis=0)
+    query_total = jnp.sum(query_part, axis=0)
     d_keys = (
         jnp.einsum("ihqk,iqhe->ikhe", d_scores, query_heads, preferred_element_type=jnp.float32)
         * factor
@@ -200,60 +483,68 @@
         input_mul(d_keyval, w_keyval), tok_normed, tok_inverse, tok_gain
     )
     token_grad = token_back.astype(jnp.bfloat16)
-    grad_query_w = jnp.dot(
-        query_in.astype(jnp.float32).T, query_total, precision=lax.Precision.HIGHEST
-    )
     query_incoming = jnp.dot(
         query_total, w_query.astype(jnp.float32).T, precision=lax.Precision.HIGHEST
     )
-    query_back, grad_query_gain = norm_back(query_incoming, query_normed, query_inverse, query_gain)
-    grad_latent = jnp.sum(d_after_cross, axis=0) + query_back
-    mine_latent = own_columns(grad_latent, frame_index, frame_count)
-    mine_query_gain = own_columns(grad_query_gain, frame_index, frame_count)
-    mine_mlp_gain = own_columns(grad_mlp_gain, frame_index, frame_count)
-    mine_self_gain = own_columns(grad_self_gain, frame_index, frame_count)
-    mine_query_w = own_columns(grad_query_w, frame_index, frame_count)
-    mine_out_w = own_columns(grad_out_w, frame_index, frame_count)
-    mine_up = own_columns(grad_up, frame_index, frame_count)
-    mine_down = own_columns(grad_down, frame_index, frame_count)
-    mine_self_qkv = own_columns(grad_self_qkv, frame_index, frame_count)
-    mine_self_out = own_columns(grad_self_out, frame_index, frame_count)
-    summed = lax.psum(
+    query_back, query_gain_part = norm_back(query_incoming, query_normed, query_inverse, query_gain)
+    own = width // frame_count
+    item_devices = lax.axis_size("items")
+    mid = jnp.concatenate(
+        [pack(part, item_devices, own) for part in (grad_out_w, grad_up, grad_down, grad_self_qkv, grad_self_out)],
+        axis=1,
+    )
+
+    def blocks(array):
+        return jnp.swapaxes(array.reshape(array.shape[0], frame_count, array.shape[1] // frame_count), 0, 1)
+
+    mine_only = (jnp.arange(frame_count) == frame_index).astype(jnp.float32)[:, None, None]
+    latent_part = blocks(query_back) + mine_only * blocks(jnp.sum(d_after_cross, axis=0))
+    gains = jnp.stack([grad_mlp_gain, grad_self_gain, tok_gain_part, query_gain_part])
+    gain_part = blocks(gains) * jnp.where(jnp.arange(4)[None, :, None] < 2, mine_only, 1.0)
+    gain_part = jnp.pad(gain_part, ((0, 0), (0, 8 * item_devices - 4), (0, 0)))
+    small = jnp.concatenate([blocks(query_total), latent_part], axis=1)
+    kv = jnp.concatenate(
+        [pack(blocks(keyval_part), item_devices, own), pack(small, item_devices, own), pack(gain_part, item_devices, own)],
+        axis=2,
+    )
+    chips = item_devices // 2
+    mid_sum, kv_sum = reduce_all(
+        mid.reshape(2, chips, mid.shape[1], own), kv.reshape(frame_count, 2, chips, kv.shape[2], own)
+    )
+    mid_sum = mid_sum.reshape(mid.shape)
+    kv_sum = kv_sum.reshape(kv.shape[1:])
+    hidden_width = w_up.shape[1]
+    sum_out, sum_up, sum_down, sum_qkv, sum_self_out = cut(
+        mid_sum,
         (
-            mine_latent,
-            mine_query_gain,
-            mine_mlp_gain,
-            mine_self_gain,
-            mine_query_w,
-            mine_out_w,
-            mine_up,
-            mine_down,
-            mine_self_qkv,
-            mine_self_out,
-            keyval_part,
-            tok_gain_part,
+            (width, own),
+            (width, hidden_width // frame_count),
+            (hidden_width, own),
+            (width, 3 * own),
+            (width, own),
         ),
-        "items",
-    )
-    keyval_grad, tok_gain_grad = (
-        lax.psum_scatter(summed[10], "frames", scatter_dimension=1, tiled=True),
-        lax.psum_scatter(summed[11], "frames", scatter_dimension=0, tiled=True),
+    )
+    sum_keyval, sum_small, sum_gains = cut(
+        kv_sum, ((width, 2 * own), (2 * latent_count, own), (8 * item_devices, own))
+    )
+    grad_query_w = jnp.dot(
+        query_in.astype(jnp.float32).T, sum_small[:latent_count], precision=lax.Precision.HIGHEST
     )
     return (
         out_latents,
         token_grad,
-        summed[0],
-        tok_gain_grad,
-        summed[1],
-        summed[2],
-        summed[3],
-        summed[4],
-        keyval_grad,
-        summed[5],
-        summed[6],
-        summed[7],
-        summed[8],
-        summed[9],
+        sum_small[latent_count:],
+        sum_gains[2],
+        sum_gains[3],
+        sum_gains[0],
+        sum_gains[1],
+        grad_query_w,
+        sum_keyval,
+        sum_out,
+        sum_up,
+        sum_down,
+        sum_qkv,
+        sum_self_out,
     )
 
 

time: 722 us -> 586 us (0.81)
  waiting for transfers between devices: 383 us -> 44.9 us
  Pallas kernels: 0 us -> 194 us
  local copies, waits for them, and re-layouts: 85 us -> 135 us
  blocking collectives: 60.5 us -> 19.8 us
    psum x2 -> x0, waiting for transfers between devices: 283 us -> none  [the longest x1 283 us: shards(): lax.psum((mine_latent, mine_query_gain, mine_mlp_gain, mine_self_gain, mi...]
    pallas_call x0 -> x1, Pallas kernels: none -> 194 us  [reduce_all(): pl.pallas_call(functools.partial(reduce_kernel, chips, frames, spans), ou...]
    reduce_scatter x1 -> x0, waiting for transfers between devices: 54.5 us -> none  [shards(): lax.psum_scatter(summed[10], 'frames', scatter_dimension=1, tiled=True)]
    psum x1 -> x0, blocking collectives: 36.2 us -> none  [shards(): lax.psum((mine_latent, mine_query_gain, mine_mlp_gain, mine_self_gain, mi...]
    reshape x0 -> x7, local copies, waits for them, and re-layouts: none -> 30.4 us  [the longest x4 24.2 us: pack(): split = array.reshape(array.shape[:-2] + (pieces, rows, columns, width))]
    slice x0 -> x6, local copies, waits for them, and re-layouts: none -> 16.4 us  [the longest x4 14.1 us: cut(): out.append(unpack(packed[:, start:start + count], rows, columns))]
    transpose x0 -> x4, local copies, waits for them, and re-layouts: none -> 13.1 us  [the longest x2 9.5 us: pack(): split = jnp.swapaxes(split, -3, -2)]
    dynamic_slice x9 -> x0, local copies, waits for them, and re-layouts: 10.8 us -> none  [own_columns(): lax.dynamic_slice_in_dim(gradient, column_index * span, span, gradient.nd...]
  transfers between devices with their start and end apart: 4 -> 1, of which waited for: 3 -> 1; matrix products, arithmetic and copies ran while one was open for 12% -> 1% of each run, Pallas kernels for 0% -> 0%
where the time goes in v1:
time: 586 us; the launch traced here: 578 us
  Pallas kernels  194 us (33%)
  local copies, waits for them, and re-layouts  135 us (23%)
  matrix products  134 us (23%)
  waiting for transfers between devices  44.9 us (8%)
  other arithmetic  34.4 us (6%)
  blocking collectives  19.8 us (3%)
  between operations  15.4 us (3%)
    pallas_call x1, Pallas kernels, reduce_all(): pl.pallas_call(functools.partial(reduce_kernel, chips, frames, spans), ou...  194 us
    psum x1, waiting for transfers between devices, shards(): heard = lax.psum(heard_part, 'frames')  44.9 us
    dot_general x6, matrix products, input_mul(): jnp.einsum('irn,kn->irk', grad_rows, weight, preferred_element_type=jnp.f...  29.8 us
    unnamed x194, local copies, waits for them, and re-layouts  27.8 us
    dot_general x6, matrix products, weight_mul(): jnp.einsum('irk,irn->kn', left, grad_rows, preferred_element_type=jnp.flo...  27.4 us
    reshape x4, local copies, waits for them, and re-layouts, pack(): split = array.reshape(array.shape[:-2] + (pieces, rows, columns, width))  24.2 us
    dot_general x6, matrix products, forward_mul(): jnp.einsum('irk,kn->irn', left, weight, preferred_element_type=jnp.float32)  22.8 us
    reshape x6, local copies, waits for them, and re-layouts, join_heads(): values.reshape(values.shape[0], values.shape[1], values.shape[2] * values...  17.4 us
  transfers between devices with their start and end apart: 1, of which 1 were waited for; matrix products, arithmetic and copies ran while one was open for 1% of the time, Pallas kernels for 0%

profile of v1, /device:TPU:0, one launch (start us, length us, event | category | flops | bytes accessed | tf_op | source)
XLA Modules:
  0.0 577.6 jit_solution(10346918962520584409)
XLA Ops:
  9.8 2.5 convert_reduce_fusion
  16.2 7.7 %convolution_convert_fusion = bf16[4,512,1536]{2,1,0:T(8,128)(2,1)S(1)} fusion(bf16[768,1536]{1,0:T(8,128)(2,1)} %param.23, bf16[4,512,768]{2,1,0:T(8,128)(2,1)} %param.15, f32[768]{0:T(1024)} %param.18, f32[4,512]{1,0:T(4,128)S(1)} %add_rsqrt_fusion, f32[4,512]{1,0:T(4,128)S(1)} %broadcast_multiply_fusion.2), kind=kOutput, calls=%fused_computation.35 | convolution fusion | flops 4842848256 | bytes 11815936 | tf_op jit(solution)/shard_map/irk,kn->irn/dot_general | solution.py:32
  24.0 3.1 fusion.93
  27.1 4.6 copy.141
  31.8 4.6 copy.139
  36.4 9.0 %multiply_reduce_fusion = (f32[4,12,128]{2,1,0:T(8,128)}, f32[4,12,128,512]{3,2,1,0:T(8,128)}) fusion(bf16[4,512,12,64]{1,3,2,0:T(8,128)(2,1)} %bitcast.202, bf16[128,12,64]{0,2,1:T(8,128)(2,1)} %bitcast.235), kind=kOutput, calls=%fused_computation.5 | convolution fusion | flops 408938496 | bytes 15949824 | tf_op jit(solution)/shard_map/iqhe,ikhe->ihqk/dot_general | solution.py:368
  45.4 11.2 %pmax.7 = f32[4,12,128]{2,1,0:T(8,128)} all-reduce(f32[4,12,128]{2,1,0:T(8,128)} %get-tuple-element.47), channel_id=1, replica_groups=mesh['items'=16,'frames'=2] {'frames'}, use_global_device_ids=true, to_apply=%region_5.0 | all-reduce | flops 6144 | bytes 49152 | tf_op jit(solution)/shard_map/pmax | solution.py:372
  56.6 7.0 %exponential_reduce_fusion = f32[4,12,128]{2,1,0:T(8,128)} fusion(f32[4,12,128,512]{3,2,1,0:T(8,128)} %get-tuple-element.48, f32[4,12,128]{2,1,0:T(8,128)} %pmax.7), kind=kLoop, calls=%fused_computation.3 | loop fusion | flops 9431040 | bytes 12632064 | tf_op jit(solution)/shard_map/reduce_sum | solution.py:373
  63.6 8.6 %psum.14 = f32[4,12,128]{2,1,0:T(8,128)} all-reduce(f32[4,12,128]{2,1,0:T(8,128)} %exponential_reduce_fusion), channel_id=1, replica_groups=mesh['items'=16,'frames'=2] {'frames'}, use_global_device_ids=true, to_apply=%region_7.0 | all-reduce | flops 6144 | bytes 49152 | tf_op jit(solution)/shard_map/psum | solution.py:373
  73.0 9.4 %fusion.59 = f32[4,12,64,128]{3,2,1,0:T(8,128)} fusion(bf16[4,512,12,64]{1,3,2,0:T(8,128)(2,1)} %bitcast.200, f32[4,12,128,512]{3,2,1,0:T(8,128)} %get-tuple-element.48, f32[4,12,128]{2,1,0:T(8,128)S(1)} %log_add_fusion), kind=kOutput, calls=%fused_computation.101 | convolution fusion | flops 412090368 | bytes 17326080 | tf_op jit(solution)/shard_map/ihqk,ikhe->iqhe/dot_general | solution.py:377
  82.4 3.0 copy.142
  87.2 3.2 convolution_convert_fusion.4
  93.8 44.9 %all-reduce.3.cloned.1.call-done = f32[4,128,768]{2,1,0:T(8,128)} async-done(((f32[4,128,768]{2,1,0:T(8,128)}), f32[4,128,768]{2,1,0:T(8,128)}) %all-reduce.3.cloned.1.call-update) | async-done | bytes 1572880 | tf_op jit(solution)/shard_map/psum | solution.py:379
  138.7 2.7 fusion.96
  142.4 5.6 fusion.28
  148.0 3.8 fusion.97
  162.7 4.9 fusion.98
  167.6 2.4 fusion.51
  178.9 2.3 copy.155
  185.8 5.4 multiply_reduce_fusion.3
  195.2 8.9 %fusion.21 = bf16[4,128,3072]{2,1,0:T(8,128)(2,1)S(1)} fusion(f32[4,128,3072]{2,1,0:T(8,128)} %copy-done.80, bf16[4,128,768]{2,1,0:T(8,128)(2,1)S(1)} %fusion.89, bf16[3072,768]{1,0:T(8,128)(2,1)} %param.26), kind=kOutput, calls=%fused_computation.29 | convolution fusion | flops 2447376384 | bytes 14942208 | tf_op jit(solution)/shard_map/irn,kn->irk/dot_general | solution.py:36
  204.1 3.0 multiply_reduce_fusion.4
  212.3 7.2 %convolution_convert_fusion.2 = bf16[4,12,64,512]{3,2,1,0:T(8,128)(2,1)} fusion(bf16[4,128,12,64]{1,3,2,0:T(8,128)(2,1)S(1)} %bitcast.214, f32[4,12,128,512]{3,2,1,0:T(8,128)} %get-tuple-element.48, f32[4,12,128]{2,1,0:T(8,128)S(1)} %copy-done.46), kind=kOutput, calls=%fused_computation.60 | convolution fusion | flops 413663232 | bytes 16539648 | tf_op jit(solution)/shard_map/ihqk,iqhe->ikhe/dot_general | solution.py:475
  219.5 3.2 copy.205
  224.7 7.7 %multiply_convert_fusion = bf16[4,12,128,512]{3,2,1,0:T(8,128)(2,1)S(1)} fusion(f32[4,12,128,512]{3,2,1,0:T(8,128)} %get-tuple-element.48, f32[4,12,128]{2,1,0:T(8,128)S(1)} %fusion.44, f32[4,12,128]{2,1,0:T(8,128)S(1)} %copy-done.46, bf16[4,128,12,64]{1,3,2,0:T(8,128)(2,1)S(1)} %bitcast.216, bf16[4,512,12,64]{1,3,2,0:T(8,128)(2,1)S(1)} %bitcast.201), kind=kOutput, calls=%fused_computation.1 | convolution fusion | flops 418381824 | bytes 22855680 | tf_op jit(solution)/shard_map/iqhe,ikhe->ihqk/dot_general | solution.py:459
  232.4 3.0 multiply_reduce_fusion.5
  236.5 2.8 copy.158
  239.3 4.8 copy.159
  244.1 10.5 %fusion.30 = f32[768,1536,1]{1,0,2:T(8,128)} fusion(bf16[4,512,768]{2,1,0:T(8,128)(2,1)} %copy.159, bf16[4,512,768]{2,1,0:T(8,128)(2,1)} %copy.158, bf16[4,512,768]{2,1,0:T(8,128)(2,1)S(1)} %copy-done.5, f32[768]{0:T(1024)S(1)} %copy-done.70, f32[4,512]{1,0:T(4,128)S(1)} %copy-done.56, f32[4,512]{1,0:T(4,128)S(1)} %broadcast_multiply_fusion.2), kind=kOutput, calls=%fused_computation.46 | convolution fusion | flops 4852285440 | bytes 14175232 | tf_op jit(solution)/shard_map/irk,irn->kn/dot_general | solution.py:40
  254.7 8.6 %fusion.13 = (f32[768]{0:T(1024)S(1)}, f32[4,512]{1,0:T(4,128)}, f32[4,512]{1,0:T(4,128)}, f32[4,512,768]{2,1,0:T(8,128)}) fusion(bf16[4,512,768]{2,1,0:T(8,128)(2,1)S(1)} %copy-done.5, f32[4,512]{1,0:T(4,128)S(1)} %copy-done.56, f32[4,512]{1,0:T(4,128)S(1)} %broadcast_multiply_fusion.2, f32[768]{0:T(1024)S(1)} %copy-done.70, ...), kind=kOutput, calls=%fused_computation.21 | convolution fusion | flops 4858571776 | bytes 18126848 | tf_op jit(solution)/shard_map/irn,kn->irk/dot_general | solution.py:36
  263.3 4.1 fusion.66
  269.0 4.4 convolution_bitcast_fusion
  273.4 6.2 %reshape.307 = f32[16,48,3,384]{3,2,1,0:T(4,128)} reshape(f32[768,1152]{1,0:T(8,128)} %convolution_bitcast_fusion) | data formatting | bytes 7077888 | tf_op jit(solution)/shard_map/reshape | solution.py:58
  279.7 4.6 copy.165
  284.3 5.1 convolution_bitcast_fusion.1
  289.4 6.2 %reshape.306 = f32[16,48,4,384]{3,2,1,0:T(4,128)} reshape(f32[768,1536]{1,0:T(8,128)} %convolution_bitcast_fusion.1) | data formatting | bytes 9437184 | tf_op jit(solution)/shard_map/reshape | solution.py:58
  295.6 5.0 copy.162
  306.5 4.9 copy.217
  311.4 6.7 %reshape.309 = f32[2,16,48,2,384]{4,3,2,1,0:T(2,128)} reshape(f32[2,768,768]{2,1,0:T(8,128)} %bitcast.205) | data formatting | bytes 9437184 | tf_op jit(solution)/shard_map/reshape | solution.py:58
  318.1 4.9 copy.168
  325.9 5.1 constant_dynamic-update-slice_fusion.2
  331.0 2.8 constant_dynamic-update-slice_fusion.1
  338.3 2.9 pad_maximum_fusion.1.kv_ref
  341.2 193.6 %reduce_all.1 = (f32[2,8,624,384]{3,2,1,0:T(8,128)}, f32[2,8,120,384]{3,2,1,0:T(8,128)}) custom-call(f32[2,8,624,384]{3,2,1,0:T(8,128)} %bitcast_dynamic-update-slice_fusion.mid_ref, f32[2,2,8,120,384]{4,3,2,1,0:T(8,128)} %pad_maximum_fusion.1.kv_ref), custom_call_target="tpu_custom_call" | custom-call | tf_op jit(solution)/shard_map/reduce_all/pallas_call | solution.py:324
  539.4 3.2 fusion.91
  544.8 6.8 %fusion.92 = (f32[16,192,384]{2,1,0:T(8,128)}, f32[16,192,384]{2,1,0:T(8,128)S(1)}) fusion(f32[16,624,384]{2,1,0:T(8,128)} %bitcast.219), kind=kLoop, calls=%fused_computation.174 | loop fusion | bytes 18874368 | tf_op jit(solution)/shard_map/slice | solution.py:73
  559.5 2.5 copy.211
  567.2 3.4 fusion.12
  (275 shorter events, 84.1 us)
Async XLA Ops:
  7.2 145.0 %copy-start = (bf16[768,2304]{1,0:T(8,128)(2,1)S(1)}, bf16[768,2304]{1,0:T(8,128)(2,1)}, u32[]{:S(2)}) copy-start(bf16[768,2304]{1,0:T(8,128)(2,1)} %param.27) | copy-start | bytes 10616836
  7.2 131.5 %all-reduce.3.cloned.1.call-start = ((), (), s32[]{:S(2)}) async-start(), calls=%async_computation | async-start | bytes 3145728 | tf_op jit(solution)/shard_map/psum | solution.py:379
  7.2 5.1 copy-start.4
  8.5 4.9 copy-start.62
  13.4 10.5 %copy-start.55 = (f32[4,512]{1,0:T(4,128)}, f32[4,512]{1,0:T(4,128)S(1)}, u32[]{:S(2)}) copy-start(f32[4,512]{1,0:T(4,128)S(1)} %add_rsqrt_fusion) | copy-start | bytes 24580
  73.0 9.4 %copy-start.45 = (f32[4,12,128]{2,1,0:T(8,128)}, f32[4,12,128]{2,1,0:T(8,128)S(1)}, u32[]{:S(2)}) copy-start(f32[4,12,128]{2,1,0:T(8,128)S(1)} %log_add_fusion) | copy-start | bytes 73732
  85.5 7.2 %copy-start.79 = (s32[4]{0:T(128)S(1)}, s32[4]{0:T(128)}, u32[]{:S(2)}) copy-start(s32[4]{0:T(128)} %param.16) | copy-start | bytes 52
  93.2 48.2 %copy-start.74 = (f32[4]{0:T(128)}, f32[4]{0:T(128)S(1)}, u32[]{:S(2)}) copy-start(f32[4]{0:T(128)S(1)} %subtract_convert_fusion) | copy-start | bytes 52
  93.8 48.5 %copy-start.47 = (f32[768]{0:T(1024)S(1)}, f32[768]{0:T(1024)}, u32[]{:S(2)}) copy-start(f32[768]{0:T(1024)} %param.20) | copy-start | bytes 9220
  141.4 6.5 %copy-start.7 = (f32[4,128,768]{2,1,0:T(8,128)}, f32[4,128,768]{2,1,0:T(8,128)S(1)}, u32[]{:S(2)}) copy-start(f32[4,128,768]{2,1,0:T(8,128)S(1)} %get-tuple-element.50) | copy-start | bytes 4718596
  141.4 6.5 %slice-start.6 = ((s8[4718592]{0:T(1024)(128)(4,1)}), s8[4194304]{0:T(1024)(128)(4,1)S(1)}, s32[]{:S(2)}) async-start(s8[4718592]{0:T(1024)(128)(4,1)} %bitcast.268), calls=%async_computation.7 | async-start | bytes 8388608
  142.4 5.6 slice-start.7
  167.6 4.5 copy-start.30
  185.8 5.4 copy-start.31
  185.8 5.4 copy-start.32
  185.8 5.4 copy-start.33
  193.6 10.5 %slice-start.8 = ((s8[4718592]{0:T(1024)(128)(4,1)}), s8[4194304]{0:T(1024)(128)(4,1)S(1)}, s32[]{:S(2)}) async-start(s8[4718592]{0:T(1024)(128)(4,1)} %bitcast.270), calls=%async_computation.9 | async-start | bytes 8388608
  195.2 8.9 %copy-start.8 = (f32[4,128,768]{2,1,0:T(8,128)S(1)}, f32[4,128,768]{2,1,0:T(8,128)}, u32[]{:S(2)}) copy-start(f32[4,128,768]{2,1,0:T(8,128)} %copy-done.7) | copy-start | bytes 4718596
  195.2 8.9 %copy-start.51 = (f32[4,128]{1,0:T(4,128)S(1)}, f32[4,128]{1,0:T(4,128)}, u32[]{:S(2)}) copy-start(f32[4,128]{1,0:T(4,128)} %copy-done.50) | copy-start | bytes 6148
  195.2 8.9 %slice-start.9 = ((s8[4718592]{0:T(1024)(128)(4,1)}), s8[524288]{0:T(1024)(128)(4,1)S(1)}, s32[]{:S(2)}) async-start(s8[4718592]{0:T(1024)(128)(4,1)} %bitcast.270), calls=%async_computation.10 | async-start | bytes 1048576
  219.5 5.2 copy-start.2
  224.7 7.7 %copy-start.3 = (bf16[4,512,768]{1,2,0:T(8,128)(2,1)S(1)}, bf16[4,512,768]{1,2,0:T(8,128)(2,1)}, u32[]{:S(2)}) copy-start(bf16[4,512,768]{1,2,0:T(8,128)(2,1)} %copy.141) | copy-start | bytes 9437188
  239.3 4.8 copy-start.5
  239.3 4.8 copy-start.56
  239.3 4.8 copy-start.70
  244.1 10.6 %copy-start.35 = (bf16[4,512,768]{2,1,0:T(8,128)(2,1)S(1)}, bf16[4,512,768]{2,1,0:T(8,128)(2,1)}, u32[]{:S(2)}) copy-start(bf16[4,512,768]{2,1,0:T(8,128)(2,1)} %copy.158) | copy-start | bytes 9437188
  244.1 10.6 %copy-start.36 = (bf16[4,512,768]{2,1,0:T(8,128)(2,1)S(1)}, bf16[4,512,768]{2,1,0:T(8,128)(2,1)}, u32[]{:S(2)}) copy-start(bf16[4,512,768]{2,1,0:T(8,128)(2,1)} %copy.159) | copy-start | bytes 9437188
  244.1 10.6 %copy-start.78 = (bf16[768,1536]{1,0:T(8,128)(2,1)S(1)}, bf16[768,1536]{1,0:T(8,128)(2,1)}, u32[]{:S(2)}) copy-start(bf16[768,1536]{1,0:T(8,128)(2,1)} %param.23) | copy-start | bytes 7077892
  244.1 19.1 %slice-start.10 = ((s8[6291456]{0:T(1024)(128)(4,1)}), s8[4194304]{0:T(1024)(128)(4,1)S(1)}, s32[]{:S(2)}) async-start(s8[6291456]{0:T(1024)(128)(4,1)} %bitcast.272), calls=%async_computation.11 | async-start | bytes 8388608
  254.7 8.6 %copy-start.44 = (bf16[4,128,768]{2,1,0:T(8,128)(2,1)S(1)}, bf16[4,128,768]{2,1,0:T(8,128)(2,1)}, u32[]{:S(2)}) copy-start(bf16[4,128,768]{2,1,0:T(8,128)(2,1)} %copy-done.43) | copy-start | bytes 2359300
  254.7 8.6 %slice-start.11 = ((s8[6291456]{0:T(1024)(128)(4,1)}), s8[2097152]{0:T(1024)(128)(4,1)S(1)}, s32[]{:S(2)}) async-start(s8[6291456]{0:T(1024)(128)(4,1)} %bitcast.272), calls=%async_computation.12 | async-start | bytes 4194304
  263.3 5.7 copy-start.72
  263.3 5.7 copy-start.12
  279.7 4.6 copy-start.9
  295.6 7.0 %copy-start.18 = (bf16[128,768]{1,0:T(8,128)(2,1)S(1)}, bf16[128,768]{1,0:T(8,128)(2,1)}, u32[]{:S(2)}) copy-start(bf16[128,768]{1,0:T(8,128)(2,1)} %param.17) | copy-start | bytes 589828
  295.6 7.0 %copy-start.27 = (bf16[768,768]{1,0:T(8,128)(2,1)S(1)}, bf16[768,768]{1,0:T(8,128)(2,1)}, u32[]{:S(2)}) copy-start(bf16[768,768]{1,0:T(8,128)(2,1)} %param.22) | copy-start | bytes 3538948
  295.6 7.0 %copy-start.28 = (f32[12,64,128]{2,1,0:T(8,128)S(1)}, f32[12,64,128]{2,1,0:T(8,128)}, u32[]{:S(2)}) copy-start(f32[12,64,128]{2,1,0:T(8,128)} %multiply_reduce_fusion.5) | copy-start | bytes 1179652
  295.6 7.0 %copy-start.49 = (f32[768]{0:T(1024)S(1)}, f32[768]{0:T(1024)}, u32[]{:S(2)}) copy-start(f32[768]{0:T(1024)} %param.19) | copy-start | bytes 9220
  295.6 7.0 %copy-start.63 = (f32[128]{0:T(128)S(1)}, f32[128]{0:T(128)}, u32[]{:S(2)}) copy-start(f32[128]{0:T(128)} %copy-done.62) | copy-start | bytes 1540
  295.6 7.0 %copy-start.66 = (f32[128]{0:T(128)S(1)}, f32[128]{0:T(128)}, u32[]{:S(2)}) copy-start(f32[128]{0:T(128)} %copy-done.65) | copy-start | bytes 1540
  318.1 5.0 copy-start.16
  325.9 5.1 slice-start.4
  325.9 5.1 slice-start.5
  333.8 4.5 slice-start
  544.8 6.9 %copy-start.20 = (bf16[4,128,12,64]{1,3,2,0:T(8,128)(2,1)S(1)}, bf16[4,128,12,64]{1,3,2,0:T(8,128)(2,1)}, u32[]{:S(2)}) copy-start(bf16[4,128,12,64]{1,3,2,0:T(8,128)(2,1)} %get-tuple-element.55) | copy-start | bytes 2359300
  544.8 6.8 %copy-start.40 = (bf16[768,768]{1,0:T(8,128)(2,1)S(1)}, bf16[768,768]{1,0:T(8,128)(2,1)}, u32[]{:S(2)}) copy-start(bf16[768,768]{1,0:T(8,128)(2,1)} %param.28) | copy-start | bytes 3538948
  559.5 7.3 %slice-start.2 = ((s8[6291456]{0:T(1024)(128)(4,1)}), s8[2097152]{0:T(1024)(128)(4,1)S(1)}, s32[]{:S(2)}) async-start(s8[6291456]{0:T(1024)(128)(4,1)} %bitcast.231), calls=%async_computation.3 | async-start | bytes 4194304
  562.1 4.8 slice-start.3
  (46 other events, 116.7 us)
Sparse Core Ops, SparseCore 0:
  85.6 53.0 all-reduce.2

commit v2 on v0

v2 whole, which is shorter than its diff:
```python
import functools

import jax
import jax.numpy as jnp
from jax import lax
from jax.experimental import pallas as pl
from jax.experimental.pallas import tpu as pltpu
from jax.sharding import PartitionSpec as P

MESH = pl.DeviceIdType.MESH
HEADS = 12
EPSILON = 1e-05
LANES = 128
BLOCK = 256
STREAMS = 2


def nn(left, right):
    return lax.dot_general(left, right, (((1,), (0,)), ((), ())), preferred_element_type=jnp.float32)


def nt(left, right):
    return lax.dot_general(left, right, (((1,), (1,)), ((), ())), preferred_element_type=jnp.float32)


def norm_down(columns):
    centered = columns - jnp.mean(columns, axis=0, keepdims=True)
    inverse = lax.rsqrt(jnp.mean(centered * centered, axis=0, keepdims=True) + EPSILON)
    return centered * inverse, inverse


def cross_forward_kernel(
    frames,
    tokens_ref, w_ref, gain_ref, latent_ref, qgain_ref, wq_ref,
    kv_out, heard_out, log_out, query_out,
    tokens, w_t, tok_in, kv, queries, sent, got,
    load_sem, kv_sem, y_send, y_recv,
):
    items, rows, width = tokens_ref.shape
    latents = latent_ref.shape[0]
    head = width // HEADS
    item = lax.axis_index("items")
    frame = lax.axis_index("frames")
    stat = sent.shape[1] - width

    barrier = pltpu.get_barrier_semaphore()
    for hop in range(1, frames):
        pl.semaphore_signal(barrier, inc=1, device_id=(item, lax.rem(frame + hop, frames)), device_id_type=MESH)

    def load(i):
        return pltpu.make_async_copy(tokens_ref.at[i], tokens.at[i], load_sem.at[i])

    def save(i):
        return pltpu.make_async_copy(kv.at[i], kv_out.at[i], kv_sem.at[i])

    def across(i, hop):
        return pltpu.make_async_remote_copy(
            src_ref=sent.at[i], dst_ref=got.at[hop - 1, i], send_sem=y_send.at[hop - 1, i], recv_sem=y_recv.at[hop - 1, i],
            device_id=(item, lax.rem(frame + hop, frames)), device_id_type=MESH,
        )

    for i in range(items):
        load(i).start()
    for block in range(2 * width // 256):
        w_t[pl.ds(block * 256, 256), :] = w_ref[:, pl.ds(block * 256, 256)].T
    rows_in = latent_ref[...].astype(jnp.float32)
    centered = rows_in - jnp.mean(rows_in, axis=-1, keepdims=True)
    inverse = lax.rsqrt(jnp.mean(centered * centered, axis=-1, keepdims=True) + EPSILON)
    query_in = (centered * inverse * qgain_ref[...]).astype(jnp.bfloat16)
    query = nn(query_in, wq_ref[...]).astype(jnp.bfloat16)
    query_out[...] = query
    scaled = query * jnp.bfloat16(head ** -0.5)
    for h in range(HEADS):
        queries[h] = scaled[:, h * head : (h + 1) * head]
    pl.semaphore_wait(barrier, frames - 1)

    def one_item(i, carry):
        load(i).wait()

        def norm_block(b, inner):
            window = pl.ds(pl.multiple_of(b * LANES, LANES), LANES)
            columns = tokens[i, window, :].T.astype(jnp.float32)
            normed, _ = norm_down(columns)
            tok_in[:, window] = (normed * gain_ref[...]).astype(jnp.bfloat16)
            return inner

        lax.fori_loop(0, rows // LANES, norm_block, 0)
        for block in range(2 * width // 256):
            window = pl.ds(block * 256, 256)
            kv[i, window, :] = nn(w_t[window, :], tok_in[...]).astype(jnp.bfloat16)
        save(i).start()
        lane = lax.broadcasted_iota(jnp.int32, (latents, LANES), 1)
        stats = jnp.zeros((latents, LANES), jnp.float32)
        for h in range(HEADS):
            scores = nn(queries[h], kv[i, pl.ds(h * head, head), :])
            most = jnp.max(scores, axis=-1, keepdims=True)
            shifted = jnp.exp(scores - most)
            total = jnp.sum(shifted, axis=-1, keepdims=True)
            stats = jnp.where(lane == h, most, stats)
            stats = jnp.where(lane == h + stat // 2, total, stats)
            sent[i, pl.ds(h * head, head), :] = nt(kv[i, pl.ds(width + h * head, head), :], shifted.astype(jnp.bfloat16))
        sent[i, pl.ds(width, stat), :] = stats.T[:stat]
        for hop in range(1, frames):
            across(i, hop).start()
        return carry

    lax.fori_loop(0, items, one_item, 0)

    def combine(i, carry):
        for hop in range(1, frames):
            across(i, hop).wait_recv()
        parts = [sent.at[i]] + [got.at[hop, i] for hop in range(frames - 1)]
        highs = [part[pl.ds(width, stat // 2), :] for part in parts]
        sums = [part[pl.ds(width + stat // 2, stat // 2), :] for part in parts]
        most = functools.reduce(jnp.maximum, highs)
        total = functools.reduce(jnp.add, [low * jnp.exp(high - most) for high, low in zip(highs, sums)])
        log_total = most + jnp.log(total)
        scales = [jnp.exp(high - log_total) for high in highs]
        for h in range(HEADS):
            window = pl.ds(h * head, head)
            heard_out[i, window, :] = functools.reduce(
                jnp.add, [part[window, :] * scale[h : h + 1] for part, scale in zip(parts, scales)]
            )
        padded = jnp.concatenate([log_total, jnp.zeros((latents - stat // 2, latents), jnp.float32)], axis=0)
        log_out[i] = padded.T
        return carry

    lax.fori_loop(0, items, combine, 0)
    for i in range(items):
        save(i).wait()
        for hop in range(1, frames):
            across(i, hop).wait_send()


def cross_forward(frames, tokens, w_keyval, tok_gain, latent_init, query_gain, w_query):
    items, rows, width = tokens.shape
    latents = latent_init.shape[0]
    dma = pltpu.SemaphoreType.DMA
    vmem = pl.BlockSpec(memory_space=pltpu.VMEM)
    anywhere = pl.BlockSpec(memory_space=pl.ANY)
    peers = max(frames - 1, 1)
    return pl.pallas_call(
        functools.partial(cross_forward_kernel, frames),
        out_shape=(
            jax.ShapeDtypeStruct((items, 2 * width, rows), jnp.bfloat16),
            jax.ShapeDtypeStruct((items, width, latents), jnp.float32),
            jax.ShapeDtypeStruct((items, latents, LANES), jnp.float32),
            jax.ShapeDtypeStruct((latents, width), jnp.bfloat16),
        ),
        in_specs=[anywhere] + [vmem] * 5,
        out_specs=(anywhere, vmem, vmem, vmem),
        scratch_shapes=[
            pltpu.VMEM((items, rows, width), jnp.bfloat16),
            pltpu.VMEM((2 * width, width), jnp.bfloat16),
            pltpu.VMEM((width, rows), jnp.bfloat16),
            pltpu.VMEM((items, 2 * width, rows), jnp.bfloat16),
            pltpu.VMEM((HEADS, latents, width // HEADS), jnp.bfloat16),
            pltpu.VMEM((items, width + 32, latents), jnp.float32),
            pltpu.VMEM((peers, items, width + 32, latents), jnp.float32),
            dma((items,)), dma((items,)), dma((peers, items)), dma((peers, items)),
        ],
        compiler_params=pltpu.CompilerParams(collective_id=1, has_side_effects=True, vmem_limit_bytes=48 * 2**20),
        name="cross_forward",
    )(tokens, w_keyval, tok_gain[:, None], latent_init, query_gain[None, :], w_query)


def gelu_parts(value):
    slope = (2 / jnp.pi) ** 0.5
    square = value * value
    tanh = jnp.tanh(slope * value * (1.0 + 0.044715 * square))
    half = 0.5 + 0.5 * tanh
    bend = (0.5 * slope) * (1.0 + (3 * 0.044715) * square)
    return value * half, half + value * (1.0 - tanh * tanh) * bend


def norm_down_back(incoming, normed, inverse, gain):
    scaled = incoming * gain
    average = jnp.mean(scaled, axis=0, keepdims=True)
    along = jnp.mean(scaled * normed, axis=0, keepdims=True)
    return inverse * (scaled - average - normed * along)


def middle_kernel(
    frames,
    heard_ref, skip_ref, latent_ref, grad_ref, mgain_ref, sgain_ref,
    w_out_ref, w_up_ref, w_down_ref, w_qkv_ref, w_self_ref,
    mid_out, latents_out, d_heard_out, delta_out, d_latent_out, gain_out,
    w_out, w_up, w_down, w_qkv, w_self,
    heard, cross, mlp_in, act, slope, after, self_in, triple, mixed, cotangent, d_mixed, d_triple, d_hidden, branch,
    rows_f32, stage,
    w_sem, stage_sem,
):
    items, width, latents = heard_ref.shape
    hidden = w_up_ref.shape[1]
    head = width // HEADS
    factor = head ** -0.5
    own = width // frames
    frame = lax.axis_index("frames")
    pieces = mid_out.shape[0]
    loads = [
        pltpu.make_async_copy(source, target, w_sem.at[index])
        for index, (source, target) in enumerate(
            ((w_self_ref, w_self), (w_out_ref, w_out), (w_up_ref, w_up), (w_down_ref, w_down), (w_qkv_ref, w_qkv))
        )
    ]
    for copy in loads:
        copy.start()

    def item_window(i):
        return pl.ds(pl.multiple_of(i * latents, latents), latents)

    def each_item(body):
        def step(i, carry):
            body(i, item_window(i))
            return carry

        lax.fori_loop(0, items, step, 0)

    def each_block(count, body):
        def step(b, carry):
            body(pl.ds(pl.multiple_of(b * BLOCK, BLOCK), BLOCK))
            return carry

        lax.fori_loop(0, count // BLOCK, step, 0)

    def down(weight, source, window):
        return nn(weight[:, window].T, source[...])

    sent = [0]

    pending = {}

    def put(first_piece, count, offset, left, right):
        size = width // count
        slot = sent[0] % stage.shape[0]
        sent[0] += 1
        if slot in pending:
            pending[slot].wait()
        view = stage.at[slot]
        for block in range(width // BLOCK):
            window = pl.ds(block * BLOCK, BLOCK)
            view[window, :] = nt(left[window, :], right[...])
        copies = pltpu.make_async_copy(
            view.reshape(count, size, own), mid_out.at[pl.ds(first_piece, count), pl.ds(offset, size)], stage_sem.at[slot]
        )
        copies.start()
        pending[slot] = copies

    def load_heard(i, window):
        heard[:, window] = heard_ref[i].astype(jnp.bfloat16)
        cotangent[:, window] = grad_ref[i].T

    each_item(load_heard)
    loads[0].wait()

    def back_mixed(window):
        d_mixed[window, :] = nn(w_self[window, :], cotangent[...]).astype(jnp.bfloat16)

    each_block(width, back_mixed)
    loads[1].wait()

    def out_block(window):
        cross[window, :] = down(w_out, heard, window)

    each_block(width, out_block)

    def cross_item(i, window):
        keep = (1 - skip_ref[i]).astype(jnp.float32)
        total = latent_ref[...].astype(jnp.float32).T + keep * cross[:, window]
        cross[:, window] = total
        normed, _ = norm_down(total)
        mlp_in[:, window] = (normed * mgain_ref[...]).astype(jnp.bfloat16)

    each_item(cross_item)
    loads[2].wait()

    def up_block(window):
        value, bend = gelu_parts(down(w_up, mlp_in, window))
        act[window, :] = value.astype(jnp.bfloat16)
        slope[window, :] = bend

    each_block(hidden, up_block)
    loads[3].wait()

    def down_block(window):
        after[window, :] = cross[window, :] + down(w_down, act, window)

    each_block(width, down_block)

    def after_item(i, window):
        normed, _ = norm_down(after[:, window])
        self_in[:, window] = (normed * sgain_ref[...]).astype(jnp.bfloat16)

    each_item(after_item)
    loads[4].wait()

    def triple_block(window):
        triple[window, :] = down(w_qkv, self_in, window).astype(jnp.bfloat16)

    each_block(3 * width, triple_block)

    def attend_item(i, window):
        for h in range(HEADS):
            part = [pl.ds(third * width + h * head, head) for third in range(3)]
            query, key, value = [triple[rows, window] for rows in part]
            d_mix = d_mixed[part[0], window]
            scores = nn(query.T, key) * factor
            shifted = jnp.exp(scores - jnp.max(scores, axis=-1, keepdims=True))
            probs = shifted / jnp.sum(shifted, axis=-1, keepdims=True)
            low = probs.astype(jnp.bfloat16)
            mixed[part[0], window] = nt(value, low).astype(jnp.bfloat16)
            d_probs = nn(d_mix.T, value)
            delta = jnp.sum(low.astype(jnp.float32) * d_probs, axis=-1, keepdims=True)
            d_scores = (probs * (d_probs - delta)).astype(jnp.bfloat16)
            d_triple[part[0], window] = (nt(key, d_scores) * factor).astype(jnp.bfloat16)
            d_triple[part[1], window] = (nn(query, d_scores) * factor).astype(jnp.bfloat16)
            d_triple[part[2], window] = nn(d_mix, low).astype(jnp.bfloat16)

    each_item(attend_item)
    up_rows, down_rows = width // pieces, hidden // pieces
    first_up = up_rows
    first_down = first_up + up_rows * (hidden // width)
    first_qkv = first_down + down_rows
    first_self = first_qkv + 3 * up_rows
    my_columns = pl.multiple_of(frame * own, own)
    put(0, pieces, first_self, mixed, cotangent.at[pl.ds(my_columns, own), :])
    for third in range(3):
        put(0, pieces, first_qkv + third * up_rows, self_in, d_triple.at[pl.ds(3 * my_columns + third * own, own), :])

    def self_block(window):
        rows_f32[window, :] = nn(w_qkv[window, :], d_triple[...])

    each_block(width, self_block)
    gain_out[...] = jnp.zeros_like(gain_out)
    lane = lax.broadcasted_iota(jnp.int32, (width, LANES), 1)

    def self_back(i, window):
        normed, inverse = norm_down(after[:, window])
        incoming = rows_f32[:, window]
        gain_out[...] += jnp.where(lane == 1, jnp.sum(incoming * normed, axis=-1, keepdims=True), 0.0)
        d_after = cotangent[:, window].astype(jnp.float32) + norm_down_back(incoming, normed, inverse, sgain_ref[...])
        branch[:, window] = d_after.astype(jnp.bfloat16)
        rows_f32[:, window] = d_after

    each_item(self_back)

    def latents_block(window):
        after[window, :] = after[window, :] + down(w_self, mixed, window)

    each_block(width, latents_block)
    share = latents // frames

    def latents_item(i, window):
        d_latent_out[...] = after[:, window].T
        latents_out[i] = d_latent_out[pl.ds(pl.multiple_of(frame * share, share), share), :].astype(jnp.bfloat16)

    each_item(latents_item)

    for group in range(hidden // width):
        left = act.at[pl.ds(group * width, width), :]
        count = pieces * width // hidden
        put(group * count, count, first_down, left, branch.at[pl.ds(my_columns, own), :])

    def hidden_block(window):
        d_hidden[window, :] = (nn(w_down[window, :], branch[...]) * slope[window, :]).astype(jnp.bfloat16)

    each_block(hidden, hidden_block)
    for part in range(hidden // width):
        put(0, pieces, first_up + part * up_rows, mlp_in, d_hidden.at[pl.ds(frame * (hidden // frames) + part * own, own), :])

    def mlp_block(window):
        after[window, :] = nn(w_up[window, :], d_hidden[...])

    each_block(width, mlp_block)
    d_latent_out[...] = jnp.zeros_like(d_latent_out)

    def mlp_back(i, window):
        normed, inverse = norm_down(cross[:, window])
        incoming = after[:, window]
        gain_out[...] += jnp.where(lane == 0, jnp.sum(incoming * normed, axis=-1, keepdims=True), 0.0)
        d_cross = rows_f32[:, window] + norm_down_back(incoming, normed, inverse, mgain_ref[...])
        d_latent_out[...] += d_cross.T
        keep = (1 - skip_ref[i]).astype(jnp.float32)
        branch[:, window] = (keep * d_cross).astype(jnp.bfloat16)

    each_item(mlp_back)
    put(0, pieces, 0, heard, branch.at[pl.ds(my_columns, own), :])

    def heard_block(window):
        d_heard_out[window, :] = nn(w_out[window, :], branch[...]).astype(jnp.bfloat16)

    each_block(width, heard_block)

    def delta_item(i, window):
        product = d_heard_out[:, window].astype(jnp.float32) * heard_ref[i]
        sums = jnp.sum(product.reshape(HEADS, head, latents), axis=1)
        padded = jnp.concatenate([sums, jnp.zeros((latents - HEADS, latents), jnp.float32)], axis=0)
        delta_out[i] = padded.T

    each_item(delta_item)
    for copy in pending.values():
        copy.wait()


def middle(frames, pieces, heard, skip, latent_init, grad_out, mlp_gain, self_gain, w_out, w_up, w_down, w_self_qkv, w_self_out):
    items, width, latents = heard.shape
    hidden = w_up.shape[1]
    own = width // frames
    columns = items * latents
    rows = (width + hidden + hidden + 3 * width + width) // pieces
    bf16, f32 = jnp.bfloat16, jnp.float32
    vmem = pl.BlockSpec(memory_space=pltpu.VMEM)
    anywhere = pl.BlockSpec(memory_space=pl.ANY)
    dma = pltpu.SemaphoreType.DMA
    return pl.pallas_call(
        functools.partial(middle_kernel, frames),
        out_shape=(
            jax.ShapeDtypeStruct((pieces, rows, own), f32),
            jax.ShapeDtypeStruct((items, latents // frames, width), bf16),
            jax.ShapeDtypeStruct((width, columns), bf16),
            jax.ShapeDtypeStruct((items, latents, LANES), f32),
            jax.ShapeDtypeStruct((latents, width), f32),
            jax.ShapeDtypeStruct((width, LANES), f32),
        ),
        in_specs=[vmem, pl.BlockSpec(memory_space=pltpu.SMEM)] + [vmem] * 4 + [anywhere] * 5,
        out_specs=(anywhere,) + (vmem,) * 5,
        scratch_shapes=[pltpu.VMEM(w.shape, bf16) for w in (w_out, w_up, w_down, w_self_qkv, w_self_out)]
        + [
            pltpu.VMEM((width, columns), bf16),
            pltpu.VMEM((width, columns), f32),
            pltpu.VMEM((width, columns), bf16),
            pltpu.VMEM((hidden, columns), bf16),
            pltpu.VMEM((hidden, columns), f32),
            pltpu.VMEM((width, columns), f32),
            pltpu.VMEM((width, columns), bf16),
            pltpu.VMEM((3 * width, columns), bf16),
            pltpu.VMEM((width, columns), bf16),
            pltpu.VMEM((width, columns), bf16),
            pltpu.VMEM((width, columns), bf16),
            pltpu.VMEM((3 * width, columns), bf16),
            pltpu.VMEM((hidden, columns), bf16),
            pltpu.VMEM((width, columns), bf16),
            pltpu.VMEM((width, columns), f32),
            pltpu.VMEM((3, width, own), f32),
            dma((5,)), dma((3,)),
        ],
        compiler_params=pltpu.CompilerParams(vmem_limit_bytes=58 * 2**20),
        name="middle",
    )(heard, skip, latent_init, grad_out, mlp_gain[:, None], self_gain[:, None], w_out, w_up, w_down, w_self_qkv, w_self_out)


def add_into(target, parts, rows):
    step = next(size for size in (104, 80, 64, 48, 40, 24, 16, 8) if rows % size == 0)

    def body(index, carry):
        window = pl.ds(pl.multiple_of(index * step, 8), step)
        total = parts[0][window]
        for part in parts[1:]:
            total = total + part[window]
        target[window] = total
        return carry

    lax.fori_loop(0, rows // step, body, 0)


def nn_exact(left, right):
    total = jnp.zeros((left.shape[0], right.shape[1]), jnp.float32)
    rest = right
    for _ in range(3):
        part = rest.astype(jnp.bfloat16)
        total = total + nn(left, part)
        rest = rest - part.astype(jnp.float32)
    return total


def backward_kernel(
    chips, frames, spans,
    mid_ref, tokens_ref, kv_ref, d_heard_ref, log_ref, delta_ref, query_ref,
    w_ref, gain_ref, latent_ref, qgain_ref, wq_ref, d_latent_ref, gains_ref,
    mid_out, kv_out, token_out,
    mine, sib, rx, kmine, ksib, ky, krx,
    tokens, kv, tok_in, d_kv, normed, incoming, queries, queries_t, d_query, gain_sum, token_stage,
    ld_sem, sib_send, sib_recv, rs_send, rs_recv, ag_send, ag_recv, share_send, share_recv, own_sem,
    ksib_send, ksib_recv, y_send, y_recv, krs_send, krs_recv, kag_send, kag_recv, kshare_send, kshare_recv,
    tok_sem, kv_sem, out_sem,
):
    items = lax.axis_index("items")
    frame = lax.axis_index("frames")
    core = lax.rem(items, 2)
    chip = items // 2
    column = lax.rem(chip, 2)
    line = chip // 2
    place = line + column * (chips - 1 - 2 * line)
    way = 1 - 2 * core
    count, rows, width = tokens_ref.shape
    latents = latent_ref.shape[0]
    head = width // HEADS
    factor = head ** -0.5
    own = width // frames
    kv_rows = krx.shape[1]

    def device_at(position):
        position = lax.rem(position + 2 * chips, chips)
        far = position // (chips // 2)
        return (2 * (position + far * (chips - 1 - 2 * position)) + far) * 2 + core

    right, left = device_at(place + way), device_at(place - way)
    sibling = items + way

    def chunk(offset):
        return lax.rem(place + way * offset + 2 * chips, chips)

    def sib_chunk(offset):
        return lax.rem(place - way * offset + 2 * chips, chips)

    barrier = pltpu.get_barrier_semaphore()
    for peer in (left, right, sibling):
        pl.semaphore_signal(barrier, inc=1, device_id=(peer, frame), device_id_type=MESH)
    for hop in range(1, frames):
        pl.semaphore_signal(barrier, inc=1, device_id=(items, lax.rem(frame + hop, frames)), device_id_type=MESH)

    def remote(src, dst, send, recv, peer):
        return pltpu.make_async_remote_copy(
            src_ref=src, dst_ref=dst, send_sem=send, recv_sem=recv, device_id=peer, device_id_type=MESH
        )

    def load(k):
        return pltpu.make_async_copy(mid_ref.at[core, k], mine.at[k], ld_sem.at[k])

    def pair(k):
        return remote(mid_ref.at[1 - core, k], sib.at[k], sib_send.at[k], sib_recv.at[k], (sibling, frame))

    def ring(j, k):
        part = pl.ds(*spans[j])
        return remote(mine.at[k, part], rx.at[k, part], rs_send.at[j, k], rs_recv.at[j, k], (right, frame))

    def gather(j, k, source):
        part = pl.ds(*spans[j])
        return remote(source.at[k, part], mid_out.at[core, k, part], ag_send.at[j, k], ag_recv.at[j, k], (right, frame))

    def share(j, k, source):
        part = pl.ds(*spans[j])
        return remote(source.at[k, part], mid_out.at[core, k, part], share_send.at[j, k], share_recv.at[j, k], (sibling, frame))

    def share_from(j, k):
        part = pl.ds(*spans[j])
        return remote(mine.at[k, part], mid_out.at[1 - core, k, part], share_send.at[j, k], share_recv.at[j, k], (sibling, frame))

    def keep(j, k):
        part = pl.ds(*spans[j])
        return pltpu.make_async_copy(mine.at[k, part], mid_out.at[core, k, part], own_sem.at[j])

    def kpair():
        return remote(kmine.at[:, 1 - core], ksib, ksib_send, ksib_recv, (sibling, frame))

    def across(hop, k):
        other = lax.rem(frame + hop, frames)
        return remote(kmine.at[other, core, k], ky.at[hop - 1, k], y_send.at[hop - 1, k], y_recv.at[hop - 1, k], (items, other))

    def kring(k):
        return remote(kmine.at[frame, core, k], krx.at[k], krs_send.at[k], krs_recv.at[k], (right, frame))

    def kgather(k, source):
        return remote(source, kv_out.at[core, k], kag_send.at[k], kag_recv.at[k], (right, frame))

    def kshare(k, source):
        return remote(source, kv_out.at[core, k], kshare_send.at[k], kshare_recv.at[k], (sibling, frame))

    def kshare_from(k):
        return remote(kmine.at[frame, core, k], kv_out.at[1 - core, k], kshare_send.at[k], kshare_recv.at[k], (sibling, frame))

    def kkeep(k):
        return pltpu.make_async_copy(kmine.at[frame, core, k], kv_out.at[core, k], own_sem.at[len(spans)])

    def rs_tick(step, j, first=False):
        k = chunk(-step)
        if j == 0:
            load(k).wait()
            pair(k).wait_recv()
        start, size = spans[j]
        part = pl.ds(start, size)
        parts = [mine.at[k, part], sib.at[k, part]]
        if not first:
            ring(j, k).wait_recv()
            parts.append(rx.at[k, part])
        add_into(mine.at[k, part], parts, size)

    def rs_send_on(step, j):
        ring(j, chunk(-step)).start()

    def rs_step(step, j, first=False):
        rs_tick(step, j, first)
        rs_send_on(step, j)

    def rs_last(j):
        k = chunk(1)
        rs_tick(chips - 1, j)
        gather(j, k, mine).start()
        share(j, k, mine).start()
        keep(j, k).start()

    def ag_step(step, j):
        k = chunk(1 - step)
        gather(j, k, mine).wait_recv()
        if step < chips - 1:
            gather(j, k, mid_out.at[core]).start()
        share(j, k, mid_out.at[core]).start()

    def k_step(step):
        k = chunk(-step)
        if step < chips:
            parts = [kmine.at[frame, core, k], ksib.at[frame, k]]
            for hop in range(1, frames):
                across(hop, k).wait_recv()
                parts.append(ky.at[hop - 1, k])
            if step > 0:
                kring(k).wait_recv()
                parts.append(krx.at[k])
            add_into(kmine.at[frame, core, k], parts, kv_rows)
            if step < chips - 1:
                kring(k).start()
            else:
                kgather(k, kmine.at[frame, core, k]).start()
                kshare(k, kmine.at[frame, core, k]).start()
                kkeep(k).start()
        else:
            kgather(k, kmine.at[frame, core, k]).wait_recv()
            if step < 2 * chips - 2:
                kgather(k, kv_out.at[core, k]).start()
            kshare(k, kv_out.at[core, k]).start()

    def across_step(step):
        k = chunk(-step)
        for hop in range(1, frames):
            other = lax.rem(frame + hop, frames)
            add_into(kmine.at[other, core, k], [kmine.at[other, core, k], ksib.at[other, k]], kv_rows)
            across(hop, k).start()

    def tok_load(i):
        return pltpu.make_async_copy(tokens_ref.at[i], tokens.at[lax.rem(i, 2)], tok_sem.at[lax.rem(i, 2)])

    def kv_load(i):
        return pltpu.make_async_copy(kv_ref.at[i], kv.at[lax.rem(i, 2)], kv_sem.at[lax.rem(i, 2)])

    def token_save(i, b):
        slot = lax.rem(b, 2)
        return pltpu.make_async_copy(
            token_stage.at[slot], token_out.at[i, pl.ds(pl.multiple_of(b * LANES, LANES), LANES), :], out_sem.at[slot]
        )

    def start_stage(index, carry):
        pair(sib_chunk(-index)).start()
        load(chunk(-index)).start()
        return carry

    tok_load(0).start()
    kv_load(0).start()
    query = query_ref[...]
    scaled = query * jnp.bfloat16(factor)
    for h in range(HEADS):
        queries[h] = scaled[:, h * head : (h + 1) * head]
    queries_t[...] = scaled.T
    d_query[...] = jnp.zeros_like(d_query)
    gain_sum[...] = jnp.zeros_like(gain_sum)
    pl.semaphore_wait(barrier, 3 + frames - 1)
    lax.fori_loop(0, chips, start_stage, 0)

    def attend(i, heads):
        slot = lax.rem(i, 2)
        columns = pl.ds(pl.multiple_of(i * rows, rows), rows)
        latent_window = pl.ds(pl.multiple_of(i * latents, latents), latents)
        for h in heads:
            keys_at, values_at = pl.ds(h * head, head), pl.ds(width + h * head, head)
            keys, values = kv[slot, keys_at, :], kv[slot, values_at, :]
            d_heard_t = d_heard_ref[keys_at, latent_window]
            probs = jnp.exp(nn(queries[h], keys) - log_ref[i, :, h : h + 1])
            d_probs = nn(d_heard_t.T, values)
            d_scores = (probs * (d_probs - delta_ref[i, :, h : h + 1])).astype(jnp.bfloat16)
            d_kv[keys_at, columns] = nn(queries_t[keys_at, :], d_scores).astype(jnp.bfloat16)
            d_kv[values_at, columns] = nn(d_heard_t, probs.astype(jnp.bfloat16)).astype(jnp.bfloat16)
            d_query[keys_at, :] += nt(keys, d_scores)

    def norm_tokens(i):
        tok_load(i).wait()

        def norm_block(b, carry):
            window = pl.ds(pl.multiple_of(b * LANES, LANES), LANES)
            columns = tokens[lax.rem(i, 2), window, :].T.astype(jnp.float32)
            block, inverse = norm_down(columns)
            normed[pl.ds(0, width), window] = block
            normed[pl.ds(width, 8), window] = jnp.broadcast_to(inverse, (8, LANES))
            tok_in[:, pl.ds(pl.multiple_of(i * rows + b * LANES, LANES), LANES)] = (block * gain_ref[...]).astype(jnp.bfloat16)
            return carry

        lax.fori_loop(0, rows // LANES, norm_block, 0)

    def token_back(i):
        columns = pl.ds(pl.multiple_of(i * rows, rows), rows)

        def product(b, carry):
            window = pl.ds(pl.multiple_of(b * BLOCK, BLOCK), BLOCK)
            incoming[window, :] = nn(w_ref[window, :], d_kv[:, columns])
            return carry

        lax.fori_loop(0, width // BLOCK, product, 0)

        def back_block(b, carry):
            window = pl.ds(pl.multiple_of(b * LANES, LANES), LANES)
            block = normed[pl.ds(0, width), window]
            arriving = incoming[:, window]
            gain_sum[...] += arriving * block
            result = norm_down_back(arriving, block, normed[pl.ds(width, 1), window], gain_ref[...])

            @pl.when((i > 0) | (b > 1))
            def _():
                token_save(i, b).wait()

            token_stage[lax.rem(b, 2)] = result.T.astype(jnp.bfloat16)
            token_save(i, b).start()
            return carry

        lax.fori_loop(0, rows // LANES, back_block, 0)

    for j in range(len(spans)):
        rs_step(0, j, True)

    def one_item(i, carry):
        kv_load(i).wait()

        @pl.when(i + 1 < count)
        def _():
            kv_load(i + 1).start()
            tok_load(i + 1).start()

        norm_tokens(i)
        attend(i, range(HEADS // 2))
        rs_step(i + 1, 0)
        attend(i, range(HEADS // 2, HEADS))
        token_back(i)
        for j in range(1, len(spans)):
            rs_step(i + 1, j)
        return carry

    lax.fori_loop(0, count, one_item, 0)

    per_piece = width // (2 * chips)
    small = 2 * latents // (2 * chips)
    d_query[...] = d_query[...] * factor
    q_total = d_query[...]
    q_normed, q_inverse = norm_down(latent_ref[...].astype(jnp.float32).T)
    q_incoming = nn_exact(wq_ref[...], q_total)
    lane = lax.broadcasted_iota(jnp.int32, (width, LANES), 1)
    gain_columns = gains_ref[...]
    gain_columns = jnp.where(lane == 2, jnp.sum(gain_sum[...], axis=-1, keepdims=True), gain_columns)
    gain_columns = jnp.where(lane == 3, jnp.sum(q_incoming * q_normed, axis=-1, keepdims=True), gain_columns)
    gain_rows = gain_columns.T[:8]
    latent_rows = norm_down_back(q_incoming, q_normed, q_inverse, qgain_ref[...]).T
    query_rows = q_total.T
    for f in range(frames):
        mask = (frame == f).astype(jnp.float32)
        mine_columns = slice(f * own, (f + 1) * own)
        latent_part = latent_rows[:, mine_columns] + mask * d_latent_ref[:, mine_columns]
        both = jnp.concatenate([query_rows[:, mine_columns], latent_part], axis=0)
        kmine[f, :, :, pl.ds(2 * per_piece, small), :] = both.reshape(2, chips, small, own)
        row = lax.broadcasted_iota(jnp.int32, (8, own), 0)
        gain_block = gain_rows[:, mine_columns] * jnp.where(row < 2, mask, 1.0)
        kmine[f, :, :, pl.ds(2 * per_piece + small, 8), :] = jnp.zeros((2, chips, 8, own), jnp.float32)
        kmine[f, 0, 0, pl.ds(2 * per_piece + small, 8), :] = gain_block

    def keyval_block(f, b):
        source = d_kv.at[pl.ds((2 * f + b) * own, own), :]
        size = width // 2
        for start in range(0, width, size):
            block = nt(tok_in[pl.ds(start, size), :], source[...])
            for piece in range(size // per_piece):
                at = start // per_piece + piece
                kmine[f, at // chips, at % chips, pl.ds(b * per_piece, per_piece), :] = block[piece * per_piece : (piece + 1) * per_piece]

    done = count + 1
    blocks = [(f, b) for f in range(frames) for b in range(2)]
    for index, (f, b) in enumerate(blocks):
        keyval_block(f, b)
        if index % 2 == 1 and index + 1 < len(blocks) and done < chips - 1:
            rs_step(done, 0)
            for j in range(1, len(spans)):
                rs_step(done, j)
            done += 1
    kpair().start()
    for step in range(done, chips - 1):
        rs_step(step, 0)
        if step == done:
            kpair().wait_recv()
            for order in range(chips):
                across_step(order)
        for j in range(1, len(spans)):
            rs_step(step, j)
    for j in range(len(spans)):
        rs_last(j)
    kdone = 0
    for step in range(1, chips):
        for j in range(len(spans)):
            ag_step(step, j)
            if kdone < 2 * chips - 1:
                k_step(kdone)
                kdone += 1
    for step in range(kdone, 2 * chips - 1):
        k_step(step)

    def drain(k, carry):
        pair(k).wait_send()
        for j in range(len(spans)):
            share(j, k, mine).wait_send()
            share_from(j, k).wait_recv()
        kshare(k, kmine.at[frame, core, k]).wait_send()
        kshare_from(k).wait_recv()
        for hop in range(1, frames):
            across(hop, k).wait_send()
        return carry

    lax.fori_loop(0, chips, drain, 0)

    def drain_ring(step, carry):
        for j in range(len(spans)):
            ring(j, chunk(-step)).wait_send()
            gather(j, chunk(1 - step), mine).wait_send()
        kring(chunk(-step)).wait_send()
        kgather(chunk(1 - step), kmine.at[frame, core, 0]).wait_send()
        return carry

    lax.fori_loop(0, chips - 1, drain_ring, 0)
    kpair().wait_send()
    for j in range(len(spans)):
        keep(j, chunk(1)).wait()
    kkeep(chunk(1)).wait()
    for b in range(2):
        token_save(0, b).wait()


def backward(frames, mid, tokens, kv, d_heard, log_total, delta, query, w_keyval, tok_gain, latent_init, query_gain, w_query, d_latent, gains):
    chips, mid_rows, own = mid.shape[1:]
    items, rows, width = tokens.shape
    latents = latent_init.shape[0]
    kv_rows = 2 * width // (2 * chips) + 2 * latents // (2 * chips) + 8
    step = mid_rows // 8 // STREAMS * 8
    spans = tuple((j * step, step if j + 1 < STREAMS else mid_rows - j * step) for j in range(STREAMS))
    dma = pltpu.SemaphoreType.DMA
    peers = max(frames - 1, 1)
    n = len(spans)
    f32, bf16 = jnp.float32, jnp.bfloat16
    vmem = pl.BlockSpec(memory_space=pltpu.VMEM)
    anywhere = pl.BlockSpec(memory_space=pl.ANY)
    scratch = [
        pltpu.VMEM((chips, mid_rows, own), f32), pltpu.VMEM((chips, mid_rows, own), f32), pltpu.VMEM((chips, mid_rows, own), f32),
        pltpu.VMEM((frames, 2, chips, kv_rows, own), f32), pltpu.VMEM((frames, chips, kv_rows, own), f32),
        pltpu.VMEM((peers, chips, kv_rows, own), f32), pltpu.VMEM((chips, kv_rows, own), f32),
        pltpu.VMEM((2, rows, width), bf16),
        pltpu.VMEM((2, 2 * width, rows), bf16),
        pltpu.VMEM((width, items * rows), bf16),
        pltpu.VMEM((2 * width, items * rows), bf16),
        pltpu.VMEM((width + 8, rows), f32),
        pltpu.VMEM((width, rows), f32),
        pltpu.VMEM((HEADS, latents, width // HEADS), bf16),
        pltpu.VMEM((width, latents), bf16),
        pltpu.VMEM((width, latents), f32),
        pltpu.VMEM((width, LANES), f32),
        pltpu.VMEM((2, LANES, width), bf16),
        dma((chips,)), dma((chips,)), dma((chips,)),
        dma((n, chips)), dma((n, chips)), dma((n, chips)), dma((n, chips)), dma((n, chips)), dma((n, chips)), dma((n + 1,)),
        dma, dma,
        dma((peers, chips)), dma((peers, chips)),
        dma((chips,)), dma((chips,)), dma((chips,)), dma((chips,)), dma((chips,)), dma((chips,)),
        dma((2,)), dma((2,)), dma((2,)),
    ]
    return pl.pallas_call(
        functools.partial(backward_kernel, chips, frames, spans),
        out_shape=(
            jax.ShapeDtypeStruct(mid.shape, f32),
            jax.ShapeDtypeStruct((2, chips, kv_rows, own), f32),
            jax.ShapeDtypeStruct(tokens.shape, bf16),
        ),
        in_specs=[anywhere] * 3 + [vmem] * 11,
        out_specs=(anywhere,) * 3,
        scratch_shapes=scratch,
        compiler_params=pltpu.CompilerParams(collective_id=0, has_side_effects=True, vmem_limit_bytes=62 * 2**20),
        name="backward",
    )(
        mid, tokens, kv, d_heard, log_total, delta, query, w_keyval, tok_gain[:, None], latent_init,
        query_gain[:, None], w_query, d_latent, gains,
    )


def unpack_kernel(mid_ref, kv_ref, latent_ref, qgain_ref, *rest):
    outs, (query_out, total, sem) = rest[:-3], rest[-3:]
    pieces, _, own = mid_ref.shape
    copies = []

    def place(source, offset, out):
        rows, columns = out.shape
        size = rows // pieces
        view = out.reshape(pieces, size, columns)
        for b in range(columns // own):
            copies.append(
                pltpu.make_async_copy(
                    source.at[:, pl.ds(offset + b * size, size), :], view.at[:, :, pl.ds(b * own, own)], sem.at[len(copies)]
                )
            )
        return offset + size * columns // own

    offset = 0
    for out in outs[:5]:
        offset = place(mid_ref, offset, out)
    offset = place(kv_ref, 0, outs[5])
    latents = outs[6].shape[0]
    small = 2 * latents // pieces
    half = pieces // 2
    copies.append(
        pltpu.make_async_copy(
            kv_ref.at[pl.ds(half, half), pl.ds(offset, small), :], outs[6].reshape(half, small, own), sem.at[len(copies)]
        )
    )
    query = pltpu.make_async_copy(kv_ref.at[pl.ds(0, half), pl.ds(offset, small), :], total, sem.at[len(copies)])
    query.start()
    for copy in copies:
        copy.start()
    normed, _ = norm_down(latent_ref[...].astype(jnp.float32).T)
    query_in = (normed * qgain_ref[...]).astype(jnp.bfloat16)
    query.wait()
    query_out[...] = nn_exact(query_in, total[...].reshape(latents, own))
    for copy in copies:
        copy.wait()


def unpack_all(mid, kv, latent_init, query_gain, shapes):
    f32 = jnp.float32
    own = mid.shape[-1]
    latents, width = latent_init.shape
    pieces = mid.shape[0]
    vmem = pl.BlockSpec(memory_space=pltpu.VMEM)
    anywhere = pl.BlockSpec(memory_space=pl.ANY)
    count = sum(columns // own for _, columns in shapes) + 2
    return pl.pallas_call(
        unpack_kernel,
        out_shape=tuple(jax.ShapeDtypeStruct(shape, f32) for shape in shapes) + (
            jax.ShapeDtypeStruct((latents, own), f32), jax.ShapeDtypeStruct((width, own), f32)),
        in_specs=[anywhere] * 2 + [vmem] * 2,
        out_specs=(anywhere,) * (len(shapes) + 1) + (vmem,),
        scratch_shapes=[pltpu.VMEM((pieces // 2, 2 * latents // pieces, own), f32), pltpu.SemaphoreType.DMA((count,))],
        compiler_params=pltpu.CompilerParams(vmem_limit_bytes=16 * 2**20),
        name="unpack_all",
    )(mid, kv, latent_init, query_gain[:, None])


def unpack(packed, rows, columns):
    pieces, _, width = packed.shape
    split = packed.reshape(pieces, columns // width, rows // pieces, width)
    return jnp.swapaxes(split, 1, 2).reshape(rows, columns)


def cut(packed, shapes):
    start, out = 0, []
    for rows, columns in shapes:
        count = rows * columns // packed.shape[-1] // packed.shape[0]
        out.append(unpack(packed[:, start : start + count], rows, columns))
        start += count
    return out


def shards(
    tokens,
    skip,
    latent_init,
    tok_gain,
    query_gain,
    mlp_gain,
    self_gain,
    w_query,
    w_keyval,
    w_out,
    w_up,
    w_down,
    w_self_qkv,
    w_self_out,
    grad_out,
):
    frames, pieces = lax.axis_size("frames"), lax.axis_size("items")
    latents, width = latent_init.shape
    hidden = w_up.shape[1]
    own = width // frames
    kv, heard, log_total, query = cross_forward(frames, tokens, w_keyval, tok_gain, latent_init, query_gain, w_query)
    mid, out_latents, d_heard, delta, d_latent, gains = middle(
        frames, pieces, heard, skip, latent_init, grad_out, mlp_gain, self_gain, w_out, w_up, w_down, w_self_qkv, w_self_out
    )
    mid_sum, kv_sum, token_grad = backward(
        frames, mid.reshape(2, pieces // 2, mid.shape[1], own), tokens, kv, d_heard, log_total, delta, query,
        w_keyval, tok_gain, latent_init, query_gain, w_query, d_latent, gains,
    )
    mid_sum = mid_sum.reshape(mid.shape)
    kv_sum = kv_sum.reshape((pieces,) + kv_sum.shape[2:])
    shapes = (
        (width, own),
        (width, hidden // frames),
        (hidden, own),
        (width, 3 * own),
        (width, own),
        (width, 2 * own),
    )
    if own % LANES == 0:
        *sums, latent_grad, grad_query = unpack_all(mid_sum, kv_sum, latent_init, query_gain, shapes)
    else:
        sums = cut(mid_sum, shapes[:5])
        keyval_sum, small = cut(kv_sum, (shapes[5], (2 * latents, own)))
        sums.append(keyval_sum)
        latent_grad = small[latents:]
        normed, _ = norm_down(latent_init.astype(jnp.float32).T)
        query_in = (normed * query_gain[:, None]).astype(jnp.bfloat16)
        grad_query = jnp.dot(query_in.astype(jnp.float32), small[:latents], precision=lax.Precision.HIGHEST)
    gain_rows = kv_sum[0, -8:]
    return (
        out_latents,
        token_grad,
        latent_grad,
        gain_rows[2],
        gain_rows[3],
        gain_rows[0],
        gain_rows[1],
        grad_query,
        sums[5],
        sums[0],
        sums[1],
        sums[2],
        sums[3],
        sums[4],
    )


def solution(mesh):
    in_specs = (
        P("items", "frames", None),
        P("items"),
        P(),
        P(),
        P(),
        P(),
        P(),
        P(),
        P(),
        P(),
        P(),
        P(),
        P(),
        P(),
        P("items", None, None),
    )
    out_specs = (
        P("items", "frames", None),
        P("items", "frames", None),
        P(None, "frames"),
        P("frames"),
        P("frames"),
        P("frames"),
        P("frames"),
        P(None, "frames"),
        P(None, "frames"),
        P(None, "frames"),
        P(None, "frames"),
        P(None, "frames"),
        P(None, "frames"),
        P(None, "frames"),
    )
    return jax.shard_map(shards, mesh=mesh, in_specs=in_specs, out_specs=out_specs, check_vma=False)
```

time: 722 us -> 337 us (0.47); the launches traced: 713 us -> 337 us
  waiting for transfers between devices: 383 us -> 0 us
  Pallas kernels: 0 us -> 313 us
  matrix products: 135 us -> 0 us
  local copies, waits for them, and re-layouts: 85 us -> 23.1 us
  blocking collectives: 60.5 us -> 0 us
  other arithmetic: 32.2 us -> 0 us
  between operations: 15.5 us -> 0.74 us
    psum x3 -> x0, waiting for transfers between devices: 329 us -> none  [the longest x1 283 us: shards(): lax.psum((mine_latent, mine_query_gain, mine_mlp_gain, mine_self_gain, mi...]
    pallas_call x0 -> x4, Pallas kernels: none -> 313 us  [the longest x1 191 us: backward(): pl.pallas_call(functools.partial(backward_kernel, chips, frames, spans),...]
    dot_general x32 -> x0, matrix products: 130 us -> none  [the longest x6 32.4 us: input_mul(): jnp.einsum('irn,kn->irk', grad_rows, weight, preferred_element_type=jnp.f...]
    reduce_scatter x1 -> x0, waiting for transfers between devices: 54.5 us -> none  [shards(): lax.psum_scatter(summed[10], 'frames', scatter_dimension=1, tiled=True)]
    psum x2 -> x0, blocking collectives: 44.3 us -> none  [the longest x1 36.2 us: shards(): lax.psum((mine_latent, mine_query_gain, mine_mlp_gain, mine_self_gain, mi...]
    reshape x6 -> x0, local copies, waits for them, and re-layouts: 19.5 us -> none  [join_heads(): values.reshape(values.shape[0], values.shape[1], values.shape[2] * values...]
    slice x7 -> x1, local copies, waits for them, and re-layouts: 20.7 us -> 1.47 us  [shards(): gain_rows[1]]
    reduce_sum x9 -> x0, other arithmetic: 17 us -> none  [the longest x1 7.02 us: shards(): jnp.sum(jnp.exp(scores - row_max[..., None]), axis=-1)]
  transfers between devices with their start and end apart: 4 -> 0, of which waited for: 3 -> 0; matrix products, arithmetic and copies ran while one was open for 12% -> 0% of each run, Pallas kernels for 0% -> 0%
where the time goes in v2:
time: 337 us
  Pallas kernels  313 us (93%)
  local copies, waits for them, and re-layouts  23.1 us (7%)
    pallas_call x1, Pallas kernels, backward(): pl.pallas_call(functools.partial(backward_kernel, chips, frames, spans),...  191 us
    pallas_call x1, Pallas kernels, middle(): pl.pallas_call(functools.partial(middle_kernel, frames), out_shape=(jax.S...  70 us
    pallas_call x1, Pallas kernels, cross_forward(): pl.pallas_call(functools.partial(cross_forward_kernel, frames), out_shape...  44.4 us
    unnamed x25, local copies, waits for them, and re-layouts  15.3 us
    pallas_call x1, Pallas kernels, unpack_all(): pl.pallas_call(unpack_kernel, out_shape=tuple((jax.ShapeDtypeStruct(shape...  7.8 us

profile of v2, /device:TPU:0, one launch (start us, length us, event | category | flops | bytes accessed | tf_op | source)
XLA Modules:
  0.0 336.7 jit_solution(2925078397981069649)
XLA Ops:
  0.6 0.7 broadcast_in_dim.18.qgain_ref
  1.3 0.8 broadcast_in_dim.22.gain_ref
  2.2 0.0 copy-start.3
  2.2 1.6 broadcast_in_dim.25.qgain_ref
  3.8 1.6 broadcast_in_dim.23.mgain_ref
  5.4 1.6 broadcast_in_dim.24.sgain_ref
  7.0 0.0 copy-start.1
  7.0 1.7 copy-done.1
  8.7 0.0 copy-start.2
  8.7 1.3 copy-done.2
  10.0 0.0 copy-start.5
  10.0 0.9 copy-done.5
  10.9 44.4 %cross_forward.1 = (bf16[4,1536,512]{2,1,0:T(8,128)(2,1)}, f32[4,768,128]{2,1,0:T(8,128)S(1)}, f32[4,128,128]{2,1,0:T(8,128)S(1)}, bf16[128,768]{1,0:T(8,128)(2,1)S(1)}) custom-call(bf16[4,512,768]{2,1,0:T(8,128)(2,1)} %tokens_ref.3, bf16[768,1536]{1,0:T(8,128)(2,1)S(1)} %copy-done.1, f32[768,1]{1,0:T(8,128)S(1)} %broadcast_in_dim.22.gain_ref, ...), custom_call_target="tpu_custom_call" | custom-call | tf_op jit(solution)/shard_map/cross_forward/pallas_call | solution.py:142
  55.2 0.0 copy-done.3
  55.3 0.0 copy-start.8
  55.3 1.1 copy-done.8
  56.4 0.0 copy-start.9
  56.4 0.7 copy-done.9
  57.1 0.0 copy-start.10
  57.1 0.7 copy-done.10
  57.8 70.0 %middle.1 = (f32[16,624,384]{2,1,0:T(8,128)}, bf16[4,64,768]{2,1,0:T(8,128)(2,1)}, bf16[768,512]{1,0:T(8,128)(2,1)}, f32[4,128,128]{2,1,0:T(8,128)}, f32[128,768]{1,0:T(8,128)}, /*index=5*/f32[768,128]{1,0:T(8,128)}) custom-call(f32[4,768,128]{2,1,0:T(8,128)} %copy-done.8, s32[4]{0:T(128)} %skip_ref.1, bf16[128,768]{1,0:T(8,128)(2,1)} %latent_ref.7, ...), custom_call_target="tpu_custom_call" | custom-call | tf_op jit(solution)/shard_map/middle/pallas_call | solution.py:415
  127.8 0.0 copy-start.4
  127.8 0.0 copy-start.6
  127.8 190.7 %backward.1 = (f32[2,8,624,384]{3,2,1,0:T(8,128)}, f32[2,8,120,384]{3,2,1,0:T(8,128)}, bf16[4,512,768]{2,1,0:T(8,128)(2,1)}) custom-call(f32[2,8,624,384]{3,2,1,0:T(8,128)} %bitcast.6, bf16[4,512,768]{2,1,0:T(8,128)(2,1)} %tokens_ref.3, bf16[4,1536,512]{2,1,0:T(8,128)(2,1)} %get-tuple-element.38.kv_ref, bf16[768,512]{1,0:T(8,128)(2,1)} %get-tuple-element.39.d_heard_ref, ...), custom_call_target="tpu_custom_call" | custom-call | tf_op jit(solution)/shard_map/backward/pallas_call | solution.py:874
  318.5 1.5 slice_reduce_fusion
  320.0 0.0 copy-done.4
  320.0 0.0 copy-done.6
  320.0 0.0 copy-start
  320.0 5.4 %copy-done = f32[2,8,624,384]{3,2,1,0:T(8,128)S(1)} copy-done((f32[2,8,624,384]{3,2,1,0:T(8,128)S(1)}, f32[2,8,624,384]{3,2,1,0:T(8,128)}, u32[]{:S(2)}) %copy-start) | copy-done | bytes 15335448
  325.4 0.0 copy-start.7
  325.4 1.8 copy-done.7
  327.2 0.0 copy-start.11
  327.2 7.8 %unpack_all.1 = (f32[768,384]{1,0:T(8,128)}, f32[768,1536]{1,0:T(8,128)}, f32[3072,384]{1,0:T(8,128)}, f32[768,1152]{1,0:T(8,128)}, f32[768,384]{1,0:T(8,128)}, ...) custom-call(f32[16,624,384]{2,1,0:T(8,128)S(1)} %bitcast.3, f32[16,120,384]{2,1,0:T(8,128)S(1)} %bitcast.5, ...), custom_call_target="tpu_custom_call" | custom-call | tf_op jit(solution)/shard_map/unpack_all/pallas_call | solution.py:941
  335.0 0.0 copy-done.11
  335.0 1.7 copy.36
Async XLA Ops:
  2.2 53.1 %copy-start.3 = (f32[768,1]{1,0:T(8,128)}, f32[768,1]{1,0:T(8,128)S(1)}, u32[]{:S(2)}) copy-start(f32[768,1]{1,0:T(8,128)S(1)} %broadcast_in_dim.22.gain_ref) | copy-start | bytes 9220
  7.0 1.7 copy-start.1
  8.7 1.3 copy-start.2
  10.0 0.9 copy-start.5
  55.3 1.1 copy-start.8
  56.4 0.7 copy-start.9
  57.1 0.7 copy-start.10
  127.8 192.2 %copy-start.4 = (f32[768,1]{1,0:T(8,128)S(1)}, f32[768,1]{1,0:T(8,128)}, u32[]{:S(2)}) copy-start(f32[768,1]{1,0:T(8,128)} %broadcast_in_dim.25.qgain_ref) | copy-start | bytes 9220
  127.8 192.2 %copy-start.6 = (bf16[128,768]{1,0:T(8,128)(2,1)S(1)}, bf16[128,768]{1,0:T(8,128)(2,1)}, u32[]{:S(2)}) copy-start(bf16[128,768]{1,0:T(8,128)(2,1)} %latent_ref.7) | copy-start | bytes 589828
  320.0 5.4 %copy-start = (f32[2,8,624,384]{3,2,1,0:T(8,128)S(1)}, f32[2,8,624,384]{3,2,1,0:T(8,128)}, u32[]{:S(2)}) copy-start(f32[2,8,624,384]{3,2,1,0:T(8,128)} %get-tuple-element.46) | copy-start | bytes 46006276
  325.4 1.8 copy-start.7
  327.2 7.8 %copy-start.11 = (bf16[4,512,768]{2,1,0:T(8,128)(2,1)S(1)}, bf16[4,512,768]{2,1,0:T(8,128)(2,1)}, u32[]{:S(2)}) copy-start(bf16[4,512,768]{2,1,0:T(8,128)(2,1)} %get-tuple-element.75) | copy-start | bytes 9437188

commit v3 on v2

--- a/solution.py
+++ b/solution.py
@@ -12,7 +12,7 @@
 EPSILON = 1e-05
 LANES = 128
 BLOCK = 256
-STREAMS = 2
+STREAMS = 3
 
 
 def nn(left, right):
@@ -29,87 +29,204 @@
     return centered * inverse, inverse
 
 
-def cross_forward_kernel(
-    frames,
-    tokens_ref, w_ref, gain_ref, latent_ref, qgain_ref, wq_ref,
-    kv_out, heard_out, log_out, query_out,
-    tokens, w_t, tok_in, kv, queries, sent, got,
-    load_sem, kv_sem, y_send, y_recv,
+def gelu_parts(value):
+    slope = (2 / jnp.pi) ** 0.5
+    square = value * value
+    tanh = jnp.tanh(slope * value * (1.0 + 0.044715 * square))
+    half = 0.5 + 0.5 * tanh
+    bend = (0.5 * slope) * (1.0 + (3 * 0.044715) * square)
+    return value * half, half + value * (1.0 - tanh * tanh) * bend
+
+
+def norm_down_back(incoming, normed, inverse, gain):
+    scaled = incoming * gain
+    average = jnp.mean(scaled, axis=0, keepdims=True)
+    along = jnp.mean(scaled * normed, axis=0, keepdims=True)
+    return inverse * (scaled - average - normed * along)
+
+
+def gain_columns(gain_ref):
+    return jnp.broadcast_to(gain_ref[...].reshape(1, -1), (LANES, gain_ref.shape[0])).T
+
+
+def loop(count, body):
+    def step(index, carry):
+        body(index)
+        return carry
+
+    lax.fori_loop(0, count, step, 0)
+
+
+def window_at(index, size):
+    return pl.ds(pl.multiple_of(index * size, size), size)
+
+
+def forward_kernel(
+    frames, groups,
+    tokens_ref, skip_ref, latent_ref, tok_gain_ref, query_gain_ref, mlp_gain_ref, self_gain_ref,
+    w_query_ref, w_keyval_ref, w_out_ref, w_up_ref, w_down_ref, w_qkv_ref, w_self_ref, grad_ref,
+    kv_out, log_out, query_out, mid_out, latents_out, d_heard_out, delta_out, d_latent_out, gain_out, arrived,
+    tokens, tok_in, queries, sent, got,
+    w_out, w_out_t, w_self, w_self_t, w_qkv, tall, up_down, down_up,
+    heard, cross, mlp_in, act, slope, after, self_in, triple, mixed, cotangent, d_mixed, d_triple, branch, rows_f32,
+    tok_gain, mlp_gain, self_gain, stage,
+    tok_sem, kv_sem, y_send, y_recv, w_sem, stage_sem, got_sem,
 ):
     items, rows, width = tokens_ref.shape
     latents = latent_ref.shape[0]
+    hidden = w_up_ref.shape[1]
     head = width // HEADS
+    factor = head ** -0.5
+    own = width // frames
+    stat = sent.shape[1] - width
+    pieces = mid_out.shape[0]
     item = lax.axis_index("items")
     frame = lax.axis_index("frames")
-    stat = sent.shape[1] - width
 
     barrier = pltpu.get_barrier_semaphore()
     for hop in range(1, frames):
         pl.semaphore_signal(barrier, inc=1, device_id=(item, lax.rem(frame + hop, frames)), device_id_type=MESH)
 
-    def load(i):
-        return pltpu.make_async_copy(tokens_ref.at[i], tokens.at[i], load_sem.at[i])
-
-    def save(i):
-        return pltpu.make_async_copy(kv.at[i], kv_out.at[i], kv_sem.at[i])
+    wide = 2 * width
+    load_query = pltpu.make_async_copy(w_query_ref, w_self_t, w_sem.at[0])
+    load_keyval = pltpu.make_async_copy(w_keyval_ref, down_up.at[:, pl.ds(0, wide)], w_sem.at[1])
+    load_self = pltpu.make_async_copy(w_self_ref, w_self, w_sem.at[2])
+    load_out = pltpu.make_async_copy(w_out_ref, w_out, w_sem.at[3])
+    load_qkv = pltpu.make_async_copy(w_qkv_ref, w_qkv, w_sem.at[4])
+    load_up = pltpu.make_async_copy(w_up_ref, down_up, w_sem.at[5])
+    load_down_again = pltpu.make_async_copy(w_down_ref, up_down, w_sem.at[6])
+    load_up_again = pltpu.make_async_copy(w_up_ref, down_up, w_sem.at[7])
+
+    def load_tokens(i):
+        return pltpu.make_async_copy(tokens_ref.at[i], tokens.at[lax.rem(i, 2)], tok_sem.at[lax.rem(i, 2)])
+
+    def load_down(part):
+        return pltpu.make_async_copy(w_down_ref.at[pl.ds(part * rows, rows), :], tokens.at[part % 2], tok_sem.at[part % 2])
+
+    def kv_at(i):
+        return pl.ds(pl.multiple_of(lax.rem(i, 2) * wide, wide), wide)
+
+    def save_kv(i):
+        return pltpu.make_async_copy(act.at[kv_at(i), pl.ds(0, rows)], kv_out.at[i], kv_sem.at[lax.rem(i, 2)])
 
     def across(i, hop):
         return pltpu.make_async_remote_copy(
-            src_ref=sent.at[i], dst_ref=got.at[hop - 1, i], send_sem=y_send.at[hop - 1, i], recv_sem=y_recv.at[hop - 1, i],
+            src_ref=sent.at[i], dst_ref=(arrived if frames > 2 else got).at[hop - 1, i], send_sem=y_send.at[hop - 1, i], recv_sem=y_recv.at[hop - 1, i],
             device_id=(item, lax.rem(frame + hop, frames)), device_id_type=MESH,
         )
 
-    for i in range(items):
-        load(i).start()
-    for block in range(2 * width // 256):
-        w_t[pl.ds(block * 256, 256), :] = w_ref[:, pl.ds(block * 256, 256)].T
-    rows_in = latent_ref[...].astype(jnp.float32)
-    centered = rows_in - jnp.mean(rows_in, axis=-1, keepdims=True)
-    inverse = lax.rsqrt(jnp.mean(centered * centered, axis=-1, keepdims=True) + EPSILON)
-    query_in = (centered * inverse * qgain_ref[...]).astype(jnp.bfloat16)
-    query = nn(query_in, wq_ref[...]).astype(jnp.bfloat16)
+    load_tokens(0).start()
+    load_query.start()
+    load_keyval.start()
+    load_tokens(1).start()
+    for copy in (load_self, load_out, load_qkv):
+        copy.start()
+
+    latent_t = latent_ref[...].astype(jnp.float32).T
+    query_normed, _ = norm_down(latent_t)
+    query_in = (query_normed * gain_columns(query_gain_ref)).T.astype(jnp.bfloat16)
+    tok_gain[...] = gain_columns(tok_gain_ref)
+    mlp_gain[...] = gain_columns(mlp_gain_ref)
+    self_gain[...] = gain_columns(self_gain_ref)
+    load_query.wait()
+    query = nn(query_in, w_self_t[...]).astype(jnp.bfloat16)
     query_out[...] = query
-    scaled = query * jnp.bfloat16(head ** -0.5)
+    scaled = query * jnp.bfloat16(factor)
     for h in range(HEADS):
         queries[h] = scaled[:, h * head : (h + 1) * head]
+    load_keyval.wait()
+    for block in range(wide // BLOCK):
+        window = pl.ds(block * BLOCK, BLOCK)
+        tall[window, :] = down_up[:, window].T
+    load_up.start()
     pl.semaphore_wait(barrier, frames - 1)
 
-    def one_item(i, carry):
-        load(i).wait()
-
-        def norm_block(b, inner):
-            window = pl.ds(pl.multiple_of(b * LANES, LANES), LANES)
-            columns = tokens[i, window, :].T.astype(jnp.float32)
-            normed, _ = norm_down(columns)
-            tok_in[:, window] = (normed * gain_ref[...]).astype(jnp.bfloat16)
-            return inner
-
-        lax.fori_loop(0, rows // LANES, norm_block, 0)
-        for block in range(2 * width // 256):
-            window = pl.ds(block * 256, 256)
-            kv[i, window, :] = nn(w_t[window, :], tok_in[...]).astype(jnp.bfloat16)
-        save(i).start()
+    def heard_item(i):
+        slot = lax.rem(i, 2)
+        load_tokens(i).wait()
+
+        def norm_block(b):
+            window = window_at(b, LANES)
+            normed, _ = norm_down(tokens[slot, window, :].T.astype(jnp.float32))
+            tok_in[:, window] = (normed * tok_gain[...]).astype(jnp.bfloat16)
+
+        loop(rows // LANES, norm_block)
+
+        @pl.when(i + 2 < items)
+        def _():
+            load_tokens(i + 2).start()
+
+        @pl.when(i >= 2)
+        def _():
+            save_kv(i - 2).wait()
+
+        base = pl.multiple_of(slot * wide, wide)
+        for block in range(wide // BLOCK):
+            act[pl.ds(base + block * BLOCK, BLOCK), pl.ds(0, rows)] = nn(
+                tall[pl.ds(block * BLOCK, BLOCK), :], tok_in[...]
+            ).astype(jnp.bfloat16)
+        save_kv(i).start()
         lane = lax.broadcasted_iota(jnp.int32, (latents, LANES), 1)
         stats = jnp.zeros((latents, LANES), jnp.float32)
         for h in range(HEADS):
-            scores = nn(queries[h], kv[i, pl.ds(h * head, head), :])
+            scores = nn(queries[h], act[pl.ds(base + h * head, head), pl.ds(0, rows)])
             most = jnp.max(scores, axis=-1, keepdims=True)
             shifted = jnp.exp(scores - most)
             total = jnp.sum(shifted, axis=-1, keepdims=True)
             stats = jnp.where(lane == h, most, stats)
             stats = jnp.where(lane == h + stat // 2, total, stats)
-            sent[i, pl.ds(h * head, head), :] = nt(kv[i, pl.ds(width + h * head, head), :], shifted.astype(jnp.bfloat16))
+            sent[i, pl.ds(h * head, head), :] = nt(
+                act[pl.ds(base + width + h * head, head), pl.ds(0, rows)], shifted.astype(jnp.bfloat16)
+            )
         sent[i, pl.ds(width, stat), :] = stats.T[:stat]
         for hop in range(1, frames):
             across(i, hop).start()
-        return carry
-
-    lax.fori_loop(0, items, one_item, 0)
-
-    def combine(i, carry):
+
+    loop(items, heard_item)
+    load_down(0).start()
+    load_down(1).start()
+
+    def turn(source, target, count):
+        def block(b):
+            window = window_at(b, BLOCK)
+            target[window, :] = source[:, window].T
+
+        loop(count // BLOCK, block)
+
+    load_self.wait()
+
+    def load_cotangent(i):
+        cotangent[:, window_at(i, latents)] = grad_ref[i].T
+
+    loop(items, load_cotangent)
+    for block in range(width // BLOCK):
+        window = pl.ds(block * BLOCK, BLOCK)
+        d_mixed[window, :] = nn(w_self[window, :], cotangent[...]).astype(jnp.bfloat16)
+    turn(w_self, w_self_t, width)
+    load_out.wait()
+    turn(w_out, w_out_t, width)
+    load_up.wait()
+    turn(down_up, up_down, hidden)
+    for part in range(hidden // rows):
+        load_down(part).wait()
+        for block in range(rows // BLOCK):
+            down_up[:, pl.ds(part * rows + block * BLOCK, BLOCK)] = tokens[part % 2, pl.ds(block * BLOCK, BLOCK), :].T
+        if part + 2 < hidden // rows:
+            load_down(part + 2).start()
+    load_qkv.wait()
+    turn(w_qkv, tall, 3 * width)
+    for i in range(max(items - 2, 0), items):
+        save_kv(i).wait()
+
+    def combine(i):
         for hop in range(1, frames):
+            across(i, hop).wait_send()
             across(i, hop).wait_recv()
-        parts = [sent.at[i]] + [got.at[hop, i] for hop in range(frames - 1)]
+            if frames > 2:
+                near = pltpu.make_async_copy(arrived.at[hop - 1, i], got.at[hop - 1, 0], got_sem)
+                near.start()
+                near.wait()
+        parts = [sent.at[i]] + [got.at[hop, 0 if frames > 2 else i] for hop in range(frames - 1)]
         highs = [part[pl.ds(width, stat // 2), :] for part in parts]
         sums = [part[pl.ds(width + stat // 2, stat // 2), :] for part in parts]
         most = functools.reduce(jnp.maximum, highs)
@@ -118,205 +235,121 @@
         scales = [jnp.exp(high - log_total) for high in highs]
         for h in range(HEADS):
             window = pl.ds(h * head, head)
-            heard_out[i, window, :] = functools.reduce(
+            together = functools.reduce(
                 jnp.add, [part[window, :] * scale[h : h + 1] for part, scale in zip(parts, scales)]
             )
-        padded = jnp.concatenate([log_total, jnp.zeros((latents - stat // 2, latents), jnp.float32)], axis=0)
+            sent[i, window, :] = together
+            heard[window, window_at(i, latents)] = together.astype(jnp.bfloat16)
+        padded = jnp.concatenate([log_total, jnp.zeros((LANES - stat // 2, latents), jnp.float32)], axis=0)
         log_out[i] = padded.T
-        return carry
-
-    lax.fori_loop(0, items, combine, 0)
-    for i in range(items):
-        save(i).wait()
-        for hop in range(1, frames):
-            across(i, hop).wait_send()
-
-
-def cross_forward(frames, tokens, w_keyval, tok_gain, latent_init, query_gain, w_query):
-    items, rows, width = tokens.shape
-    latents = latent_init.shape[0]
-    dma = pltpu.SemaphoreType.DMA
-    vmem = pl.BlockSpec(memory_space=pltpu.VMEM)
-    anywhere = pl.BlockSpec(memory_space=pl.ANY)
-    peers = max(frames - 1, 1)
-    return pl.pallas_call(
-        functools.partial(cross_forward_kernel, frames),
-        out_shape=(
-            jax.ShapeDtypeStruct((items, 2 * width, rows), jnp.bfloat16),
-            jax.ShapeDtypeStruct((items, width, latents), jnp.float32),
-            jax.ShapeDtypeStruct((items, latents, LANES), jnp.float32),
-            jax.ShapeDtypeStruct((latents, width), jnp.bfloat16),
-        ),
-        in_specs=[anywhere] + [vmem] * 5,
-        out_specs=(anywhere, vmem, vmem, vmem),
-        scratch_shapes=[
-            pltpu.VMEM((items, rows, width), jnp.bfloat16),
-            pltpu.VMEM((2 * width, width), jnp.bfloat16),
-            pltpu.VMEM((width, rows), jnp.bfloat16),
-            pltpu.VMEM((items, 2 * width, rows), jnp.bfloat16),
-            pltpu.VMEM((HEADS, latents, width // HEADS), jnp.bfloat16),
-            pltpu.VMEM((items, width + 32, latents), jnp.float32),
-            pltpu.VMEM((peers, items, width + 32, latents), jnp.float32),
-            dma((items,)), dma((items,)), dma((peers, items)), dma((peers, items)),
-        ],
-        compiler_params=pltpu.CompilerParams(collective_id=1, has_side_effects=True, vmem_limit_bytes=48 * 2**20),
-        name="cross_forward",
-    )(tokens, w_keyval, tok_gain[:, None], latent_init, query_gain[None, :], w_query)
-
-
-def gelu_parts(value):
-    slope = (2 / jnp.pi) ** 0.5
-    square = value * value
-    tanh = jnp.tanh(slope * value * (1.0 + 0.044715 * square))
-    half = 0.5 + 0.5 * tanh
-    bend = (0.5 * slope) * (1.0 + (3 * 0.044715) * square)
-    return value * half, half + value * (1.0 - tanh * tanh) * bend
-
-
-def norm_down_back(incoming, normed, inverse, gain):
-    scaled = incoming * gain
-    average = jnp.mean(scaled, axis=0, keepdims=True)
-    along = jnp.mean(scaled * normed, axis=0, keepdims=True)
-    return inverse * (scaled - average - normed * along)
-
-
-def middle_kernel(
-    frames,
-    heard_ref, skip_ref, latent_ref, grad_ref, mgain_ref, sgain_ref,
-    w_out_ref, w_up_ref, w_down_ref, w_qkv_ref, w_self_ref,
-    mid_out, latents_out, d_heard_out, delta_out, d_latent_out, gain_out,
-    w_out, w_up, w_down, w_qkv, w_self,
-    heard, cross, mlp_in, act, slope, after, self_in, triple, mixed, cotangent, d_mixed, d_triple, d_hidden, branch,
-    rows_f32, stage,
-    w_sem, stage_sem,
-):
-    items, width, latents = heard_ref.shape
-    hidden = w_up_ref.shape[1]
-    head = width // HEADS
-    factor = head ** -0.5
-    own = width // frames
-    frame = lax.axis_index("frames")
-    pieces = mid_out.shape[0]
-    loads = [
-        pltpu.make_async_copy(source, target, w_sem.at[index])
-        for index, (source, target) in enumerate(
-            ((w_self_ref, w_self), (w_out_ref, w_out), (w_up_ref, w_up), (w_down_ref, w_down), (w_qkv_ref, w_qkv))
-        )
-    ]
-    for copy in loads:
-        copy.start()
-
-    def item_window(i):
-        return pl.ds(pl.multiple_of(i * latents, latents), latents)
+
+    def attend(i):
+        window = window_at(i, latents)
+        for first in range(0, HEADS, 4):
+            at = [[pl.ds(third * width + h * head, head) for third in range(3)] for h in range(first, first + 4)]
+            query = [triple[where[0], window] * jnp.bfloat16(factor) for where in at]
+            key = [triple[where[1], window] for where in at]
+            value = [triple[where[2], window] for where in at]
+            d_mix = [d_mixed[where[0], window] for where in at]
+            scores = [nn(k.T, q) for k, q in zip(key, query)]
+            d_probs = [nn(v.T, d) for v, d in zip(value, d_mix)]
+            shifted = [jnp.exp(s - jnp.max(s, axis=0, keepdims=True)) for s in scores]
+            probs = [s * (1.0 / jnp.sum(s, axis=0, keepdims=True)) for s in shifted]
+            low = [p.astype(jnp.bfloat16) for p in probs]
+            mix = [nn(v, p) for v, p in zip(value, low)]
+            delta = [jnp.sum(d.astype(jnp.float32) * m, axis=0, keepdims=True) for d, m in zip(d_mix, mix)]
+            d_scores = [(p * (d - x)).astype(jnp.bfloat16) for p, d, x in zip(probs, d_probs, delta)]
+            d_query = [nn(k, d) * factor for k, d in zip(key, d_scores)]
+            d_key = [nt(q, d) for q, d in zip(query, d_scores)]
+            d_value = [nt(d, p) for d, p in zip(d_mix, low)]
+            for where, m, dq, dk, dv in zip(at, mix, d_query, d_key, d_value):
+                mixed[where[0], window] = m.astype(jnp.bfloat16)
+                d_triple[where[0], window] = dq.astype(jnp.bfloat16)
+                d_triple[where[1], window] = dk.astype(jnp.bfloat16)
+                d_triple[where[2], window] = dv.astype(jnp.bfloat16)
+
+    def forward_group(group):
+        size = items // groups
+        first = group * size
+        columns = pl.ds(first * latents, size * latents)
+
+        def each_item(body):
+            loop(size, lambda i: body(first + i))
+
+        def each_block(count, body):
+            loop(count // BLOCK, lambda b: body(window_at(b, BLOCK)))
+
+        each_item(combine)
+
+        def out_block(window):
+            cross[window, columns] = nn(w_out_t[window, :], heard[:, columns])
+
+        each_block(width, out_block)
+
+        def cross_item(i):
+            window = window_at(i, latents)
+            keep = (1 - skip_ref[i]).astype(jnp.float32)
+            total = latent_ref[...].astype(jnp.float32).T + keep * cross[:, window]
+            cross[:, window] = total
+            normed, _ = norm_down(total)
+            mlp_in[:, window] = (normed * mlp_gain[...]).astype(jnp.bfloat16)
+
+        each_item(cross_item)
+
+        def up_block(window):
+            value, bend = gelu_parts(nn(up_down[window, :], mlp_in[:, columns]))
+            act[window, columns] = value.astype(jnp.bfloat16)
+            slope[window, columns] = bend
+
+        each_block(hidden, up_block)
+        if group == groups - 1:
+            load_down_again.start()
+
+        def down_block(window):
+            after[window, columns] = cross[window, columns] + nn(down_up[window, :], act[:, columns])
+
+        each_block(width, down_block)
+        if group == groups - 1:
+            load_up_again.start()
+
+        def after_item(i):
+            window = window_at(i, latents)
+            normed, _ = norm_down(after[:, window])
+            self_in[:, window] = (normed * self_gain[...]).astype(jnp.bfloat16)
+
+        each_item(after_item)
+
+        def triple_block(window):
+            triple[window, columns] = nn(tall[window, :], self_in[:, columns]).astype(jnp.bfloat16)
+
+        each_block(3 * width, triple_block)
+        each_item(attend)
+
+    for group in range(groups):
+        forward_group(group)
 
     def each_item(body):
-        def step(i, carry):
-            body(i, item_window(i))
-            return carry
-
-        lax.fori_loop(0, items, step, 0)
+        loop(items, lambda i: body(i, window_at(i, latents)))
 
     def each_block(count, body):
-        def step(b, carry):
-            body(pl.ds(pl.multiple_of(b * BLOCK, BLOCK), BLOCK))
-            return carry
-
-        lax.fori_loop(0, count // BLOCK, step, 0)
-
-    def down(weight, source, window):
-        return nn(weight[:, window].T, source[...])
-
-    sent = [0]
+        loop(count // BLOCK, lambda b: body(window_at(b, BLOCK)))
 
     pending = {}
 
     def put(first_piece, count, offset, left, right):
         size = width // count
-        slot = sent[0] % stage.shape[0]
-        sent[0] += 1
-        if slot in pending:
-            pending[slot].wait()
+        slot = len(pending) % stage.shape[0]
+        for key in [key for key in pending if key % stage.shape[0] == slot and pending[key] is not None]:
+            pending[key].wait()
+            pending[key] = None
         view = stage.at[slot]
-        for block in range(width // BLOCK):
-            window = pl.ds(block * BLOCK, BLOCK)
-            view[window, :] = nt(left[window, :], right[...])
-        copies = pltpu.make_async_copy(
+        view[...] = nt(left[...], right[...])
+        copy = pltpu.make_async_copy(
             view.reshape(count, size, own), mid_out.at[pl.ds(first_piece, count), pl.ds(offset, size)], stage_sem.at[slot]
         )
-        copies.start()
-        pending[slot] = copies
-
-    def load_heard(i, window):
-        heard[:, window] = heard_ref[i].astype(jnp.bfloat16)
-        cotangent[:, window] = grad_ref[i].T
-
-    each_item(load_heard)
-    loads[0].wait()
-
-    def back_mixed(window):
-        d_mixed[window, :] = nn(w_self[window, :], cotangent[...]).astype(jnp.bfloat16)
-
-    each_block(width, back_mixed)
-    loads[1].wait()
-
-    def out_block(window):
-        cross[window, :] = down(w_out, heard, window)
-
-    each_block(width, out_block)
-
-    def cross_item(i, window):
-        keep = (1 - skip_ref[i]).astype(jnp.float32)
-        total = latent_ref[...].astype(jnp.float32).T + keep * cross[:, window]
-        cross[:, window] = total
-        normed, _ = norm_down(total)
-        mlp_in[:, window] = (normed * mgain_ref[...]).astype(jnp.bfloat16)
-
-    each_item(cross_item)
-    loads[2].wait()
-
-    def up_block(window):
-        value, bend = gelu_parts(down(w_up, mlp_in, window))
-        act[window, :] = value.astype(jnp.bfloat16)
-        slope[window, :] = bend
-
-    each_block(hidden, up_block)
-    loads[3].wait()
-
-    def down_block(window):
-        after[window, :] = cross[window, :] + down(w_down, act, window)
-
-    each_block(width, down_block)
-
-    def after_item(i, window):
-        normed, _ = norm_down(after[:, window])
-        self_in[:, window] = (normed * sgain_ref[...]).astype(jnp.bfloat16)
-
-    each_item(after_item)
-    loads[4].wait()
-
-    def triple_block(window):
-        triple[window, :] = down(w_qkv, self_in, window).astype(jnp.bfloat16)
-
-    each_block(3 * width, triple_block)
-
-    def attend_item(i, window):
-        for h in range(HEADS):
-            part = [pl.ds(third * width + h * head, head) for third in range(3)]
-            query, key, value = [triple[rows, window] for rows in part]
-            d_mix = d_mixed[part[0], window]
-            scores = nn(query.T, key) * factor
-            shifted = jnp.exp(scores - jnp.max(scores, axis=-1, keepdims=True))
-            probs = shifted / jnp.sum(shifted, axis=-1, keepdims=True)
-            low = probs.astype(jnp.bfloat16)
-            mixed[part[0], window] = nt(value, low).astype(jnp.bfloat16)
-            d_probs = nn(d_mix.T, value)
-            delta = jnp.sum(low.astype(jnp.float32) * d_probs, axis=-1, keepdims=True)
-            d_scores = (probs * (d_probs - delta)).astype(jnp.bfloat16)
-            d_triple[part[0], window] = (nt(key, d_scores) * factor).astype(jnp.bfloat16)
-            d_triple[part[1], window] = (nn(query, d_scores) * factor).astype(jnp.bfloat16)
-            d_triple[part[2], window] = nn(d_mix, low).astype(jnp.bfloat16)
-
-    each_item(attend_item)
+        copy.start()
+        pending[len(pending)] = copy
+
     up_rows, down_rows = width // pieces, hidden // pieces
     first_up = up_rows
     first_down = first_up + up_rows * (hidden // width)
@@ -338,14 +371,14 @@
         normed, inverse = norm_down(after[:, window])
         incoming = rows_f32[:, window]
         gain_out[...] += jnp.where(lane == 1, jnp.sum(incoming * normed, axis=-1, keepdims=True), 0.0)
-        d_after = cotangent[:, window].astype(jnp.float32) + norm_down_back(incoming, normed, inverse, sgain_ref[...])
+        d_after = cotangent[:, window].astype(jnp.float32) + norm_down_back(incoming, normed, inverse, self_gain[...])
         branch[:, window] = d_after.astype(jnp.bfloat16)
         rows_f32[:, window] = d_after
 
     each_item(self_back)
 
     def latents_block(window):
-        after[window, :] = after[window, :] + down(w_self, mixed, window)
+        after[window, :] = after[window, :] + nn(w_self_t[window, :], mixed[...])
 
     each_block(width, latents_block)
     share = latents // frames
@@ -355,21 +388,21 @@
         latents_out[i] = d_latent_out[pl.ds(pl.multiple_of(frame * share, share), share), :].astype(jnp.bfloat16)
 
     each_item(latents_item)
-
     for group in range(hidden // width):
-        left = act.at[pl.ds(group * width, width), :]
         count = pieces * width // hidden
-        put(group * count, count, first_down, left, branch.at[pl.ds(my_columns, own), :])
+        put(group * count, count, first_down, act.at[pl.ds(group * width, width), :], branch.at[pl.ds(my_columns, own), :])
+    load_down_again.wait()
 
     def hidden_block(window):
-        d_hidden[window, :] = (nn(w_down[window, :], branch[...]) * slope[window, :]).astype(jnp.bfloat16)
+        triple[window, :] = (nn(up_down[window, :], branch[...]) * slope[window, :]).astype(jnp.bfloat16)
 
     each_block(hidden, hidden_block)
     for part in range(hidden // width):
-        put(0, pieces, first_up + part * up_rows, mlp_in, d_hidden.at[pl.ds(frame * (hidden // frames) + part * own, own), :])
+        put(0, pieces, first_up + part * up_rows, mlp_in, triple.at[pl.ds(frame * (hidden // frames) + part * own, own), :])
+    load_up_again.wait()
 
     def mlp_block(window):
-        after[window, :] = nn(w_up[window, :], d_hidden[...])
+        after[window, :] = nn(down_up[window, :], triple[...])
 
     each_block(width, mlp_block)
     d_latent_out[...] = jnp.zeros_like(d_latent_out)
@@ -378,7 +411,7 @@
         normed, inverse = norm_down(cross[:, window])
         incoming = after[:, window]
         gain_out[...] += jnp.where(lane == 0, jnp.sum(incoming * normed, axis=-1, keepdims=True), 0.0)
-        d_cross = rows_f32[:, window] + norm_down_back(incoming, normed, inverse, mgain_ref[...])
+        d_cross = rows_f32[:, window] + norm_down_back(incoming, normed, inverse, mlp_gain[...])
         d_latent_out[...] += d_cross.T
         keep = (1 - skip_ref[i]).astype(jnp.float32)
         branch[:, window] = (keep * d_cross).astype(jnp.bfloat16)
@@ -392,61 +425,87 @@
     each_block(width, heard_block)
 
     def delta_item(i, window):
-        product = d_heard_out[:, window].astype(jnp.float32) * heard_ref[i]
+        product = d_heard_out[:, window].astype(jnp.float32) * sent[i, pl.ds(0, width), :]
         sums = jnp.sum(product.reshape(HEADS, head, latents), axis=1)
-        padded = jnp.concatenate([sums, jnp.zeros((latents - HEADS, latents), jnp.float32)], axis=0)
+        padded = jnp.concatenate([sums, jnp.zeros((LANES - HEADS, latents), jnp.float32)], axis=0)
         delta_out[i] = padded.T
 
     each_item(delta_item)
     for copy in pending.values():
-        copy.wait()
-
-
-def middle(frames, pieces, heard, skip, latent_init, grad_out, mlp_gain, self_gain, w_out, w_up, w_down, w_self_qkv, w_self_out):
-    items, width, latents = heard.shape
+        if copy is not None:
+            copy.wait()
+
+
+def forward(
+    frames, pieces, tokens, skip, latent_init, tok_gain, query_gain, mlp_gain, self_gain,
+    w_query, w_keyval, w_out, w_up, w_down, w_self_qkv, w_self_out, grad_out,
+):
+    items, rows, width = tokens.shape
+    latents = latent_init.shape[0]
     hidden = w_up.shape[1]
     own = width // frames
     columns = items * latents
-    rows = (width + hidden + hidden + 3 * width + width) // pieces
+    mid_rows = (5 * width + 2 * hidden) // pieces
     bf16, f32 = jnp.bfloat16, jnp.float32
     vmem = pl.BlockSpec(memory_space=pltpu.VMEM)
     anywhere = pl.BlockSpec(memory_space=pl.ANY)
     dma = pltpu.SemaphoreType.DMA
+    peers = max(frames - 1, 1)
     return pl.pallas_call(
-        functools.partial(middle_kernel, frames),
+        functools.partial(forward_kernel, frames, 2 if items % 2 == 0 else 1),
         out_shape=(
-            jax.ShapeDtypeStruct((pieces, rows, own), f32),
+            jax.ShapeDtypeStruct((items, 2 * width, rows), bf16),
+            jax.ShapeDtypeStruct((items, latents, LANES), f32),
+            jax.ShapeDtypeStruct((latents, width), bf16),
+            jax.ShapeDtypeStruct((pieces, mid_rows, own), f32),
             jax.ShapeDtypeStruct((items, latents // frames, width), bf16),
             jax.ShapeDtypeStruct((width, columns), bf16),
             jax.ShapeDtypeStruct((items, latents, LANES), f32),
             jax.ShapeDtypeStruct((latents, width), f32),
             jax.ShapeDtypeStruct((width, LANES), f32),
+            jax.ShapeDtypeStruct((peers, items if frames > 2 else 1, width + 32, latents), f32),
         ),
-        in_specs=[vmem, pl.BlockSpec(memory_space=pltpu.SMEM)] + [vmem] * 4 + [anywhere] * 5,
-        out_specs=(anywhere,) + (vmem,) * 5,
-        scratch_shapes=[pltpu.VMEM(w.shape, bf16) for w in (w_out, w_up, w_down, w_self_qkv, w_self_out)]
+        in_specs=[anywhere, pl.BlockSpec(memory_space=pltpu.SMEM)] + [vmem] * 5 + [anywhere] * 7 + [vmem],
+        out_specs=(anywhere, vmem, vmem, anywhere) + (vmem,) * 5 + (anywhere,),
+        scratch_shapes=[
+            pltpu.VMEM((2, rows, width), bf16),
+            pltpu.VMEM((width, rows), bf16),
+            pltpu.VMEM((HEADS, latents, width // HEADS), bf16),
+            pltpu.VMEM((items, width + 32, latents), f32),
+            pltpu.VMEM((peers, 1 if frames > 2 else items, width + 32, latents), f32),
+        ]
+        + [pltpu.VMEM((width, width), bf16)] * 4
         + [
+            pltpu.VMEM((width, 3 * width), bf16),
+            pltpu.VMEM((3 * width, width), bf16),
+            pltpu.VMEM((hidden, width), bf16),
+            pltpu.VMEM((width, hidden), bf16),
             pltpu.VMEM((width, columns), bf16),
             pltpu.VMEM((width, columns), f32),
             pltpu.VMEM((width, columns), bf16),
-            pltpu.VMEM((hidden, columns), bf16),
+            pltpu.VMEM((hidden, max(columns, rows)), bf16),
             pltpu.VMEM((hidden, columns), f32),
             pltpu.VMEM((width, columns), f32),
             pltpu.VMEM((width, columns), bf16),
-            pltpu.VMEM((3 * width, columns), bf16),
+            pltpu.VMEM((hidden, columns), bf16),
             pltpu.VMEM((width, columns), bf16),
             pltpu.VMEM((width, columns), bf16),
             pltpu.VMEM((width, columns), bf16),
             pltpu.VMEM((3 * width, columns), bf16),
-            pltpu.VMEM((hidden, columns), bf16),
             pltpu.VMEM((width, columns), bf16),
             pltpu.VMEM((width, columns), f32),
-            pltpu.VMEM((3, width, own), f32),
-            dma((5,)), dma((3,)),
+            pltpu.VMEM((width, LANES), f32),
+            pltpu.VMEM((width, LANES), f32),
+            pltpu.VMEM((width, LANES), f32),
+            pltpu.VMEM((2, width, own), f32),
+            dma((2,)), dma((2,)), dma((peers, items)), dma((peers, items)), dma((8,)), dma((2,)), dma,
         ],
-        compiler_params=pltpu.CompilerParams(vmem_limit_bytes=58 * 2**20),
-        name="middle",
-    )(heard, skip, latent_init, grad_out, mlp_gain[:, None], self_gain[:, None], w_out, w_up, w_down, w_self_qkv, w_self_out)
+        compiler_params=pltpu.CompilerParams(collective_id=1, has_side_effects=True, vmem_limit_bytes=62 * 2**20),
+        name="forward",
+    )(
+        tokens, skip, latent_init, tok_gain, query_gain, mlp_gain, self_gain,
+        w_query, w_keyval, w_out, w_up, w_down, w_self_qkv, w_self_out, grad_out,
+    )
 
 
 def add_into(target, parts, rows):
@@ -479,7 +538,7 @@
     w_ref, gain_ref, latent_ref, qgain_ref, wq_ref, d_latent_ref, gains_ref,
     mid_out, kv_out, token_out,
     mine, sib, rx, kmine, ksib, ky, krx,
-    tokens, kv, tok_in, d_kv, normed, incoming, queries, queries_t, d_query, gain_sum, token_stage,
+    tokens, kv, tok_in, d_kv, normed, incoming, queries, queries_t, d_query, gain_sum, tok_gain, token_stage,
     ld_sem, sib_send, sib_recv, rs_send, rs_recv, ag_send, ag_recv, share_send, share_recv, own_sem,
     ksib_send, ksib_recv, y_send, y_recv, krs_send, krs_recv, kag_send, kag_recv, kshare_send, kshare_recv,
     tok_sem, kv_sem, out_sem,
@@ -660,6 +719,7 @@
     for h in range(HEADS):
         queries[h] = scaled[:, h * head : (h + 1) * head]
     queries_t[...] = scaled.T
+    tok_gain[...] = gain_columns(gain_ref)
     d_query[...] = jnp.zeros_like(d_query)
     gain_sum[...] = jnp.zeros_like(gain_sum)
     pl.semaphore_wait(barrier, 3 + frames - 1)
@@ -689,7 +749,7 @@
             block, inverse = norm_down(columns)
             normed[pl.ds(0, width), window] = block
             normed[pl.ds(width, 8), window] = jnp.broadcast_to(inverse, (8, LANES))
-            tok_in[:, pl.ds(pl.multiple_of(i * rows + b * LANES, LANES), LANES)] = (block * gain_ref[...]).astype(jnp.bfloat16)
+            tok_in[:, pl.ds(pl.multiple_of(i * rows + b * LANES, LANES), LANES)] = (block * tok_gain[...]).astype(jnp.bfloat16)
             return carry
 
         lax.fori_loop(0, rows // LANES, norm_block, 0)
@@ -709,7 +769,7 @@
             block = normed[pl.ds(0, width), window]
             arriving = incoming[:, window]
             gain_sum[...] += arriving * block
-            result = norm_down_back(arriving, block, normed[pl.ds(width, 1), window], gain_ref[...])
+            result = norm_down_back(arriving, block, normed[pl.ds(width, 1), window], tok_gain[...])
 
             @pl.when((i > 0) | (b > 1))
             def _():
@@ -750,11 +810,11 @@
     q_normed, q_inverse = norm_down(latent_ref[...].astype(jnp.float32).T)
     q_incoming = nn_exact(wq_ref[...], q_total)
     lane = lax.broadcasted_iota(jnp.int32, (width, LANES), 1)
-    gain_columns = gains_ref[...]
-    gain_columns = jnp.where(lane == 2, jnp.sum(gain_sum[...], axis=-1, keepdims=True), gain_columns)
-    gain_columns = jnp.where(lane == 3, jnp.sum(q_incoming * q_normed, axis=-1, keepdims=True), gain_columns)
-    gain_rows = gain_columns.T[:8]
-    latent_rows = norm_down_back(q_incoming, q_normed, q_inverse, qgain_ref[...]).T
+    all_gains = gains_ref[...]
+    all_gains = jnp.where(lane == 2, jnp.sum(gain_sum[...], axis=-1, keepdims=True), all_gains)
+    all_gains = jnp.where(lane == 3, jnp.sum(q_incoming * q_normed, axis=-1, keepdims=True), all_gains)
+    gain_rows = all_gains.T[:8]
+    latent_rows = norm_down_back(q_incoming, q_normed, q_inverse, gain_columns(qgain_ref)).T
     query_rows = q_total.T
     for f in range(frames):
         mask = (frame == f).astype(jnp.float32)
@@ -863,6 +923,7 @@
         pltpu.VMEM((width, latents), bf16),
         pltpu.VMEM((width, latents), f32),
         pltpu.VMEM((width, LANES), f32),
+        pltpu.VMEM((width, LANES), f32),
         pltpu.VMEM((2, LANES, width), bf16),
         dma((chips,)), dma((chips,)), dma((chips,)),
         dma((n, chips)), dma((n, chips)), dma((n, chips)), dma((n, chips)), dma((n, chips)), dma((n, chips)), dma((n + 1,)),
@@ -884,28 +945,33 @@
         compiler_params=pltpu.CompilerParams(collective_id=0, has_side_effects=True, vmem_limit_bytes=62 * 2**20),
         name="backward",
     )(
-        mid, tokens, kv, d_heard, log_total, delta, query, w_keyval, tok_gain[:, None], latent_init,
-        query_gain[:, None], w_query, d_latent, gains,
+        mid, tokens, kv, d_heard, log_total, delta, query, w_keyval, tok_gain, latent_init,
+        query_gain, w_query, d_latent, gains,
     )
 
 
 def unpack_kernel(mid_ref, kv_ref, latent_ref, qgain_ref, *rest):
-    outs, (query_out, total, sem) = rest[:-3], rest[-3:]
+    outs, (query_out, *gain_outs), (blocks, total, tail, in_sem, out_sem) = rest[:7], rest[7:12], rest[12:]
     pieces, _, own = mid_ref.shape
-    copies = []
+    loads, stores = [], []
 
     def place(source, offset, out):
         rows, columns = out.shape
         size = rows // pieces
         view = out.reshape(pieces, size, columns)
         for b in range(columns // own):
-            copies.append(
-                pltpu.make_async_copy(
-                    source.at[:, pl.ds(offset + b * size, size), :], view.at[:, :, pl.ds(b * own, own)], sem.at[len(copies)]
-                )
-            )
+            at = len(loads)
+            area = blocks.at[pl.ds(starts[at], pieces * size), :].reshape(pieces, size, own)
+            loads.append(pltpu.make_async_copy(source.at[:, pl.ds(offset + b * size, size), :], area, in_sem.at[at]))
+            stores.append(pltpu.make_async_copy(area, view.at[:, :, pl.ds(b * own, own)], out_sem.at[at]))
         return offset + size * columns // own
 
+    starts, start = [], 0
+    for out in outs[:6]:
+        rows, columns = out.shape
+        for b in range(columns // own):
+            starts.append(start)
+            start += rows
     offset = 0
     for out in outs[:5]:
         offset = place(mid_ref, offset, out)
@@ -913,21 +979,25 @@
     latents = outs[6].shape[0]
     small = 2 * latents // pieces
     half = pieces // 2
-    copies.append(
-        pltpu.make_async_copy(
-            kv_ref.at[pl.ds(half, half), pl.ds(offset, small), :], outs[6].reshape(half, small, own), sem.at[len(copies)]
-        )
-    )
-    query = pltpu.make_async_copy(kv_ref.at[pl.ds(0, half), pl.ds(offset, small), :], total, sem.at[len(copies)])
+    query = pltpu.make_async_copy(kv_ref.at[:, pl.ds(offset, small), :], total, in_sem.at[len(loads)])
+    gains = pltpu.make_async_copy(kv_ref.at[0, pl.ds(offset + small, 8), :], tail, in_sem.at[len(loads) + 1])
     query.start()
-    for copy in copies:
+    gains.start()
+    for copy in loads:
         copy.start()
     normed, _ = norm_down(latent_ref[...].astype(jnp.float32).T)
-    query_in = (normed * qgain_ref[...]).astype(jnp.bfloat16)
+    query_in = (normed * gain_columns(qgain_ref)).astype(jnp.bfloat16)
     query.wait()
-    query_out[...] = nn_exact(query_in, total[...].reshape(latents, own))
-    for copy in copies:
-        copy.wait()
+    query_out[...] = nn_exact(query_in, total[pl.ds(0, half)].reshape(latents, own))
+    outs[6][...] = total[pl.ds(half, half)].reshape(latents, own)
+    gains.wait()
+    for out, row in zip(gain_outs, (2, 3, 0, 1)):
+        out[...] = tail[row]
+    for load, store in zip(loads, stores):
+        load.wait()
+        store.start()
+    for store in stores:
+        store.wait()
 
 
 def unpack_all(mid, kv, latent_init, query_gain, shapes):
@@ -937,17 +1007,22 @@
     pieces = mid.shape[0]
     vmem = pl.BlockSpec(memory_space=pltpu.VMEM)
     anywhere = pl.BlockSpec(memory_space=pl.ANY)
-    count = sum(columns // own for _, columns in shapes) + 2
+    count = sum(columns // own for _, columns in shapes)
+    size = sum(rows * columns // own for rows, columns in shapes)
     return pl.pallas_call(
         unpack_kernel,
         out_shape=tuple(jax.ShapeDtypeStruct(shape, f32) for shape in shapes) + (
-            jax.ShapeDtypeStruct((latents, own), f32), jax.ShapeDtypeStruct((width, own), f32)),
+            jax.ShapeDtypeStruct((latents, own), f32), jax.ShapeDtypeStruct((width, own), f32))
+        + (jax.ShapeDtypeStruct((own,), f32),) * 4,
         in_specs=[anywhere] * 2 + [vmem] * 2,
-        out_specs=(anywhere,) * (len(shapes) + 1) + (vmem,),
-        scratch_shapes=[pltpu.VMEM((pieces // 2, 2 * latents // pieces, own), f32), pltpu.SemaphoreType.DMA((count,))],
-        compiler_params=pltpu.CompilerParams(vmem_limit_bytes=16 * 2**20),
+        out_specs=(anywhere,) * len(shapes) + (vmem,) * 6,
+        scratch_shapes=[
+            pltpu.VMEM((size, own), f32), pltpu.VMEM((pieces, 2 * latents // pieces, own), f32), pltpu.VMEM((8, own), f32),
+            pltpu.SemaphoreType.DMA((count + 2,)), pltpu.SemaphoreType.DMA((count,)),
+        ],
+        compiler_params=pltpu.CompilerParams(vmem_limit_bytes=60 * 2**20),
         name="unpack_all",
-    )(mid, kv, latent_init, query_gain[:, None])
+    )(mid, kv, latent_init, query_gain)
 
 
 def unpack(packed, rows, columns):
@@ -986,9 +1061,9 @@
     latents, width = latent_init.shape
     hidden = w_up.shape[1]
     own = width // frames
-    kv, heard, log_total, query = cross_forward(frames, tokens, w_keyval, tok_gain, latent_init, query_gain, w_query)
-    mid, out_latents, d_heard, delta, d_latent, gains = middle(
-        frames, pieces, heard, skip, latent_init, grad_out, mlp_gain, self_gain, w_out, w_up, w_down, w_self_qkv, w_self_out
+    kv, log_total, query, mid, out_latents, d_heard, delta, d_latent, gains, _ = forward(
+        frames, pieces, tokens, skip, latent_init, tok_gain, query_gain, mlp_gain, self_gain,
+        w_query, w_keyval, w_out, w_up, w_down, w_self_qkv, w_self_out, grad_out,
     )
     mid_sum, kv_sum, token_grad = backward(
         frames, mid.reshape(2, pieces // 2, mid.shape[1], own), tokens, kv, d_heard, log_total, delta, query,
@@ -1005,7 +1080,9 @@
         (width, 2 * own),
     )
     if own % LANES == 0:
-        *sums, latent_grad, grad_query = unpack_all(mid_sum, kv_sum, latent_init, query_gain, shapes)
+        *sums, latent_grad, grad_query, gain_tok, gain_query, gain_mlp, gain_self = unpack_all(
+            mid_sum, kv_sum, latent_init, query_gain, shapes
+        )
     else:
         sums = cut(mid_sum, shapes[:5])
         keyval_sum, small = cut(kv_sum, (shapes[5], (2 * latents, own)))
@@ -1014,15 +1091,15 @@
         normed, _ = norm_down(latent_init.astype(jnp.float32).T)
         query_in = (normed * query_gain[:, None]).astype(jnp.bfloat16)
         grad_query = jnp.dot(query_in.astype(jnp.float32), small[:latents], precision=lax.Precision.HIGHEST)
-    gain_rows = kv_sum[0, -8:]
+        gain_mlp, gain_self, gain_tok, gain_query = [kv_sum[0, row - 8] for row in range(4)]
     return (
         out_latents,
         token_grad,
         latent_grad,
-        gain_rows[2],
-        gain_rows[3],
-        gain_rows[0],
-        gain_rows[1],
+        gain_tok,
+        gain_query,
+        gain_mlp,
+        gain_self,
         grad_query,
         sums[5],
         sums[0],

time: 337 us -> 293 us (0.87)
  Pallas kernels: 313 us -> 290 us
  local copies, waits for them, and re-layouts: 23.1 us -> 2.42 us
    pallas_call x2 -> x1, Pallas kernels: 114 us -> 90.6 us  [forward(): pl.pallas_call(functools.partial(forward_kernel, frames, 2 if items % 2 =...]
    unnamed x25 -> x6, local copies, waits for them, and re-layouts: 15.3 us -> 2.42 us
    pallas_call x1, Pallas kernels: 7.8 us -> 14.2 us  [unpack_all(): pl.pallas_call(unpack_kernel, out_shape=tuple((jax.ShapeDtypeStruct(shape...]
    broadcast_in_dim x5 -> x0, local copies, waits for them, and re-layouts: 6.35 us -> none  [the longest x1 1.63 us: backward(): query_gain[:, None]]
    pallas_call x1, Pallas kernels: 191 us -> 185 us  [backward(): pl.pallas_call(functools.partial(backward_kernel, chips, frames, spans),...]
where the time goes in v3:
time: 293 us
  Pallas kernels  290 us (99%)
    pallas_call x1, Pallas kernels, backward(): pl.pallas_call(functools.partial(backward_kernel, chips, frames, spans),...  185 us
    pallas_call x1, Pallas kernels, forward(): pl.pallas_call(functools.partial(forward_kernel, frames, 2 if items % 2 =...  90.6 us
    pallas_call x1, Pallas kernels, unpack_all(): pl.pallas_call(unpack_kernel, out_shape=tuple((jax.ShapeDtypeStruct(shape...  14.2 us

profile of v3, /device:TPU:0, one launch (start us, length us, event | category | flops | bytes accessed | tf_op | source)
XLA Modules:
  0.0 292.7 jit_solution(14001331767395382630)
XLA Ops:
  0.6 90.6 %forward.1 = (bf16[4,1536,512]{2,1,0:T(8,128)(2,1)}, f32[4,128,128]{2,1,0:T(8,128)}, bf16[128,768]{1,0:T(8,128)(2,1)}, f32[16,624,384]{2,1,0:T(8,128)}, bf16[4,6...) custom-call(bf16[4,512,768]{2,1,0:T(8,128)(2,1)} %tokens_ref.3, ...), custom_call_target="tpu_custom_call" | custom-call | tf_op jit(solution)/shard_map/forward/pallas_call | solution.py:454
  91.3 184.8 %backward.1 = (f32[2,8,624,384]{3,2,1,0:T(8,128)}, f32[2,8,120,384]{3,2,1,0:T(8,128)}, bf16[4,512,768]{2,1,0:T(8,128)(2,1)}) custom-call(f32[2,8,624,384]{3,2,1,0:T(8,128)} %bitcast.4, bf16[4,512,768]{2,1,0:T(8,128)(2,1)} %tokens_ref.3, bf16[4,1536,512]{2,1,0:T(8,128)(2,1)} %get-tuple-element.40.kv_ref, bf16[768,512]{1,0:T(8,128)(2,1)} %get-tuple-element.41.d_heard_ref, ...), custom_call_target="tpu_custom_call" | custom-call | tf_op jit(solution)/shard_map/backward/pallas_call | solution.py:935
  276.1 0.0 copy-start.1
  276.1 0.0 copy-start
  276.1 14.2 %unpack_all.1 = (f32[768,384]{1,0:T(8,128)}, f32[768,1536]{1,0:T(8,128)}, f32[3072,384]{1,0:T(8,128)}, f32[768,1152]{1,0:T(8,128)}, f32[768,384]{1,0:T(8,128)}, ...) custom-call(f32[16,624,384]{2,1,0:T(8,128)} %bitcast.3, ...), custom_call_target="tpu_custom_call" | custom-call | tf_op jit(solution)/shard_map/unpack_all/pallas_call | solution.py:1012
  290.3 0.0 copy-done.1
  290.3 0.7 copy.31
  291.0 0.0 copy-done
  291.0 1.7 copy.32
Async XLA Ops:
  276.1 14.2 %copy-start.1 = (bf16[4,64,768]{2,1,0:T(8,128)(2,1)S(1)}, bf16[4,64,768]{2,1,0:T(8,128)(2,1)}, u32[]{:S(2)}) copy-start(bf16[4,64,768]{2,1,0:T(8,128)(2,1)} %get-tuple-element.76) | copy-start | bytes 1179652
  276.1 14.9 %copy-start = (bf16[4,512,768]{2,1,0:T(8,128)(2,1)S(1)}, bf16[4,512,768]{2,1,0:T(8,128)(2,1)}, u32[]{:S(2)}) copy-start(bf16[4,512,768]{2,1,0:T(8,128)(2,1)} %get-tuple-element.77) | copy-start | bytes 9437188

commit v4 on v3

v4 whole, which is shorter than its diff:
```python
import functools

import jax
import jax.numpy as jnp
from jax import lax
from jax.experimental import pallas as pl
from jax.experimental.pallas import tpu as pltpu
from jax.sharding import PartitionSpec as P

MESH = pl.DeviceIdType.MESH
HEADS = 12
EPSILON = 1e-05
LANES = 128
BLOCK = 256


def nn(left, right):
    return lax.dot_general(left, right, (((1,), (0,)), ((), ())), preferred_element_type=jnp.float32)


def nt(left, right):
    return lax.dot_general(left, right, (((1,), (1,)), ((), ())), preferred_element_type=jnp.float32)


def norm_down(columns):
    centered = columns - jnp.mean(columns, axis=0, keepdims=True)
    inverse = lax.rsqrt(jnp.mean(centered * centered, axis=0, keepdims=True) + EPSILON)
    return centered * inverse, inverse


def gelu(value):
    slope = (2 / jnp.pi) ** 0.5
    tanh = jnp.tanh(value * (slope + (slope * 0.044715) * (value * value)))
    return value * (0.5 + 0.5 * tanh)


def norm_down_back(incoming, normed, inverse, gain):
    scaled = incoming * gain
    average = jnp.mean(scaled, axis=0, keepdims=True)
    along = jnp.mean(scaled * normed, axis=0, keepdims=True)
    return inverse * (scaled - average - normed * along)


def gain_columns(gain_ref):
    return jnp.broadcast_to(gain_ref[...].reshape(1, -1), (LANES, gain_ref.shape[0])).T


def loop(count, body):
    def step(index, carry):
        body(index)
        return carry

    lax.fori_loop(0, count, step, 0)


def window_at(index, size):
    return pl.ds(pl.multiple_of(index * size, size), size)


def forward_kernel(
    frames, groups,
    tokens_ref, skip_ref, latent_ref, tok_gain_ref, query_gain_ref, mlp_gain_ref, self_gain_ref,
    w_query_ref, w_keyval_ref, w_out_ref, w_up_ref, w_down_ref, w_qkv_ref, w_self_ref, grad_ref,
    kv_out, log_out, query_out, mid_out, latents_out, act_out, hidden_out, mlp_out, cross_out, after_out, cot_out, heard_out,
    heard_f32_out, d_triple_out, arrived,
    tokens, tok_in, queries, sent, got,
    w_out, w_out_t, w_self, w_self_t, w_qkv, tall, up_down, down_up,
    heard, cross, mlp_in, act, hidden_rows, after, self_in, triple, mixed, cotangent, d_mixed, d_triple, heard_f32, turned,
    tok_gain, mlp_gain, self_gain, stage,
    tok_sem, kv_sem, y_send, y_recv, w_sem, stage_sem, got_sem, save_sem,
):
    items, rows, width = tokens_ref.shape
    latents = latent_ref.shape[0]
    hidden = w_up_ref.shape[1]
    head = width // HEADS
    factor = head ** -0.5
    own = width // frames
    stat = sent.shape[1] - width
    pieces = mid_out.shape[0]
    item = lax.axis_index("items")
    frame = lax.axis_index("frames")

    barrier = pltpu.get_barrier_semaphore()
    for hop in range(1, frames):
        pl.semaphore_signal(barrier, inc=1, device_id=(item, lax.rem(frame + hop, frames)), device_id_type=MESH)

    wide = 2 * width
    load_query = pltpu.make_async_copy(w_query_ref, w_self_t, w_sem.at[0])
    load_keyval = pltpu.make_async_copy(w_keyval_ref, down_up.at[:, pl.ds(0, wide)], w_sem.at[1])
    load_self = pltpu.make_async_copy(w_self_ref, w_self, w_sem.at[2])
    load_out = pltpu.make_async_copy(w_out_ref, w_out, w_sem.at[3])
    load_qkv = pltpu.make_async_copy(w_qkv_ref, w_qkv, w_sem.at[4])
    load_up = pltpu.make_async_copy(w_up_ref, down_up, w_sem.at[5])

    def load_tokens(i):
        return pltpu.make_async_copy(tokens_ref.at[i], tokens.at[lax.rem(i, 2)], tok_sem.at[lax.rem(i, 2)])

    def load_down(part):
        return pltpu.make_async_copy(w_down_ref.at[pl.ds(part * rows, rows), :], tokens.at[part % 2], tok_sem.at[part % 2])

    def kv_at(i):
        return pl.ds(pl.multiple_of(lax.rem(i, 2) * wide, wide), wide)

    def save_kv(i):
        return pltpu.make_async_copy(act.at[kv_at(i), pl.ds(0, rows)], kv_out.at[i], kv_sem.at[lax.rem(i, 2)])

    def across(i, hop):
        return pltpu.make_async_remote_copy(
            src_ref=sent.at[i], dst_ref=(arrived if frames > 2 else got).at[hop - 1, i], send_sem=y_send.at[hop - 1, i], recv_sem=y_recv.at[hop - 1, i],
            device_id=(item, lax.rem(frame + hop, frames)), device_id_type=MESH,
        )

    load_tokens(0).start()
    load_query.start()
    load_keyval.start()
    load_tokens(1).start()
    for copy in (load_self, load_out, load_qkv):
        copy.start()

    latent_t = latent_ref[...].astype(jnp.float32).T
    query_normed, _ = norm_down(latent_t)
    query_in = (query_normed * gain_columns(query_gain_ref)).T.astype(jnp.bfloat16)
    tok_gain[...] = gain_columns(tok_gain_ref)
    mlp_gain[...] = gain_columns(mlp_gain_ref)
    self_gain[...] = gain_columns(self_gain_ref)
    load_query.wait()
    query = nn(query_in, w_self_t[...]).astype(jnp.bfloat16)
    query_out[...] = query
    scaled = query * jnp.bfloat16(factor)
    for h in range(HEADS):
        queries[h] = scaled[:, h * head : (h + 1) * head]
    load_keyval.wait()
    for block in range(wide // BLOCK):
        window = pl.ds(block * BLOCK, BLOCK)
        tall[window, :] = down_up[:, window].T
    load_up.start()
    pl.semaphore_wait(barrier, frames - 1)

    def heard_item(i):
        slot = lax.rem(i, 2)
        load_tokens(i).wait()

        def norm_block(b):
            window = window_at(b, LANES)
            normed, _ = norm_down(tokens[slot, window, :].T.astype(jnp.float32))
            tok_in[:, window] = (normed * tok_gain[...]).astype(jnp.bfloat16)

        loop(rows // LANES, norm_block)

        @pl.when(i + 2 < items)
        def _():
            load_tokens(i + 2).start()

        @pl.when(i >= 2)
        def _():
            save_kv(i - 2).wait()

        base = pl.multiple_of(slot * wide, wide)
        for block in range(wide // BLOCK):
            act[pl.ds(base + block * BLOCK, BLOCK), pl.ds(0, rows)] = nn(
                tall[pl.ds(block * BLOCK, BLOCK), :], tok_in[...]
            ).astype(jnp.bfloat16)
        save_kv(i).start()
        lane = lax.broadcasted_iota(jnp.int32, (latents, LANES), 1)
        stats = jnp.zeros((latents, LANES), jnp.float32)
        for h in range(HEADS):
            scores = nn(queries[h], act[pl.ds(base + h * head, head), pl.ds(0, rows)])
            most = jnp.max(scores, axis=-1, keepdims=True)
            shifted = jnp.exp(scores - most)
            total = jnp.sum(shifted, axis=-1, keepdims=True)
            stats = jnp.where(lane == h, most, stats)
            stats = jnp.where(lane == h + stat // 2, total, stats)
            sent[i, pl.ds(h * head, head), :] = nt(
                act[pl.ds(base + width + h * head, head), pl.ds(0, rows)], shifted.astype(jnp.bfloat16)
            )
        sent[i, pl.ds(width, stat), :] = stats.T[:stat]
        for hop in range(1, frames):
            across(i, hop).start()

    loop(items, heard_item)
    load_down(0).start()
    load_down(1).start()

    def turn(source, target, count):
        def block(b):
            window = window_at(b, BLOCK)
            target[window, :] = source[:, window].T

        loop(count // BLOCK, block)

    load_self.wait()

    def load_cotangent(i):
        cotangent[:, window_at(i, latents)] = grad_ref[i].T

    loop(items, load_cotangent)
    for block in range(width // BLOCK):
        window = pl.ds(block * BLOCK, BLOCK)
        d_mixed[window, :] = nn(w_self[window, :], cotangent[...]).astype(jnp.bfloat16)
    turn(w_self, w_self_t, width)
    load_out.wait()
    turn(w_out, w_out_t, width)
    load_up.wait()
    turn(down_up, up_down, hidden)
    for part in range(hidden // rows):
        load_down(part).wait()
        for block in range(rows // BLOCK):
            down_up[:, pl.ds(part * rows + block * BLOCK, BLOCK)] = tokens[part % 2, pl.ds(block * BLOCK, BLOCK), :].T
        if part + 2 < hidden // rows:
            load_down(part + 2).start()
    load_qkv.wait()
    turn(w_qkv, tall, 3 * width)
    for i in range(max(items - 2, 0), items):
        save_kv(i).wait()

    def combine(i):
        for hop in range(1, frames):
            across(i, hop).wait_send()
            across(i, hop).wait_recv()
            if frames > 2:
                near = pltpu.make_async_copy(arrived.at[hop - 1, i], got.at[hop - 1, 0], got_sem)
                near.start()
                near.wait()
        parts = [sent.at[i]] + [got.at[hop, 0 if frames > 2 else i] for hop in range(frames - 1)]
        highs = [part[pl.ds(width, stat // 2), :] for part in parts]
        sums = [part[pl.ds(width + stat // 2, stat // 2), :] for part in parts]
        most = functools.reduce(jnp.maximum, highs)
        total = functools.reduce(jnp.add, [low * jnp.exp(high - most) for high, low in zip(highs, sums)])
        log_total = most + jnp.log(total)
        scales = [jnp.exp(high - log_total) for high in highs]
        for h in range(HEADS):
            window = pl.ds(h * head, head)
            together = functools.reduce(
                jnp.add, [part[window, :] * scale[h : h + 1] for part, scale in zip(parts, scales)]
            )
            heard_f32[window, window_at(i, latents)] = together
            heard[window, window_at(i, latents)] = together.astype(jnp.bfloat16)
        padded = jnp.concatenate([log_total, jnp.zeros((LANES - stat // 2, latents), jnp.float32)], axis=0)
        log_out[i] = padded.T

    def attend(i):
        window = window_at(i, latents)
        for first in range(0, HEADS, 4):
            at = [[pl.ds(third * width + h * head, head) for third in range(3)] for h in range(first, first + 4)]
            query = [triple[where[0], window] * jnp.bfloat16(factor) for where in at]
            key = [triple[where[1], window] for where in at]
            value = [triple[where[2], window] for where in at]
            d_mix = [d_mixed[where[0], window] for where in at]
            scores = [nn(k.T, q) for k, q in zip(key, query)]
            d_probs = [nn(v.T, d) for v, d in zip(value, d_mix)]
            shifted = [jnp.exp(s - jnp.max(s, axis=0, keepdims=True)) for s in scores]
            probs = [s * (1.0 / jnp.sum(s, axis=0, keepdims=True)) for s in shifted]
            low = [p.astype(jnp.bfloat16) for p in probs]
            mix = [nn(v, p) for v, p in zip(value, low)]
            delta = [jnp.sum(d.astype(jnp.float32) * m, axis=0, keepdims=True) for d, m in zip(d_mix, mix)]
            d_scores = [(p * (d - x)).astype(jnp.bfloat16) for p, d, x in zip(probs, d_probs, delta)]
            d_query = [nn(k, d) * factor for k, d in zip(key, d_scores)]
            d_key = [nt(q, d) for q, d in zip(query, d_scores)]
            d_value = [nt(d, p) for d, p in zip(d_mix, low)]
            for where, m, dq, dk, dv in zip(at, mix, d_query, d_key, d_value):
                mixed[where[0], window] = m.astype(jnp.bfloat16)
                d_triple[where[0], window] = dq.astype(jnp.bfloat16)
                d_triple[where[1], window] = dk.astype(jnp.bfloat16)
                d_triple[where[2], window] = dv.astype(jnp.bfloat16)

    def forward_group(group):
        size = items // groups
        first = group * size
        columns = pl.ds(first * latents, size * latents)

        def each_item(body):
            loop(size, lambda i: body(first + i))

        def each_block(count, body):
            loop(count // BLOCK, lambda b: body(window_at(b, BLOCK)))

        each_item(combine)

        def out_block(window):
            cross[window, columns] = nn(w_out_t[window, :], heard[:, columns])

        each_block(width, out_block)

        def cross_item(i):
            window = window_at(i, latents)
            keep = (1 - skip_ref[i]).astype(jnp.float32)
            total = latent_ref[...].astype(jnp.float32).T + keep * cross[:, window]
            cross[:, window] = total
            normed, _ = norm_down(total)
            mlp_in[:, window] = (normed * mlp_gain[...]).astype(jnp.bfloat16)

        each_item(cross_item)

        def up_block(window):
            value = nn(up_down[window, :], mlp_in[:, columns])
            hidden_rows[window, columns] = value
            act[window, columns] = gelu(value).astype(jnp.bfloat16)

        each_block(hidden, up_block)
        if group == groups - 1:
            for at in range(5):
                saves[at].start()

        def down_block(window):
            after[window, columns] = cross[window, columns] + nn(down_up[window, :], act[:, columns])

        each_block(width, down_block)
        if group == groups - 1:
            saves[5].start()

        def after_item(i):
            window = window_at(i, latents)
            normed, _ = norm_down(after[:, window])
            self_in[:, window] = (normed * self_gain[...]).astype(jnp.bfloat16)

        each_item(after_item)

        def triple_block(window):
            triple[window, columns] = nn(tall[window, :], self_in[:, columns]).astype(jnp.bfloat16)

        each_block(3 * width, triple_block)
        each_item(attend)

    saves = [
        pltpu.make_async_copy(source, target, save_sem.at[at])
        for at, (source, target) in enumerate(
            (
                (hidden_rows, hidden_out), (act.at[:, pl.ds(0, items * latents)], act_out), (mlp_in, mlp_out), (cross, cross_out),
                (heard_f32, heard_f32_out), (after, after_out), (heard, heard_out), (cotangent, cot_out), (d_triple, d_triple_out),
            )
        )
    ]
    saves[7].start()
    for group in range(groups):
        forward_group(group)
    saves[8].start()
    saves[6].start()

    pending = {}

    def put(first_piece, count, offset, left, right):
        size = width // count
        slot = len(pending) % stage.shape[0]
        for key in [key for key in pending if key % stage.shape[0] == slot and pending[key] is not None]:
            pending[key].wait()
            pending[key] = None
        view = stage.at[slot]
        view[...] = nt(left[...], right[...])
        copy = pltpu.make_async_copy(
            view.reshape(count, size, own), mid_out.at[pl.ds(first_piece, count), pl.ds(offset, size)], stage_sem.at[slot]
        )
        copy.start()
        pending[len(pending)] = copy

    size = width // pieces
    my_columns = pl.multiple_of(frame * own, own)
    for third in range(3):
        put(0, pieces, third * size, self_in, d_triple.at[pl.ds(3 * my_columns + third * own, own), :])
    put(0, pieces, 3 * size, mixed, cotangent.at[pl.ds(my_columns, own), :])

    share = latents // frames

    def latents_item(i):
        window = window_at(i, latents)
        for block in range(width // BLOCK):
            piece = pl.ds(block * BLOCK, BLOCK)
            turned[:, piece] = (after[piece, window] + nn(w_self_t[piece, :], mixed[:, window])).T
        latents_out[i] = turned[pl.ds(pl.multiple_of(frame * share, share), share), :].astype(jnp.bfloat16)

    loop(items, latents_item)
    for copy in saves:
        copy.wait()
    for copy in pending.values():
        if copy is not None:
            copy.wait()


def forward(
    frames, pieces, tokens, skip, latent_init, tok_gain, query_gain, mlp_gain, self_gain,
    w_query, w_keyval, w_out, w_up, w_down, w_self_qkv, w_self_out, grad_out,
):
    items, rows, width = tokens.shape
    latents = latent_init.shape[0]
    hidden = w_up.shape[1]
    own = width // frames
    columns = items * latents
    mid_rows = 4 * width // pieces
    bf16, f32 = jnp.bfloat16, jnp.float32
    vmem = pl.BlockSpec(memory_space=pltpu.VMEM)
    anywhere = pl.BlockSpec(memory_space=pl.ANY)
    dma = pltpu.SemaphoreType.DMA
    peers = max(frames - 1, 1)
    return pl.pallas_call(
        functools.partial(forward_kernel, frames, 2 if items % 2 == 0 else 1),
        out_shape=(
            jax.ShapeDtypeStruct((items, 2 * width, rows), bf16),
            jax.ShapeDtypeStruct((items, latents, LANES), f32),
            jax.ShapeDtypeStruct((latents, width), bf16),
            jax.ShapeDtypeStruct((pieces, mid_rows, own), f32),
            jax.ShapeDtypeStruct((items, latents // frames, width), bf16),
            jax.ShapeDtypeStruct((hidden, columns), bf16),
            jax.ShapeDtypeStruct((hidden, columns), f32),
            jax.ShapeDtypeStruct((width, columns), bf16),
            jax.ShapeDtypeStruct((width, columns), f32),
            jax.ShapeDtypeStruct((width, columns), f32),
            jax.ShapeDtypeStruct((width, columns), bf16),
            jax.ShapeDtypeStruct((width, columns), bf16),
            jax.ShapeDtypeStruct((width, columns), f32),
            jax.ShapeDtypeStruct((3 * width, columns), bf16),
            jax.ShapeDtypeStruct((peers, items if frames > 2 else 1, width + 32, latents), f32),
        ),
        in_specs=[anywhere, pl.BlockSpec(memory_space=pltpu.SMEM)] + [vmem] * 5 + [anywhere] * 7 + [vmem],
        out_specs=(anywhere, vmem, vmem, anywhere, vmem) + (anywhere,) * 10,
        scratch_shapes=[
            pltpu.VMEM((2, rows, width), bf16),
            pltpu.VMEM((width, rows), bf16),
            pltpu.VMEM((HEADS, latents, width // HEADS), bf16),
            pltpu.VMEM((items, width + 32, latents), f32),
            pltpu.VMEM((peers, 1 if frames > 2 else items, width + 32, latents), f32),
        ]
        + [pltpu.VMEM((width, width), bf16)] * 4
        + [
            pltpu.VMEM((width, 3 * width), bf16),
            pltpu.VMEM((3 * width, width), bf16),
            pltpu.VMEM((hidden, width), bf16),
            pltpu.VMEM((width, hidden), bf16),
            pltpu.VMEM((width, columns), bf16),
            pltpu.VMEM((width, columns), f32),
            pltpu.VMEM((width, columns), bf16),
            pltpu.VMEM((hidden, max(columns, rows)), bf16),
            pltpu.VMEM((hidden, columns), f32),
            pltpu.VMEM((width, columns), f32),
            pltpu.VMEM((width, columns), bf16),
            pltpu.VMEM((hidden, columns), bf16),
            pltpu.VMEM((width, columns), bf16),
            pltpu.VMEM((width, columns), bf16),
            pltpu.VMEM((width, columns), bf16),
            pltpu.VMEM((3 * width, columns), bf16),
            pltpu.VMEM((width, columns), f32),
            pltpu.VMEM((latents, width), f32),
            pltpu.VMEM((width, LANES), f32),
            pltpu.VMEM((width, LANES), f32),
            pltpu.VMEM((width, LANES), f32),
            pltpu.VMEM((2, width, own), f32),
            dma((2,)), dma((2,)), dma((peers, items)), dma((peers, items)), dma((8,)), dma((2,)), dma, dma((9,)),
        ],
        compiler_params=pltpu.CompilerParams(collective_id=1, has_side_effects=True, vmem_limit_bytes=62 * 2**20),
        name="forward",
    )(
        tokens, skip, latent_init, tok_gain, query_gain, mlp_gain, self_gain,
        w_query, w_keyval, w_out, w_up, w_down, w_self_qkv, w_self_out, grad_out,
    )


def add_into(target, parts, rows):
    step = next(size for size in (96, 80, 64, 60, 48, 40, 24, 16, 8) if rows % size == 0 and size % 8 == 0)

    def body(index):
        window = window_at(index, step)
        total = parts[0][window]
        for part in parts[1:]:
            total = total + part[window]
        target[window] = total

    loop(rows // step, body)


def gelu_slope(value):
    slope = (2 / jnp.pi) ** 0.5
    square = value * value
    tanh = jnp.tanh(value * (slope + (slope * 0.044715) * square))
    half = 0.5 + 0.5 * tanh
    bend = value * (2 * slope + (6 * slope * 0.044715) * square)
    return half + half * (1.0 - half) * bend


def nn_exact(left, right):
    total = jnp.zeros((left.shape[0], right.shape[1]), jnp.float32)
    rest = right
    for _ in range(3):
        part = rest.astype(jnp.bfloat16)
        total = total + nn(left, part)
        rest = rest - part.astype(jnp.float32)
    return total


def backward_kernel(
    chips, frames, streams,
    loc_a, tokens_ref, kv_ref, act_ref, hidden_ref, mlp_ref, cross_ref, after_ref, cot_ref, heard_ref, heard_f32_ref, dtri_ref,
    w_qkv_ref, w_up_ref, w_down_ref, w_out_ref, w_keyval_ref, w_query_ref,
    skip_ref, log_ref, query_ref, latent_ref, tok_gain_ref, query_gain_ref, mlp_gain_ref, self_gain_ref,
    *rest,
):
    outs, rest = rest[:12], rest[12:]
    sums, token_out, (loc_b, loc_c, loc_d), sibs = outs[:4], outs[4], outs[5:8], outs[8:12]
    locs = (loc_a, loc_b, loc_c, loc_d)
    (
        flat, tall, w_square, act, pool, mlp_in, heard, cotangent, branch, d_heard, queries, queries_t, token_stage,
        hidden_stage, after, cross, rows_f32, incoming, stage, small_stage, d_query, gain_sum, tok_gain, mlp_gain, self_gain,
        d_latent, gain_cols, delta, inverse, y_mine, y_sib, ky,
    ), rest = rest[:32], rest[32:]
    n = len(streams)
    mines, sib_slots, rxs = rest[:n], rest[n : 2 * n], rest[2 * n : 3 * n]
    (
        pair_send, pair_recv, ld_sem, ls_sem, rs_send, rs_recv, ag_send, ag_recv, share_send, share_recv, own_sem,
        kpair_send, kpair_recv, y_send, y_recv, y_sem, in_sem, tok_sem, kv_sem, out_sem, hidden_sem, stage_sem, small_sem,
    ) = rest[3 * n :]

    item_index = lax.axis_index("items")
    frame = lax.axis_index("frames")
    core = lax.rem(item_index, 2)
    chip = item_index // 2
    column = lax.rem(chip, 2)
    line = chip // 2
    place = line + column * (chips - 1 - 2 * line)
    way = 1 - 2 * core
    count, rows, width = tokens_ref.shape
    latents = latent_ref.shape[0]
    hidden = hidden_ref.shape[0]
    head = width // HEADS
    factor = head ** -0.5
    own = width // frames
    pieces = 2 * chips
    per_piece = width // pieces
    kv_rows = loc_d.shape[3]
    last = n - 1

    def device_at(position):
        position = lax.rem(position + 2 * chips, chips)
        far = position // (chips // 2)
        return (2 * (position + far * (chips - 1 - 2 * position)) + far) * 2 + core

    right, left = device_at(place + way), device_at(place - way)
    sibling = item_index + way

    def chunk(offset):
        return lax.rem(place + way * offset + 4 * chips, chips)

    def sib_chunk(offset):
        return lax.rem(place - way * offset + 4 * chips, chips)

    barrier = pltpu.get_barrier_semaphore()
    for peer in (left, right, sibling):
        pl.semaphore_signal(barrier, inc=1, device_id=(peer, frame), device_id_type=MESH)
    for hop in range(1, frames):
        pl.semaphore_signal(barrier, inc=1, device_id=(item_index, lax.rem(frame + hop, frames)), device_id_type=MESH)

    def remote(src, dst, send, recv, peer):
        return pltpu.make_async_remote_copy(
            src_ref=src, dst_ref=dst, send_sem=send, recv_sem=recv, device_id=peer, device_id_type=MESH
        )

    def pair(source, k):
        return remote(
            locs[source].at[1 - core, k], sibs[source].at[k], pair_send.at[source, k], pair_recv.at[source, k], (sibling, frame)
        )

    def frame_at(hop):
        return lax.rem(frame + hop, frames)

    def pair_frame(hop, k):
        f = frame_at(hop)
        return remote(
            loc_d.at[f, 1 - core, k], sibs[3].at[f, k], kpair_send.at[hop - 1, k], kpair_recv.at[hop - 1, k], (sibling, frame)
        )

    def start_pairs(source):
        loop(chips, lambda index: pair(source, sib_chunk(-index)).start())

    def part_of(j):
        source, start, size = streams[j]
        return source, pl.ds(start, size)

    def load_mine(j, k, slot):
        source, part = part_of(j)
        src = loc_d.at[frame, core, k, part] if source == 3 else locs[source].at[core, k, part]
        return pltpu.make_async_copy(src, mines[j].at[slot], ld_sem.at[j, slot])

    def load_sib(j, k, slot):
        source, part = part_of(j)
        src = sibs[3].at[frame, k, part] if source == 3 else sibs[source].at[k, part]
        return pltpu.make_async_copy(src, sib_slots[j].at[slot], ls_sem.at[j, slot])

    def ring(j, k, slot):
        return remote(mines[j].at[slot], rxs[j].at[k], rs_send.at[j, slot], rs_recv.at[j, k], (right, frame))

    def own_at(j, k):
        source, part = part_of(j)
        return sums[source].at[core, k, part]

    def gather(j, k, src):
        return remote(src, own_at(j, k), ag_send.at[j, k], ag_recv.at[j, k], (right, frame))

    def share(j, k, src):
        return remote(src, own_at(j, k), share_send.at[j, k], share_recv.at[j, k], (sibling, frame))

    def share_from(j, k):
        source, part = part_of(j)
        return remote(mines[j].at[0], sums[source].at[1 - core, k, part], share_send.at[j, k], share_recv.at[j, k], (sibling, frame))

    def keep(j, k, slot):
        return pltpu.make_async_copy(mines[j].at[slot], own_at(j, k), own_sem.at[j])

    def across(hop, k):
        other = lax.rem(frame + hop, frames)
        return remote(y_mine.at[k], ky.at[hop - 1, k], y_send.at[hop - 1, k], y_recv.at[hop - 1, k], (item_index, other))

    def prefetch(j, op):
        k, slot = chunk(-op), lax.rem(op, 2)
        source, part = part_of(j)
        if source < 3 and (j == 0 or streams[j - 1][0] != source):
            pair(source, k).wait_recv()
        load_mine(j, k, slot).start()
        load_sib(j, k, slot).start()

    def when(condition, body):
        if isinstance(condition, (bool, int)):
            if condition:
                body()
        else:
            pl.when(condition)(body)

    def tick(j, op):
        source, part = part_of(j)
        size = streams[j][2]
        slot = lax.rem(op, 2)

        def reduce_op():
            k = chunk(-op)
            load_mine(j, k, slot).wait()
            load_sib(j, k, slot).wait()
            parts = [mines[j].at[slot], sib_slots[j].at[slot]]
            if source == 3:
                for hop in range(1, frames):
                    across(hop, k).wait_recv()
                    parts.append(ky.at[hop - 1, k])
            if not (isinstance(op, int) and op == 0):
                ring(j, k, slot).wait_recv()
                parts.append(rxs[j].at[k])
            add_into(mines[j].at[slot], parts, size)

            def pass_on():
                ring(j, k, slot).start()
                if isinstance(op, int) and op == 0:
                    prefetch(j, op + 1)
                else:
                    ring(j, k, 1 - slot).wait_send()
                    prefetch(j, op + 1)

            def finish():
                gather(j, k, mines[j].at[slot]).start()
                share(j, k, mines[j].at[slot]).start()
                keep(j, k, slot).start()

            when(op < chips - 1, pass_on)
            when(op == chips - 1, finish)

        def gather_op():
            k = chunk(-op)
            gather(j, k, mines[j].at[0]).wait_recv()

            def forward_on():
                gather(j, k, own_at(j, k)).start()

            when(op < 2 * chips - 2, forward_on)
            share(j, k, own_at(j, k)).start()

        when(op < chips, reduce_op)
        when((op >= chips) & (op < 2 * chips - 1) if not isinstance(op, int) else chips <= op < 2 * chips - 1, gather_op)

    third = 3 * width
    names = [
        (dtri_ref, pool.at[pl.ds(hidden, third), :]),
        (w_qkv_ref, flat.at[:, pl.ds(0, third)]),
        (after_ref, after),
        (cot_ref, cotangent),
        (act_ref, act),
        (w_down_ref, tall),
        (mlp_ref, mlp_in),
        (cross_ref, cross),
        (heard_ref, heard),
        (w_out_ref, w_square),
        (w_up_ref, flat),
        (heard_f32_ref, cross),
        (w_query_ref, w_square),
        (w_keyval_ref.at[:, pl.ds(0, width)], tall.at[pl.ds(2 * rows, width), :]),
        (w_keyval_ref.at[:, pl.ds(width, width)], tall.at[pl.ds(2 * rows + width, width), :]),
    ]
    copies = [pltpu.make_async_copy(src, dst, in_sem.at[at]) for at, (src, dst) in enumerate(names)]
    (
        get_dtri, get_qkv, get_after, get_cot, get_act, get_down, get_mlp, get_cross, get_heard, get_out, get_up, get_heard_f32,
        get_query, get_keys, get_values,
    ) = copies

    def load_hidden(b):
        slot = lax.rem(b, 4)
        return pltpu.make_async_copy(hidden_ref.at[window_at(b, BLOCK), :], hidden_stage.at[slot], hidden_sem.at[slot])

    def tok_load(i):
        slot = lax.rem(i, 2)
        return pltpu.make_async_copy(tokens_ref.at[i], tall.at[window_at(slot, rows), :], tok_sem.at[slot])

    def kv_load(i):
        slot = lax.rem(i, 2)
        return pltpu.make_async_copy(kv_ref.at[i], act.at[window_at(slot, 2 * width), pl.ds(0, rows)], kv_sem.at[slot])

    def token_save(i, b):
        slot = lax.rem(b, 2)
        return pltpu.make_async_copy(token_stage.at[slot], token_out.at[i, window_at(b, LANES), :], out_sem.at[slot])

    for copy in (get_dtri, get_qkv, get_after, get_cot, get_act, get_down, get_mlp, get_cross, get_heard, get_out):
        copy.start()
    for b in range(3):
        load_hidden(b).start()
    pl.semaphore_wait(barrier, 3 + frames - 1)
    start_pairs(0)
    tok_gain[...] = gain_columns(tok_gain_ref)
    mlp_gain[...] = gain_columns(mlp_gain_ref)
    self_gain[...] = gain_columns(self_gain_ref)
    scaled = query_ref[...] * jnp.bfloat16(factor)
    for h in range(HEADS):
        queries[h] = scaled[:, h * head : (h + 1) * head]
    queries_t[...] = scaled.T
    d_query[...] = jnp.zeros_like(d_query)
    gain_sum[...] = jnp.zeros_like(gain_sum)
    gain_cols[...] = jnp.zeros_like(gain_cols)
    d_latent[...] = jnp.zeros_like(d_latent)
    prefetch(0, 0)

    done = [0] * n

    def advance(*which):
        for j in which:
            if done[j] < 2 * chips - 1:
                tick(j, done[j])
                done[j] += 1

    def each_item(body):
        loop(count, lambda i: body(i, window_at(i, latents)))

    def each_block(first, total, body):
        loop(total // BLOCK, lambda b: body(b + first, window_at(b + first, BLOCK)))

    pending = {}

    def put(target, left, right):
        slot = len(pending) % stage.shape[0]
        for key in [key for key in pending if key % stage.shape[0] == slot and pending[key] is not None]:
            pending[key].wait()
            pending[key] = None
        view = stage.at[slot]
        view[...] = nt(left[...], right[...])
        put_start(target, slot)

    def put_start(target, slot):
        copy = pltpu.make_async_copy(stage.at[slot].reshape(*target.shape), target, stage_sem.at[slot])
        copy.start()
        pending[len(pending)] = copy

    def put_done():
        for key in pending:
            if pending[key] is not None:
                pending[key].wait()
                pending[key] = None

    my_columns = pl.multiple_of(frame * own, own)
    lane = lax.broadcasted_iota(jnp.int32, (width, LANES), 1)

    get_dtri.wait()
    get_qkv.wait()
    advance(0)

    def self_block(b, window):
        incoming[window, :] = nn(flat[window, pl.ds(0, third)], pool[pl.ds(hidden, third), :])

    each_block(0, width, self_block)
    get_up.start()
    get_after.wait()
    get_cot.wait()

    def self_back(i, window):
        normed, inverse_row = norm_down(after[:, window])
        arriving = incoming[:, window]
        gain_cols[...] += jnp.where(lane == 1, jnp.sum(arriving * normed, axis=-1, keepdims=True), 0.0)
        d_after = cotangent[:, window].astype(jnp.float32) + norm_down_back(arriving, normed, inverse_row, self_gain[...])
        branch[:, window] = d_after.astype(jnp.bfloat16)
        rows_f32[:, window] = d_after

    each_item(self_back)
    advance(0)
    get_act.wait()
    groups = hidden // width
    for group in range(groups):
        size = hidden // pieces
        span = pieces // groups
        target = loc_b.at[group * span // chips, pl.ds(group * span % chips, span)] if span <= chips else None
        put(target, act.at[pl.ds(group * width, width), :], branch.at[pl.ds(my_columns, own), :])
    put_done()
    start_pairs(1)
    kv_load(0).start()
    get_down.wait()

    def hidden_block(b, window):
        load_hidden(b).wait()

        @pl.when(b + 3 < hidden // BLOCK)
        def _():
            load_hidden(b + 3).start()

        d_act = nn(tall[window, :], branch[...])
        pool[window, :] = (d_act * gelu_slope(hidden_stage[lax.rem(b, 4)])).astype(jnp.bfloat16)

    half = hidden // BLOCK // 2
    each_block(0, half * BLOCK, hidden_block)
    advance(0)
    prefetch(1, 0)
    each_block(half, hidden - half * BLOCK, hidden_block)
    advance(1)
    tok_load(0).start()
    get_keys.start()
    get_values.start()
    get_mlp.wait()
    advance(0)
    for part in range(groups):
        source = pool.at[pl.ds(frame * (hidden // frames) + part * own, own), :]
        put(loc_c.at[:, :, pl.ds(part * per_piece, per_piece)], mlp_in, source)
        if part == groups // 2 - 1:
            advance(1)
    get_up.wait()
    advance(0)

    def mlp_block(b, window):
        incoming[window, :] = nn(flat[window, :], pool[pl.ds(0, hidden), :])

    each_block(0, width, mlp_block)
    get_cross.wait()
    advance(1)

    def mlp_back(i, window):
        normed, inverse_row = norm_down(cross[:, window])
        arriving = incoming[:, window]
        gain_cols[...] += jnp.where(lane == 0, jnp.sum(arriving * normed, axis=-1, keepdims=True), 0.0)
        d_cross = rows_f32[:, window] + norm_down_back(arriving, normed, inverse_row, mlp_gain[...])
        d_latent[...] += d_cross.T
        keep_item = (1 - skip_ref[i]).astype(jnp.float32)
        branch[:, window] = (keep_item * d_cross).astype(jnp.bfloat16)

    each_item(mlp_back)
    get_heard_f32.start()
    get_heard.wait()
    advance(0)
    put(loc_c.at[:, :, pl.ds(groups * per_piece, per_piece)], heard, branch.at[pl.ds(my_columns, own), :])
    put_done()
    start_pairs(2)
    get_out.wait()

    def heard_block(b, window):
        d_heard[window, :] = nn(w_square[window, :], branch[...]).astype(jnp.bfloat16)

    each_block(0, width, heard_block)
    get_query.start()
    get_heard_f32.wait()
    advance(1)

    def delta_item(i, window):
        product = d_heard[:, window].astype(jnp.float32) * cross[:, window]
        sums_of = jnp.sum(product.reshape(HEADS, head, latents), axis=1)
        padded = jnp.concatenate([sums_of, jnp.zeros((LANES - HEADS, latents), jnp.float32)], axis=0)
        delta[i] = padded.T

    each_item(delta_item)
    prefetch(2, 0)
    get_keys.wait()
    get_values.wait()
    advance(0, 2)

    def attend(i, heads):
        base = pl.multiple_of(lax.rem(i, 2) * 2 * width, 2 * width)
        target = pl.multiple_of(i * 2 * width, 2 * width)
        latent_window = window_at(i, latents)
        for h in heads:
            keys_at = pl.ds(h * head, head)
            keys = act[pl.ds(base + h * head, head), pl.ds(0, rows)]
            values = act[pl.ds(base + width + h * head, head), pl.ds(0, rows)]
            d_heard_t = d_heard[keys_at, latent_window]
            probs = jnp.exp(nn(queries[h], keys) - log_ref[i, :, h : h + 1])
            d_probs = nn(d_heard_t.T, values)
            d_scores = (probs * (d_probs - delta[i, :, h : h + 1])).astype(jnp.bfloat16)
            pool[pl.ds(target + h * head, head), pl.ds(0, rows)] = nn(queries_t[keys_at, :], d_scores).astype(jnp.bfloat16)
            pool[pl.ds(target + width + h * head, head), pl.ds(0, rows)] = nn(d_heard_t, probs.astype(jnp.bfloat16)).astype(
                jnp.bfloat16
            )
            d_query[keys_at, :] += nt(keys, d_scores)

    def norm_tokens(i):
        tok_load(i).wait()
        base = pl.multiple_of(lax.rem(i, 2) * rows, rows)

        def norm_block(b):
            window = window_at(b, LANES)
            columns = tall[pl.ds(base + b * LANES, LANES), :].T.astype(jnp.float32)
            block, inverse_row = norm_down(columns)
            after[:, window] = block
            inverse[:, window] = jnp.broadcast_to(inverse_row, (8, LANES))
            flat[:, pl.ds(pl.multiple_of(i * rows + b * LANES, LANES), LANES)] = (block * tok_gain[...]).astype(jnp.bfloat16)

        loop(rows // LANES, norm_block)

    def token_back(i):
        base = pl.multiple_of(i * 2 * width, 2 * width)

        def product(b):
            window = window_at(b, BLOCK)
            keys_w = tall[pl.ds(pl.multiple_of(2 * rows + b * BLOCK, BLOCK), BLOCK), :]
            values_w = tall[pl.ds(pl.multiple_of(2 * rows + width + b * BLOCK, BLOCK), BLOCK), :]
            incoming[window, :] = nn(keys_w, pool[pl.ds(base, width), pl.ds(0, rows)]) + nn(
                values_w, pool[pl.ds(base + width, width), pl.ds(0, rows)]
            )

        loop(width // BLOCK, product)

        def back_block(b):
            window = window_at(b, LANES)
            block = after[:, window]
            arriving = incoming[:, window]
            gain_sum[...] += arriving * block
            result = norm_down_back(arriving, block, inverse[pl.ds(0, 1), window], tok_gain[...])

            @pl.when((i > 0) | (b > 1))
            def _():
                token_save(i, b).wait()

            token_stage[lax.rem(b, 2)] = result.T.astype(jnp.bfloat16)
            token_save(i, b).start()

        loop(rows // LANES, back_block)

    base_ops = list(done)

    def one_item(i):
        kv_load(i).wait()

        @pl.when(i + 1 < count)
        def _():
            kv_load(i + 1).start()
            tok_load(i + 1).start()

        norm_tokens(i)
        attend(i, range(HEADS // 2))
        tick(1, base_ops[1] + i)
        attend(i, range(HEADS // 2, HEADS))
        tick(2, base_ops[2] + i)
        token_back(i)
        tick(0, base_ops[0] + i)

    loop(count, one_item)
    for j in range(last):
        done[j] = base_ops[j] + count

    small = 2 * latents // pieces
    get_query.wait()
    d_query[...] = d_query[...] * factor
    q_total = d_query[...]
    q_normed, q_inverse = norm_down(latent_ref[...].astype(jnp.float32).T)
    q_incoming = nn_exact(w_square[...], q_total)
    all_gains = gain_cols[...]
    all_gains = jnp.where(lane == 2, jnp.sum(gain_sum[...], axis=-1, keepdims=True), all_gains)
    all_gains = jnp.where(lane == 3, jnp.sum(q_incoming * q_normed, axis=-1, keepdims=True), all_gains)
    gain_rows = all_gains.T[:8]
    latent_rows = norm_down_back(q_incoming, q_normed, q_inverse, gain_columns(query_gain_ref)).T
    query_rows = q_total.T
    for f in range(frames):
        mask = (frame == f).astype(jnp.float32)
        mine_columns = slice(f * own, (f + 1) * own)
        latent_part = latent_rows[:, mine_columns] + mask * d_latent[:, mine_columns]
        both = jnp.concatenate([query_rows[:, mine_columns], latent_part], axis=0)
        small_stage[f, :, :, pl.ds(0, small), :] = both.reshape(2, chips, small, own)
        row = lax.broadcasted_iota(jnp.int32, (8, own), 0)
        gain_block = gain_rows[:, mine_columns] * jnp.where(row < 2, mask, 1.0)
        small_stage[f, :, :, pl.ds(small, 8), :] = jnp.zeros((2, chips, 8, own), jnp.float32)
        small_stage[f, 0, 0, pl.ds(small, 8), :] = gain_block
    put_small = pltpu.make_async_copy(small_stage, loc_d.at[:, :, :, pl.ds(2 * per_piece, small + 8)], small_sem)
    put_small.start()
    advance(1)
    for hop in range(1, frames + 1):
        f = frame_at(hop)
        for b in range(2):
            slot = len(pending) % stage.shape[0]
            for key in [key for key in pending if key % stage.shape[0] == slot and pending[key] is not None]:
                pending[key].wait()
                pending[key] = None
            first_row = pl.multiple_of((2 * f + b) * own, own)
            source = jnp.concatenate(
                [pool[pl.ds(i * 2 * width + first_row, own), pl.ds(0, rows)] for i in range(count)], axis=1
            )
            stage[slot] = nt(flat[:, pl.ds(0, count * rows)], source)
            put_start(loc_d.at[f, :, :, pl.ds(b * per_piece, per_piece)], slot)
        if hop == 1:
            put_small.wait()
        put_done()
        loop(chips, lambda index: pair_frame(hop, sib_chunk(-index)).start())
        if hop <= 2:
            advance(2 if hop == 1 else 0)
    advance(1)
    for hop in range(1, frames):
        other = frame_at(hop)
        if hop > 1:
            for k in range(chips):
                across(hop - 1, k).wait_send()
        for k in range(chips):
            pair_frame(hop, k).wait_recv()
        one = pltpu.make_async_copy(loc_d.at[other, core], y_mine, y_sem.at[0])
        two = pltpu.make_async_copy(sibs[3].at[other], y_sib, y_sem.at[1])
        one.start()
        two.start()
        one.wait()
        two.wait()

        def send_across(index, hop=hop):
            k = chunk(-index)
            add_into(y_mine.at[k], [y_mine.at[k], y_sib.at[k]], kv_rows)
            across(hop, k).start()

        loop(chips, send_across)
    advance(2)
    for k in range(chips):
        pair_frame(frames, k).wait_recv()
    load_mine(last, chunk(0), 0).start()
    load_sib(last, chunk(0), 0).start()
    advance(0)
    total = 2 * chips - 1
    others = sum(total - done[j] for j in range(last))
    turns, taken = total - done[last], 0
    for turn in range(turns):
        while taken * turns < (turn + 1) * others:
            j = max(range(last), key=lambda j: (total - done[j]) * (streams[j][2] + 160))
            advance(j)
            taken += 1
        advance(last)

    def drain(k):
        for source in range(3):
            pair(source, k).wait_send()
        for hop in range(1, frames + 1):
            pair_frame(hop, k).wait_send()
        for j in range(n):
            share(j, k, mines[j].at[0]).wait_send()
            share_from(j, k).wait_recv()
        if frames > 1:
            across(frames - 1, k).wait_send()

    loop(chips, drain)

    def drain_ring(step):
        for j in range(n):
            gather(j, chunk(1 - step), mines[j].at[0]).wait_send()

    loop(chips - 1, drain_ring)
    for j in range(n):
        ring(j, 0, (chips - 2) % 2).wait_send()
        keep(j, chunk(1), (chips - 1) % 2).wait()
    for b in range(2):
        token_save(0, b).wait()


def backward(
    frames, first, tokens, kv, act, hidden, mlp_in, cross, after, cotangent, heard, heard_f32, d_triple, skip, log_total, query,
    latent_init, tok_gain, query_gain, mlp_gain, self_gain, w_query, w_keyval, w_out, w_up, w_down, w_self_qkv,
):
    chips, first_rows, own = first.shape[1:]
    items, rows, width = tokens.shape
    latents = latent_init.shape[0]
    hidden_width, columns = hidden.shape
    pieces = 2 * chips
    per_piece = width // pieces
    kv_rows = 2 * per_piece + 2 * latents // pieces + 8
    source_rows = (first_rows, hidden_width // pieces, per_piece * (hidden_width // width + 1), kv_rows)
    streams = tuple((source, 0, size) for source, size in enumerate(source_rows))
    n = len(streams)
    dma = pltpu.SemaphoreType.DMA
    peers = max(frames - 1, 1)
    f32, bf16 = jnp.float32, jnp.bfloat16
    vmem = pl.BlockSpec(memory_space=pltpu.VMEM)
    anywhere = pl.BlockSpec(memory_space=pl.ANY)
    wide = max(columns, rows)
    scratch = [
        pltpu.VMEM((width, max(hidden_width, items * rows)), bf16),
        pltpu.VMEM((max(hidden_width, 2 * rows + 2 * width), width), bf16),
        pltpu.VMEM((width, width), bf16),
        pltpu.VMEM((max(hidden_width, 4 * width), wide), bf16),
        pltpu.VMEM((max(hidden_width + 3 * width, items * 2 * width), wide), bf16),
        pltpu.VMEM((width, columns), bf16),
        pltpu.VMEM((width, columns), bf16),
        pltpu.VMEM((width, columns), bf16),
        pltpu.VMEM((width, columns), bf16),
        pltpu.VMEM((width, columns), bf16),
        pltpu.VMEM((HEADS, latents, width // HEADS), bf16),
        pltpu.VMEM((width, latents), bf16),
        pltpu.VMEM((2, LANES, width), bf16),
        pltpu.VMEM((4, BLOCK, columns), f32),
        pltpu.VMEM((width, wide), f32),
        pltpu.VMEM((width, columns), f32),
        pltpu.VMEM((width, columns), f32),
        pltpu.VMEM((width, wide), f32),
        pltpu.VMEM((2, width, own), f32),
        pltpu.VMEM((frames, 2, chips, 2 * latents // pieces + 8, own), f32),
        pltpu.VMEM((width, latents), f32),
        pltpu.VMEM((width, LANES), f32),
        pltpu.VMEM((width, LANES), f32),
        pltpu.VMEM((width, LANES), f32),
        pltpu.VMEM((width, LANES), f32),
        pltpu.VMEM((latents, width), f32),
        pltpu.VMEM((width, LANES), f32),
        pltpu.VMEM((items, latents, LANES), f32),
        pltpu.VMEM((8, rows), f32),
        pltpu.VMEM((chips, kv_rows, own), f32),
        pltpu.VMEM((chips, kv_rows, own), f32),
        pltpu.VMEM((peers, chips, kv_rows, own), f32),
    ]
    scratch += [pltpu.VMEM((2, size, own), f32) for _, _, size in streams]
    scratch += [pltpu.VMEM((2, size, own), f32) for _, _, size in streams]
    scratch += [pltpu.VMEM((chips, size, own), f32) for _, _, size in streams]
    scratch += [
        dma((3, chips)), dma((3, chips)), dma((n, 2)), dma((n, 2)), dma((n, 2)), dma((n, chips)),
        dma((n, chips)), dma((n, chips)), dma((n, chips)), dma((n, chips)), dma((n,)),
        dma((frames, chips)), dma((frames, chips)), dma((peers, chips)), dma((peers, chips)), dma((2,)), dma((15,)), dma((2,)), dma((2,)), dma((2,)), dma((4,)), dma((2,)), dma,
    ]
    shape = jax.ShapeDtypeStruct
    summed = tuple(shape((2, chips, size, own), f32) for size in source_rows)
    return pl.pallas_call(
        functools.partial(backward_kernel, chips, frames, streams),
        out_shape=summed
        + (shape(tokens.shape, bf16),)
        + summed[1:3]
        + (shape((frames, 2, chips, kv_rows, own), f32),)
        + tuple(shape((chips, size, own), f32) for size in source_rows[:3])
        + (shape((frames, chips, kv_rows, own), f32),),
        in_specs=[anywhere] * 18 + [pl.BlockSpec(memory_space=pltpu.SMEM)] + [vmem] * 7,
        out_specs=(anywhere,) * 12,
        scratch_shapes=scratch,
        compiler_params=pltpu.CompilerParams(collective_id=0, has_side_effects=True, vmem_limit_bytes=62 * 2**20),
        name="backward",
    )(
        first, tokens, kv, act, hidden, mlp_in, cross, after, cotangent, heard, heard_f32, d_triple,
        w_self_qkv, w_up, w_down, w_out, w_keyval, w_query, skip, log_total, query, latent_init,
        tok_gain, query_gain, mlp_gain, self_gain,
    )


def unpack_kernel(first_ref, second_ref, third_ref, kv_ref, latent_ref, qgain_ref, *rest):
    outs, (query_out, *gain_outs), (blocks, total, tail, in_sem, out_sem) = rest[:7], rest[7:12], rest[12:]
    pieces, _, own = first_ref.shape
    loads, stores = [], []

    def place(source, offset, out):
        rows, columns = out.shape
        size = rows // pieces
        view = out.reshape(pieces, size, columns)
        for b in range(columns // own):
            at = len(loads)
            area = blocks.at[pl.ds(starts[at], pieces * size), :].reshape(pieces, size, own)
            loads.append(pltpu.make_async_copy(source.at[:, pl.ds(offset + b * size, size), :], area, in_sem.at[at]))
            stores.append(pltpu.make_async_copy(area, view.at[:, :, pl.ds(b * own, own)], out_sem.at[at]))
        return offset + size * columns // own

    starts, start = [], 0
    for out in outs[:6]:
        rows, columns = out.shape
        for b in range(columns // own):
            starts.append(start)
            start += rows
    place(first_ref, place(first_ref, 0, outs[0]), outs[1])
    place(second_ref, 0, outs[2])
    place(third_ref, place(third_ref, 0, outs[3]), outs[4])
    offset = place(kv_ref, 0, outs[5])
    latents = outs[6].shape[0]
    small = 2 * latents // pieces
    half = pieces // 2
    query = pltpu.make_async_copy(kv_ref.at[:, pl.ds(offset, small), :], total, in_sem.at[len(loads)])
    gains = pltpu.make_async_copy(kv_ref.at[0, pl.ds(offset + small, 8), :], tail, in_sem.at[len(loads) + 1])
    query.start()
    gains.start()
    for copy in loads:
        copy.start()
    normed, _ = norm_down(latent_ref[...].astype(jnp.float32).T)
    query_in = (normed * gain_columns(qgain_ref)).astype(jnp.bfloat16)
    query.wait()
    query_out[...] = nn_exact(query_in, total[pl.ds(0, half)].reshape(latents, own))
    outs[6][...] = total[pl.ds(half, half)].reshape(latents, own)
    gains.wait()
    for out, row in zip(gain_outs, (2, 3, 0, 1)):
        out[...] = tail[row]
    for load, store in zip(loads, stores):
        load.wait()
        store.start()
    for store in stores:
        store.wait()


def unpack_all(sums, latent_init, query_gain, shapes):
    f32 = jnp.float32
    own = sums[0].shape[-1]
    latents, width = latent_init.shape
    pieces = sums[0].shape[0]
    vmem = pl.BlockSpec(memory_space=pltpu.VMEM)
    anywhere = pl.BlockSpec(memory_space=pl.ANY)
    count = sum(columns // own for _, columns in shapes)
    size = sum(rows * columns // own for rows, columns in shapes)
    return pl.pallas_call(
        unpack_kernel,
        out_shape=tuple(jax.ShapeDtypeStruct(shape, f32) for shape in shapes) + (
            jax.ShapeDtypeStruct((latents, own), f32), jax.ShapeDtypeStruct((width, own), f32))
        + (jax.ShapeDtypeStruct((own,), f32),) * 4,
        in_specs=[anywhere] * 4 + [vmem] * 2,
        out_specs=(anywhere,) * len(shapes) + (vmem,) * 6,
        scratch_shapes=[
            pltpu.VMEM((size, own), f32), pltpu.VMEM((pieces, 2 * latents // pieces, own), f32), pltpu.VMEM((8, own), f32),
            pltpu.SemaphoreType.DMA((count + 2,)), pltpu.SemaphoreType.DMA((count,)),
        ],
        compiler_params=pltpu.CompilerParams(vmem_limit_bytes=60 * 2**20),
        name="unpack_all",
    )(*sums, latent_init, query_gain)


def unpack(packed, rows, columns):
    pieces, _, width = packed.shape
    split = packed.reshape(pieces, columns // width, rows // pieces, width)
    return jnp.swapaxes(split, 1, 2).reshape(rows, columns)


def cut(packed, shapes):
    start, out = 0, []
    for rows, columns in shapes:
        count = rows * columns // packed.shape[-1] // packed.shape[0]
        out.append(unpack(packed[:, start : start + count], rows, columns))
        start += count
    return out


def shards(
    tokens,
    skip,
    latent_init,
    tok_gain,
    query_gain,
    mlp_gain,
    self_gain,
    w_query,
    w_keyval,
    w_out,
    w_up,
    w_down,
    w_self_qkv,
    w_self_out,
    grad_out,
):
    frames, pieces = lax.axis_size("frames"), lax.axis_size("items")
    latents, width = latent_init.shape
    hidden = w_up.shape[1]
    own = width // frames
    kv, log_total, query, first, out_latents, act, hidden_rows, mlp_in, cross, after, cotangent, heard, heard_f32, d_triple, _ = forward(
        frames, pieces, tokens, skip, latent_init, tok_gain, query_gain, mlp_gain, self_gain,
        w_query, w_keyval, w_out, w_up, w_down, w_self_qkv, w_self_out, grad_out,
    )
    *sums, token_grad = backward(
        frames, first.reshape((2, pieces // 2) + first.shape[1:]), tokens, kv, act, hidden_rows, mlp_in, cross, after, cotangent,
        heard, heard_f32, d_triple, skip, log_total, query, latent_init, tok_gain, query_gain, mlp_gain, self_gain,
        w_query, w_keyval, w_out, w_up, w_down, w_self_qkv,
    )[:5]
    sums = [array.reshape((pieces,) + array.shape[2:]) for array in sums]
    shapes = ((width, 3 * own), (width, own), (hidden, own), (width, hidden // frames), (width, own), (width, 2 * own))
    if own % LANES == 0:
        *grads, latent_grad, grad_query, gain_tok, gain_query, gain_mlp, gain_self = unpack_all(
            sums, latent_init, query_gain, shapes
        )
    else:
        grads = cut(sums[0], shapes[:2]) + cut(sums[1], shapes[2:3]) + cut(sums[2], shapes[3:5])
        keyval_sum, small = cut(sums[3], (shapes[5], (2 * latents, own)))
        grads.append(keyval_sum)
        latent_grad = small[latents:]
        normed, _ = norm_down(latent_init.astype(jnp.float32).T)
        query_in = (normed * query_gain[:, None]).astype(jnp.bfloat16)
        grad_query = jnp.dot(query_in.astype(jnp.float32), small[:latents], precision=lax.Precision.HIGHEST)
        gain_mlp, gain_self, gain_tok, gain_query = [sums[3][0, row - 8] for row in range(4)]
    return (
        out_latents,
        token_grad,
        latent_grad,
        gain_tok,
        gain_query,
        gain_mlp,
        gain_self,
        grad_query,
        grads[5],
        grads[4],
        grads[3],
        grads[2],
        grads[0],
        grads[1],
    )


def solution(mesh):
    in_specs = (
        P("items", "frames", None),
        P("items"),
        P(),
        P(),
        P(),
        P(),
        P(),
        P(),
        P(),
        P(),
        P(),
        P(),
        P(),
        P(),
        P("items", None, None),
    )
    out_specs = (
        P("items", "frames", None),
        P("items", "frames", None),
        P(None, "frames"),
        P("frames"),
        P("frames"),
        P("frames"),
        P("frames"),
        P(None, "frames"),
        P(None, "frames"),
        P(None, "frames"),
        P(None, "frames"),
        P(None, "frames"),
        P(None, "frames"),
        P(None, "frames"),
    )
    return jax.shard_map(shards, mesh=mesh, in_specs=in_specs, out_specs=out_specs, check_vma=False)
```

time: 293 us -> 289 us (0.986)
  Pallas kernels: 290 us -> 285 us
    pallas_call x1, Pallas kernels: 90.6 us -> 67.8 us  [forward(): pl.pallas_call(functools.partial(forward_kernel, frames, 2 if items % 2 =...]
    pallas_call x1, Pallas kernels: 185 us -> 203 us  [backward(): pl.pallas_call(functools.partial(backward_kernel, chips, frames, streams)...]
where the time goes in v4:
time: 289 us; the launch traced here: 288 us
  Pallas kernels  285 us (99%)
    pallas_call x1, Pallas kernels, backward(): pl.pallas_call(functools.partial(backward_kernel, chips, frames, streams)...  203 us
    pallas_call x1, Pallas kernels, forward(): pl.pallas_call(functools.partial(forward_kernel, frames, 2 if items % 2 =...  67.8 us
    pallas_call x1, Pallas kernels, unpack_all(): pl.pallas_call(unpack_kernel, out_shape=tuple((jax.ShapeDtypeStruct(shape...  14.5 us

profile of v4, /device:TPU:0, one launch (start us, length us, event | category | flops | bytes accessed | tf_op | source)
XLA Modules:
  0.0 288.2 jit_solution(856332189362306470)
XLA Ops:
  0.6 67.8 %forward.1 = (bf16[4,1536,512]{2,1,0:T(8,128)(2,1)}, f32[4,128,128]{2,1,0:T(8,128)}, bf16[128,768]{1,0:T(8,128)(2,1)}, f32[16,192,384]{2,1,0:T(8,128)}, bf16[4,6...) custom-call(bf16[4,512,768]{2,1,0:T(8,128)(2,1)} %tokens_ref.3, ...), custom_call_target="tpu_custom_call" | custom-call | tf_op jit(solution)/shard_map/forward/pallas_call | solution.py:393
  68.4 202.8 %backward.1 = (f32[2,8,192,384]{3,2,1,0:T(8,128)}, f32[2,8,192,384]{3,2,1,0:T(8,128)}, f32[2,8,240,384]{3,2,1,0:T(8,128)}, f32[2,8,120,384]{3,2,1,0:T(8,128)}, b...) custom-call(f32[2,8,192,384]{3,2,1,0:T(8,128)} %bitcast.6, ...), custom_call_target="tpu_custom_call" | custom-call | tf_op jit(solution)/shard_map/backward/pallas_call | solution.py:1130
  271.2 0.0 copy-start.1
  271.3 0.0 copy-start
  271.3 14.5 %unpack_all.1 = (f32[768,1152]{1,0:T(8,128)}, f32[768,384]{1,0:T(8,128)}, f32[3072,384]{1,0:T(8,128)}, f32[768,1536]{1,0:T(8,128)}, f32[768,384]{1,0:T(8,128)}, ...) custom-call(f32[16,192,384]{2,1,0:T(8,128)} %bitcast.7, ...), custom_call_target="tpu_custom_call" | custom-call | tf_op jit(solution)/shard_map/unpack_all/pallas_call | solution.py:1209
  285.8 0.0 copy-done.1
  285.8 0.7 copy.31
  286.6 0.0 copy-done
  286.6 1.7 copy.32
Async XLA Ops:
  271.2 14.6 %copy-start.1 = (bf16[4,64,768]{2,1,0:T(8,128)(2,1)S(1)}, bf16[4,64,768]{2,1,0:T(8,128)(2,1)}, u32[]{:S(2)}) copy-start(bf16[4,64,768]{2,1,0:T(8,128)(2,1)} %get-tuple-element.90) | copy-start | bytes 1179652
  271.3 15.3 %copy-start = (bf16[4,512,768]{2,1,0:T(8,128)(2,1)S(1)}, bf16[4,512,768]{2,1,0:T(8,128)(2,1)}, u32[]{:S(2)}) copy-start(bf16[4,512,768]{2,1,0:T(8,128)(2,1)} %get-tuple-element.91) | copy-start | bytes 9437188

commit v5 on v4

--- a/solution.py
+++ b/solution.py
@@ -95,8 +95,20 @@
     def load_tokens(i):
         return pltpu.make_async_copy(tokens_ref.at[i], tokens.at[lax.rem(i, 2)], tok_sem.at[lax.rem(i, 2)])
 
-    def load_down(part):
-        return pltpu.make_async_copy(w_down_ref.at[pl.ds(part * rows, rows), :], tokens.at[part % 2], tok_sem.at[part % 2])
+    columns_all = items * latents
+    spare = width - columns_all
+    third = 3 * width
+    loads_down = [
+        pltpu.make_async_copy(w_down_ref.at[:, pl.ds(0, columns_all)], triple, w_sem.at[6]),
+        pltpu.make_async_copy(
+            w_down_ref.at[pl.ds(0, third), pl.ds(columns_all, spare)], d_triple.at[:, pl.ds(0, spare)], w_sem.at[7]
+        ),
+        pltpu.make_async_copy(
+            w_down_ref.at[pl.ds(third, hidden - third), pl.ds(columns_all, spare)],
+            d_triple.at[pl.ds(0, hidden - third), pl.ds(spare, spare)],
+            w_sem.at[8],
+        ),
+    ]
 
     def kv_at(i):
         return pl.ds(pl.multiple_of(lax.rem(i, 2) * wide, wide), wide)
@@ -134,6 +146,8 @@
         window = pl.ds(block * BLOCK, BLOCK)
         tall[window, :] = down_up[:, window].T
     load_up.start()
+    for copy in loads_down:
+        copy.start()
     pl.semaphore_wait(barrier, frames - 1)
 
     def heard_item(i):
@@ -178,8 +192,6 @@
             across(i, hop).start()
 
     loop(items, heard_item)
-    load_down(0).start()
-    load_down(1).start()
 
     def turn(source, target, count):
         def block(b):
@@ -202,12 +214,20 @@
     turn(w_out, w_out_t, width)
     load_up.wait()
     turn(down_up, up_down, hidden)
-    for part in range(hidden // rows):
-        load_down(part).wait()
-        for block in range(rows // BLOCK):
-            down_up[:, pl.ds(part * rows + block * BLOCK, BLOCK)] = tokens[part % 2, pl.ds(block * BLOCK, BLOCK), :].T
-        if part + 2 < hidden // rows:
-            load_down(part + 2).start()
+    for copy in loads_down:
+        copy.wait()
+
+    def turn_down(b):
+        window = window_at(b, BLOCK)
+        down_up[pl.ds(0, columns_all), window] = triple[window, :].T
+
+    loop(hidden // BLOCK, turn_down)
+    for b in range(hidden // BLOCK):
+        window = pl.ds(b * BLOCK, BLOCK)
+        if b * BLOCK < third:
+            down_up[pl.ds(columns_all, spare), window] = d_triple[window, pl.ds(0, spare)].T
+        else:
+            down_up[pl.ds(columns_all, spare), window] = d_triple[pl.ds(b * BLOCK - third, BLOCK), pl.ds(spare, spare)].T
     load_qkv.wait()
     turn(w_qkv, tall, 3 * width)
     for i in range(max(items - 2, 0), items):
@@ -442,7 +462,7 @@
             pltpu.VMEM((width, LANES), f32),
             pltpu.VMEM((width, LANES), f32),
             pltpu.VMEM((2, width, own), f32),
-            dma((2,)), dma((2,)), dma((peers, items)), dma((peers, items)), dma((8,)), dma((2,)), dma, dma((9,)),
+            dma((2,)), dma((2,)), dma((peers, items)), dma((peers, items)), dma((9,)), dma((2,)), dma, dma((9,)),
         ],
         compiler_params=pltpu.CompilerParams(collective_id=1, has_side_effects=True, vmem_limit_bytes=62 * 2**20),
         name="forward",
@@ -502,7 +522,7 @@
     n = len(streams)
     mines, sib_slots, rxs = rest[:n], rest[n : 2 * n], rest[2 * n : 3 * n]
     (
-        pair_send, pair_recv, ld_sem, ls_sem, rs_send, rs_recv, ag_send, ag_recv, share_send, share_recv, own_sem,
+        pair_send, pair_recv, ld_sem, ls_sem, rs_send, rs_recv, ag_send, ag_recv, share_send, share_recv, own_sem, krs_send, krs_recv,
         kpair_send, kpair_recv, y_send, y_recv, y_sem, in_sem, tok_sem, kv_sem, out_sem, hidden_sem, stage_sem, small_sem,
     ) = rest[3 * n :]
 
@@ -573,13 +593,11 @@
 
     def load_mine(j, k, slot):
         source, part = part_of(j)
-        src = loc_d.at[frame, core, k, part] if source == 3 else locs[source].at[core, k, part]
-        return pltpu.make_async_copy(src, mines[j].at[slot], ld_sem.at[j, slot])
+        return pltpu.make_async_copy(locs[source].at[core, k, part], mines[j].at[slot], ld_sem.at[j, slot])
 
     def load_sib(j, k, slot):
         source, part = part_of(j)
-        src = sibs[3].at[frame, k, part] if source == 3 else sibs[source].at[k, part]
-        return pltpu.make_async_copy(src, sib_slots[j].at[slot], ls_sem.at[j, slot])
+        return pltpu.make_async_copy(sibs[source].at[k, part], sib_slots[j].at[slot], ls_sem.at[j, slot])
 
     def ring(j, k, slot):
         return remote(mines[j].at[slot], rxs[j].at[k], rs_send.at[j, slot], rs_recv.at[j, k], (right, frame))
@@ -608,8 +626,7 @@
     def prefetch(j, op):
         k, slot = chunk(-op), lax.rem(op, 2)
         source, part = part_of(j)
-        if source < 3 and (j == 0 or streams[j - 1][0] != source):
-            pair(source, k).wait_recv()
+        pair(source, k).wait_recv()
         load_mine(j, k, slot).start()
         load_sib(j, k, slot).start()
 
@@ -630,10 +647,6 @@
             load_mine(j, k, slot).wait()
             load_sib(j, k, slot).wait()
             parts = [mines[j].at[slot], sib_slots[j].at[slot]]
-            if source == 3:
-                for hop in range(1, frames):
-                    across(hop, k).wait_recv()
-                    parts.append(ky.at[hop - 1, k])
             if not (isinstance(op, int) and op == 0):
                 ring(j, k, slot).wait_recv()
                 parts.append(rxs[j].at[k])
@@ -667,6 +680,61 @@
 
         when(op < chips, reduce_op)
         when((op >= chips) & (op < 2 * chips - 1) if not isinstance(op, int) else chips <= op < 2 * chips - 1, gather_op)
+
+    ahead = chips // 2
+    behind = chips - 1 - ahead
+    kmine, krx = mines[last], rxs[last]
+
+    def kv_ring(flow, k, arriving_own):
+        peer = (right, left)[flow]
+        slot = chips if flow == 1 and arriving_own else k
+        return remote(kmine.at[k], krx.at[slot], krs_send.at[flow, k], krs_recv.at[flow, k], (peer, frame))
+
+    def kv_gather(flow, k, src):
+        return remote(src, sums[3].at[core, k], ag_send.at[last + flow, k], ag_recv.at[last + flow, k], ((right, left)[flow], frame))
+
+    def kv_total(k, arrived):
+        parts = [kmine.at[k], y_sib.at[k]]
+        for hop in range(1, frames):
+            across(hop, k).wait_recv()
+            parts.append(ky.at[hop - 1, k])
+        add_into(kmine.at[k], parts + arrived, kv_rows)
+
+    def kv_tick(op):
+        if op < ahead:
+            for flow, length in ((0, ahead), (1, behind)):
+                distance = length - op
+                if distance < 1:
+                    continue
+                k = chunk(distance if flow == 0 else -distance)
+                arrived = []
+                if op > 0:
+                    kv_ring(flow, k, False).wait_recv()
+                    arrived.append(krx.at[k])
+                kv_total(k, arrived)
+                kv_ring(flow, k, distance == 1).start()
+        elif op == ahead:
+            k = chunk(0)
+            kv_ring(0, k, False).wait_recv()
+            kv_ring(1, k, True).wait_recv()
+            kv_total(k, [krx.at[k], krx.at[chips]])
+            for flow in range(2):
+                kv_gather(flow, k, kmine.at[k]).start()
+            share(last, k, kmine.at[k]).start()
+            keep(last, k, k).start()
+        else:
+            step = op - ahead
+            for flow, length in ((0, behind), (1, ahead)):
+                if step > length:
+                    continue
+                k = chunk(-step if flow == 0 else step)
+                kv_gather(flow, k, kmine.at[0]).wait_recv()
+                if step < length:
+                    kv_gather(flow, k, sums[3].at[core, k]).start()
+                share(last, k, sums[3].at[core, k]).start()
+
+    kv_order = [0] + [offset for step in range(1, ahead + 1) for offset in ((step, -step) if step <= behind else (step,))]
+    kv_order = kv_order[::-1]
 
     third = 3 * width
     names = [
@@ -951,6 +1019,7 @@
         attend(i, range(HEADS // 2, HEADS))
         tick(2, base_ops[2] + i)
         token_back(i)
+
         tick(0, base_ops[0] + i)
 
     loop(count, one_item)
@@ -1016,27 +1085,29 @@
         one.wait()
         two.wait()
 
-        def send_across(index, hop=hop):
-            k = chunk(-index)
+        for offset in kv_order:
+            k = chunk(offset)
             add_into(y_mine.at[k], [y_mine.at[k], y_sib.at[k]], kv_rows)
             across(hop, k).start()
-
-        loop(chips, send_across)
     advance(2)
     for k in range(chips):
         pair_frame(frames, k).wait_recv()
-    load_mine(last, chunk(0), 0).start()
-    load_sib(last, chunk(0), 0).start()
+    one = pltpu.make_async_copy(loc_d.at[frame, core], kmine, y_sem.at[0])
+    two = pltpu.make_async_copy(sibs[3].at[frame], y_sib, y_sem.at[1])
+    one.start()
+    two.start()
     advance(0)
+    one.wait()
+    two.wait()
     total = 2 * chips - 1
     others = sum(total - done[j] for j in range(last))
-    turns, taken = total - done[last], 0
+    turns, taken = chips + 1, 0
     for turn in range(turns):
+        kv_tick(turn)
         while taken * turns < (turn + 1) * others:
             j = max(range(last), key=lambda j: (total - done[j]) * (streams[j][2] + 160))
             advance(j)
             taken += 1
-        advance(last)
 
     def drain(k):
         for source in range(3):
@@ -1052,13 +1123,20 @@
     loop(chips, drain)
 
     def drain_ring(step):
-        for j in range(n):
+        for j in range(last):
             gather(j, chunk(1 - step), mines[j].at[0]).wait_send()
 
     loop(chips - 1, drain_ring)
-    for j in range(n):
+    for j in range(last):
         ring(j, 0, (chips - 2) % 2).wait_send()
         keep(j, chunk(1), (chips - 1) % 2).wait()
+    keep(last, chunk(0), 0).wait()
+    for distance in range(1, ahead + 1):
+        kv_ring(0, chunk(distance), False).wait_send()
+        kv_gather(1, chunk(distance - 1), kmine.at[0]).wait_send()
+    for distance in range(1, behind + 1):
+        kv_ring(1, chunk(-distance), False).wait_send()
+        kv_gather(0, chunk(1 - distance), kmine.at[0]).wait_send()
     for b in range(2):
         token_save(0, b).wait()
 
@@ -1117,12 +1195,12 @@
         pltpu.VMEM((chips, kv_rows, own), f32),
         pltpu.VMEM((peers, chips, kv_rows, own), f32),
     ]
-    scratch += [pltpu.VMEM((2, size, own), f32) for _, _, size in streams]
-    scratch += [pltpu.VMEM((2, size, own), f32) for _, _, size in streams]
-    scratch += [pltpu.VMEM((chips, size, own), f32) for _, _, size in streams]
+    scratch += [pltpu.VMEM((2 if source < 3 else chips, size, own), f32) for source, _, size in streams]
+    scratch += [pltpu.VMEM((2, size if source < 3 else 8, own), f32) for source, _, size in streams]
+    scratch += [pltpu.VMEM((chips + source // 3, size, own), f32) for source, _, size in streams]
     scratch += [
         dma((3, chips)), dma((3, chips)), dma((n, 2)), dma((n, 2)), dma((n, 2)), dma((n, chips)),
-        dma((n, chips)), dma((n, chips)), dma((n, chips)), dma((n, chips)), dma((n,)),
+        dma((n + 1, chips)), dma((n + 1, chips)), dma((n, chips)), dma((n, chips)), dma((n,)), dma((2, chips)), dma((2, chips)),
         dma((frames, chips)), dma((frames, chips)), dma((peers, chips)), dma((peers, chips)), dma((2,)), dma((15,)), dma((2,)), dma((2,)), dma((2,)), dma((4,)), dma((2,)), dma,
     ]
     shape = jax.ShapeDtypeStruct

time: 289 us -> 285 us (0.986)
  Pallas kernels: 285 us -> 281 us
    pallas_call x1, Pallas kernels: 203 us -> 199 us  [backward(): pl.pallas_call(functools.partial(backward_kernel, chips, frames, streams)...]
where the time goes in v5:
time: 285 us; the launch traced here: 284 us
  Pallas kernels  281 us (99%)
    pallas_call x1, Pallas kernels, backward(): pl.pallas_call(functools.partial(backward_kernel, chips, frames, streams)...  199 us
    pallas_call x1, Pallas kernels, forward(): pl.pallas_call(functools.partial(forward_kernel, frames, 2 if items % 2 =...  67.6 us
    pallas_call x1, Pallas kernels, unpack_all(): pl.pallas_call(unpack_kernel, out_shape=tuple((jax.ShapeDtypeStruct(shape...  14.5 us

profile of v5, /device:TPU:0, one launch (start us, length us, event | category | flops | bytes accessed | tf_op | source)
XLA Modules:
  0.0 284.4 jit_solution(10990071614051441871)
XLA Ops:
  0.6 67.6 %forward.1 = (bf16[4,1536,512]{2,1,0:T(8,128)(2,1)}, f32[4,128,128]{2,1,0:T(8,128)}, bf16[128,768]{1,0:T(8,128)(2,1)}, f32[16,192,384]{2,1,0:T(8,128)}, bf16[4,6...) custom-call(bf16[4,512,768]{2,1,0:T(8,128)(2,1)} %tokens_ref.3, ...), custom_call_target="tpu_custom_call" | custom-call | tf_op jit(solution)/shard_map/forward/pallas_call | solution.py:413
  68.3 199.1 %backward.1 = (f32[2,8,192,384]{3,2,1,0:T(8,128)}, f32[2,8,192,384]{3,2,1,0:T(8,128)}, f32[2,8,240,384]{3,2,1,0:T(8,128)}, f32[2,8,120,384]{3,2,1,0:T(8,128)}, b...) custom-call(f32[2,8,192,384]{3,2,1,0:T(8,128)} %bitcast.6, ...), custom_call_target="tpu_custom_call" | custom-call | tf_op jit(solution)/shard_map/backward/pallas_call | solution.py:1208
  267.4 0.0 copy-start.1
  267.4 0.0 copy-start
  267.4 14.5 %unpack_all.1 = (f32[768,1152]{1,0:T(8,128)}, f32[768,384]{1,0:T(8,128)}, f32[3072,384]{1,0:T(8,128)}, f32[768,1536]{1,0:T(8,128)}, f32[768,384]{1,0:T(8,128)}, ...) custom-call(f32[16,192,384]{2,1,0:T(8,128)} %bitcast.7, ...), custom_call_target="tpu_custom_call" | custom-call | tf_op jit(solution)/shard_map/unpack_all/pallas_call | solution.py:1287
  281.9 0.0 copy-done.1
  281.9 0.7 copy.31
  282.7 0.0 copy-done
  282.7 1.7 copy.32
Async XLA Ops:
  267.4 14.6 %copy-start.1 = (bf16[4,64,768]{2,1,0:T(8,128)(2,1)S(1)}, bf16[4,64,768]{2,1,0:T(8,128)(2,1)}, u32[]{:S(2)}) copy-start(bf16[4,64,768]{2,1,0:T(8,128)(2,1)} %get-tuple-element.90) | copy-start | bytes 1179652
  267.4 15.3 %copy-start = (bf16[4,512,768]{2,1,0:T(8,128)(2,1)S(1)}, bf16[4,512,768]{2,1,0:T(8,128)(2,1)}, u32[]{:S(2)}) copy-start(bf16[4,512,768]{2,1,0:T(8,128)(2,1)} %get-tuple-element.91) | copy-start | bytes 9437188
